TPU v7x, 32 devices: a whole 2x2x4 slice. The times are simulated.
32 devices in a mesh: exp: 8 (over y, x, core), tp: 4 (over z).
Axes of the slice: x: 2, y: 2, z: 4, core: 2. Of those that a mesh axis runs over, the one named last changes fastest.
Arguments:
- tokens: bfloat16 [4096, 2048], P(('exp', 'tp')), may hold values from -6 to 6
- cotangent: bfloat16 [4096, 2048], P(('exp', 'tp')), may hold values from -6 to 6
- segment_ids: int32 [4096], P('exp'), may hold values from 0 to 2, as said below
- routes: int32 [4096, 6], P('exp'), may hold values from 0 to 15, all different within a row; in each aligned block of 512 rows (0 to 511, 512 to 1023, ...) at most 256 rows name the same one
- norm1_gain: bfloat16 [2048], P('exp'), may hold values from 0.5 to 1.5
- attn_q: bfloat16 [2048, 2048], P('exp', 'tp'), may hold values from -0.21875 to 0.21875
- attn_k: bfloat16 [2048, 512], P('exp', 'tp'), may hold values from -0.125 to 0.125
- attn_v: bfloat16 [2048, 512], P('exp', 'tp'), may hold values from -0.125 to 0.125
- attn_o: bfloat16 [2048, 2048], P('tp', 'exp'), may hold values from -1 to 1
- norm2_gain: bfloat16 [2048], P('exp'), may hold values from 0.5 to 1.5
- router: bfloat16 [2048, 16], P('exp'), may hold values from -0.0625 to 0.0625
- shared_gate: bfloat16 [2048, 2816], P('exp', 'tp'), may hold values from -0.125 to 0.125
- shared_up: bfloat16 [2048, 2816], P('exp', 'tp'), may hold values from -0.125 to 0.125
- shared_down: bfloat16 [2816, 2048], P('tp', 'exp'), may hold values from -0.21875 to 0.21875
- expert_gate: bfloat16 [16, 2048, 1408], P('exp', None, 'tp'), may hold values from -0.125 to 0.125
- expert_up: bfloat16 [16, 2048, 1408], P('exp', None, 'tp'), may hold values from -0.125 to 0.125
- expert_down: bfloat16 [16, 1408, 2048], P('exp', 'tp'), may hold values from -0.625 to 0.625
Outputs:
- out: bfloat16 [4096, 2048], P(('exp', 'tp'))
- grad_tokens: float32 [4096, 2048], P(('exp', 'tp'))
- grad_norm1_gain: float32 [2048], P('exp')
- grad_attn_q: float32 [2048, 2048], P('exp', 'tp')
- grad_attn_k: float32 [2048, 512], P('exp', 'tp')
- grad_attn_v: float32 [2048, 512], P('exp', 'tp')
- grad_attn_o: float32 [2048, 2048], P('tp', 'exp')
- grad_norm2_gain: float32 [2048], P('exp')
- grad_router: float32 [2048, 16], P('exp')
- grad_shared_gate: float32 [2048, 2816], P('exp', 'tp')
- grad_shared_up: float32 [2048, 2816], P('exp', 'tp')
- grad_shared_down: float32 [2816, 2048], P('tp', 'exp')
- grad_expert_gate: float32 [16, 2048, 1408], P('exp', None, 'tp')
- grad_expert_up: float32 [16, 2048, 1408], P('exp', None, 'tp')
- grad_expert_down: float32 [16, 1408, 2048], P('exp', 'tp')
Inputs may be any that keep to these rules, and one draw needn't show every extreme that they name: `segment_ids`: within each sequence of 512 tokens the ids start at 0 and never fall, and each sequence holds three documents with ids 0, 1 and 2; a token attends only to tokens of its own id. `routes`: each row names 6 different experts. Within each aligned block of 512 rows (one sequence) no expert is named more than 256 times, and in some block some expert exactly 256 times.
All inputs are finite; a program needn't handle non-finite values.
Results may differ from a plain program's by a relative error of at most 0.023.
Values may be sent and summed in bfloat16 or wider, within the bound.
A program may use at most 320 MiB of HBM per device.

v0:
```python
import jax
import jax.numpy as jnp
from jax import lax
from jax.sharding import PartitionSpec as P

D = 2048
HEAD_DIM = 128
TOP = 6


epsilon = 1e-06
rope_base = 600000.0


def rotary_tables(length, head_width):
    half_width = head_width // 2
    frequency = rope_base ** (-(jnp.arange(half_width, dtype=jnp.float32) * 2.0 / head_width))
    angles = jnp.arange(length, dtype=jnp.float32)[:, None] * frequency[None, :]
    return (jnp.cos(angles), jnp.sin(angles))


def rotate(values, cosine, sine):
    half_width = values.shape[-1] // 2
    first_half = values[..., :half_width]
    second_half = values[..., half_width:]
    cos_rows = cosine[:, None, :]
    sin_rows = sine[:, None, :]
    return jnp.concatenate(
        [
            first_half * cos_rows - second_half * sin_rows,
            second_half * cos_rows + first_half * sin_rows,
        ],
        axis=-1,
    )


def rotate_back(gradient, cosine, sine):
    half_width = gradient.shape[-1] // 2
    first_half = gradient[..., :half_width]
    second_half = gradient[..., half_width:]
    cos_rows = cosine[:, None, :]
    sin_rows = sine[:, None, :]
    return jnp.concatenate(
        [
            first_half * cos_rows + second_half * sin_rows,
            second_half * cos_rows - first_half * sin_rows,
        ],
        axis=-1,
    )


def silu_parts(pre_act):
    sigmoid_pre = jax.nn.sigmoid(pre_act)
    return (pre_act * sigmoid_pre, sigmoid_pre * (1.0 + pre_act * (1.0 - sigmoid_pre)))


def norm_back(grad_normed, input_tokens, scale_rows, gain):
    grad_gain = jnp.sum(grad_normed * input_tokens * scale_rows, axis=0)
    scaled_grad = grad_normed * gain
    grad_inputs = (
        scale_rows * scaled_grad
        - input_tokens
        * scale_rows
        * scale_rows
        * scale_rows
        * jnp.mean(scaled_grad * input_tokens, axis=-1, keepdims=True)
    )
    return (grad_gain, grad_inputs)


def shards(
    tokens,
    cotangent,
    segment_ids,
    routes,
    norm1_gain,
    attn_q,
    attn_k,
    attn_v,
    attn_o,
    norm2_gain,
    router,
    shared_gate,
    shared_up,
    shared_down,
    expert_gate,
    expert_up,
    expert_down,
):
    exp_count = lax.axis_size("exp")
    tp_index = lax.axis_index("tp")
    quarter = tokens.shape[0]
    gathered = (
        lax.all_gather(norm1_gain, "exp", axis=0, tiled=True),
        lax.all_gather(norm2_gain, "exp", axis=0, tiled=True),
        lax.all_gather(attn_q, "exp", axis=0, tiled=True),
        lax.all_gather(attn_k, "exp", axis=0, tiled=True),
        lax.all_gather(attn_v, "exp", axis=0, tiled=True),
        lax.all_gather(attn_o, "exp", axis=1, tiled=True),
        lax.all_gather(router, "exp", axis=0, tiled=True),
        lax.all_gather(shared_gate, "exp", axis=0, tiled=True),
        lax.all_gather(shared_up, "exp", axis=0, tiled=True),
        lax.all_gather(shared_down, "exp", axis=1, tiled=True),
    )
    first_norm_scale = gathered[0].astype(jnp.float32)
    second_norm_scale = gathered[1].astype(jnp.float32)
    (
        query_weight,
        key_weight,
        value_weight,
        output_weight,
        router_weight,
        shared_gate_weight,
        shared_up_weight,
        shared_down_weight,
    ) = gathered[2:]
    rows_both = (
        lax.all_gather(tokens, "tp", axis=0, tiled=True),
        lax.all_gather(cotangent, "tp", axis=0, tiled=True),
    )
    whole = rows_both[0].astype(jnp.float32)
    grad_full = rows_both[1].astype(jnp.float32)
    seq_len = whole.shape[0]
    scale_one = lax.rsqrt(jnp.mean(whole * whole, axis=-1, keepdims=True) + epsilon)
    normed_one = (whole * scale_one * first_norm_scale).astype(jnp.bfloat16)
    heads_dev = query_weight.shape[1] // HEAD_DIM
    kv_dev = key_weight.shape[1] // HEAD_DIM
    group_size = heads_dev // kv_dev
    score_scale = HEAD_DIM ** (-0.5)
    cosine, sine = rotary_tables(seq_len, HEAD_DIM)
    query_lin = jnp.dot(normed_one, query_weight, preferred_element_type=jnp.float32).reshape(
        seq_len, heads_dev, HEAD_DIM
    )
    queries = (
        rotate(query_lin, cosine, sine)
        .astype(jnp.bfloat16)
        .reshape(seq_len, kv_dev, group_size, HEAD_DIM)
    )
    key_lin = jnp.dot(normed_one, key_weight, preferred_element_type=jnp.float32).reshape(
        seq_len, kv_dev, HEAD_DIM
    )
    keys_rot = rotate(key_lin, cosine, sine).astype(jnp.bfloat16)
    values = (
        jnp.dot(normed_one, value_weight, preferred_element_type=jnp.float32)
        .astype(jnp.bfloat16)
        .reshape(seq_len, kv_dev, HEAD_DIM)
    )
    positions = jnp.arange(seq_len, dtype=jnp.int32)
    allowed = (positions[None, :] <= positions[:, None]) & (
        segment_ids[:, None] == segment_ids[None, :]
    )

    def masked_scores():
        raw_scores = jnp.einsum(
            "qkgd,ckd->kgqc", queries, keys_rot, preferred_element_type=jnp.float32
        )
        return jnp.where(allowed, raw_scores * score_scale, -1e30)

    scores = masked_scores()
    row_max = jnp.max(scores, axis=-1, keepdims=True)
    exponent = jnp.exp(scores - row_max)
    row_total = jnp.sum(exponent, axis=-1, keepdims=True)
    log_total = row_max + jnp.log(row_total)
    attended = jnp.einsum(
        "kgqc,ckd->qkgd",
        (exponent / row_total).astype(jnp.bfloat16),
        values,
        preferred_element_type=jnp.float32,
    )
    attended = attended.reshape(seq_len, heads_dev * HEAD_DIM).astype(jnp.bfloat16)
    attn_total = lax.psum(
        jnp.dot(attended, output_weight, preferred_element_type=jnp.float32), "tp"
    )
    residual = whole + attn_total
    scale_two = lax.rsqrt(jnp.mean(residual * residual, axis=-1, keepdims=True) + epsilon)
    second_normalized = (residual * scale_two * second_norm_scale).astype(jnp.bfloat16)
    logits = jnp.dot(second_normalized, router_weight, preferred_element_type=jnp.float32)
    router_probs = jax.nn.softmax(logits, axis=-1)
    experts_all = logits.shape[1]
    member = routes[:, :, None] == jnp.arange(experts_all, dtype=jnp.int32)[None, None, :]
    chosen = jnp.sum(jnp.where(member, router_probs[:, None, :], 0.0), axis=-1)
    chosen_sum = jnp.sum(chosen, axis=-1, keepdims=True)
    gate_probabilities = chosen / chosen_sum
    assignments = seq_len * TOP
    flat_routes = routes.reshape(assignments)
    onehot = (flat_routes[:, None] == jnp.arange(experts_all, dtype=jnp.int32)[None, :]).astype(
        jnp.int32
    )
    slot_index = jnp.sum(jnp.cumsum(onehot, axis=0) * onehot, axis=-1) - 1
    capacity = 4 * assignments // (3 * experts_all)
    destination = flat_routes * capacity + slot_index
    slot_source = (
        jnp.full((experts_all * capacity,), assignments, jnp.int32)
        .at[destination]
        .set(jnp.arange(assignments, dtype=jnp.int32))
    )
    slot_token = slot_source // TOP
    padded_rows = jnp.concatenate([second_normalized, jnp.zeros((1, D), jnp.bfloat16)], axis=0)
    local_experts = expert_gate.shape[0]
    send_rows = padded_rows[slot_token].reshape(experts_all, capacity, D)
    received_rows = lax.all_to_all(send_rows, "exp", split_axis=0, concat_axis=0, tiled=True)
    received_rows = received_rows.reshape(exp_count, local_experts, capacity, D)
    gate_lin = jnp.einsum(
        "secd,edf->secf", received_rows, expert_gate, preferred_element_type=jnp.float32
    )
    up_projected = jnp.einsum(
        "secd,edf->secf", received_rows, expert_up, preferred_element_type=jnp.float32
    )
    silu_gate, silu_slope = silu_parts(gate_lin)
    activation = (silu_gate * up_projected).astype(jnp.bfloat16)
    partial_rows = jnp.einsum(
        "secf,efd->secd", activation, expert_down, preferred_element_type=jnp.float32
    ).astype(jnp.bfloat16)
    returned = lax.all_to_all(
        partial_rows.reshape(experts_all, capacity, D),
        "exp",
        split_axis=0,
        concat_axis=0,
        tiled=True,
    )
    picked = (
        returned.reshape(experts_all * capacity, D)[destination]
        .astype(jnp.float32)
        .reshape(seq_len, TOP, D)
    )
    routed_part = jnp.sum(gate_probabilities[:, :, None] * picked, axis=1)
    shared_gate_lin = jnp.dot(
        second_normalized, shared_gate_weight, preferred_element_type=jnp.float32
    )
    shared_up_lin = jnp.dot(second_normalized, shared_up_weight, preferred_element_type=jnp.float32)
    shared_silu, shared_slope = silu_parts(shared_gate_lin)
    shared_act = (shared_silu * shared_up_lin).astype(jnp.bfloat16)
    branch_mine = lax.psum_scatter(
        (
            jnp.dot(shared_act, shared_down_weight, preferred_element_type=jnp.float32)
            + routed_part
        ).astype(jnp.bfloat16),
        "tp",
        scatter_dimension=0,
        tiled=True,
    ).astype(jnp.float32)
    residual_mine = lax.dynamic_slice_in_dim(residual, tp_index * quarter, quarter, 0)
    output = (residual_mine + branch_mine).astype(jnp.bfloat16)
    grad_low = grad_full.astype(jnp.bfloat16)
    d_shared_act = jnp.einsum(
        "td,fd->tf", grad_low, shared_down_weight, preferred_element_type=jnp.float32
    )
    d_shared_gate = (d_shared_act * shared_up_lin * shared_slope).astype(jnp.bfloat16)
    d_shared_up = (d_shared_act * shared_silu).astype(jnp.bfloat16)
    grad_sdown = jnp.einsum("tf,td->fd", shared_act, grad_low, preferred_element_type=jnp.float32)
    grad_sgate = jnp.einsum(
        "td,tf->df", second_normalized, d_shared_gate, preferred_element_type=jnp.float32
    )
    grad_sup = jnp.einsum(
        "td,tf->df", second_normalized, d_shared_up, preferred_element_type=jnp.float32
    )
    d_normed_two = jnp.einsum(
        "tf,df->td", d_shared_gate, shared_gate_weight, preferred_element_type=jnp.float32
    )
    d_normed_two = d_normed_two + jnp.einsum(
        "tf,df->td", d_shared_up, shared_up_weight, preferred_element_type=jnp.float32
    )
    gate_padded = jnp.concatenate(
        [gate_probabilities.reshape(assignments), jnp.zeros((1,), jnp.float32)]
    )
    grad_padded = jnp.concatenate([grad_full, jnp.zeros((1, D), jnp.float32)], axis=0)
    slot_grads = (gate_padded[slot_source][:, None] * grad_padded[slot_token]).astype(jnp.bfloat16)
    grad_arrived = lax.all_to_all(
        slot_grads.reshape(experts_all, capacity, D), "exp", split_axis=0, concat_axis=0, tiled=True
    )
    grad_arrived = grad_arrived.reshape(exp_count, local_experts, capacity, D)
    d_activation = jnp.einsum(
        "secd,efd->secf", grad_arrived, expert_down, preferred_element_type=jnp.float32
    )
    d_gate_low = (d_activation * up_projected * silu_slope).astype(jnp.bfloat16)
    up_gradient_lower = (d_activation * silu_gate).astype(jnp.bfloat16)
    grad_edown = jnp.einsum(
        "secf,secd->efd", activation, grad_arrived, preferred_element_type=jnp.float32
    )
    grad_egate = jnp.einsum(
        "jnhz,jnhw->nzw", received_rows, d_gate_low, preferred_element_type=jnp.float32
    )
    expert_up_gradient = jnp.einsum(
        "jnhz,jnhw->nzw", received_rows, up_gradient_lower, preferred_element_type=jnp.float32
    )
    d_rows = jnp.einsum(
        "secf,edf->secd", d_gate_low, expert_gate, preferred_element_type=jnp.float32
    )
    d_rows = (
        d_rows
        + jnp.einsum(
            "secf,edf->secd", up_gradient_lower, expert_up, preferred_element_type=jnp.float32
        )
    ).astype(jnp.bfloat16)
    back_rows = lax.all_to_all(
        d_rows.reshape(experts_all, capacity, D), "exp", split_axis=0, concat_axis=0, tiled=True
    )
    back_picked = (
        back_rows.reshape(experts_all * capacity, D)[destination]
        .astype(jnp.float32)
        .reshape(seq_len, TOP, D)
    )
    d_normed_two = d_normed_two + jnp.sum(back_picked, axis=1)
    d_gates = jnp.sum(picked * grad_full[:, None, :], axis=-1)
    d_normed_two, d_gates = lax.psum((d_normed_two, d_gates), "tp")
    d_chosen = (
        d_gates - jnp.sum(d_gates * gate_probabilities, axis=-1, keepdims=True)
    ) / chosen_sum
    d_probs = jnp.sum(jnp.where(member, d_chosen[:, :, None], 0.0), axis=1)
    d_logits = (
        router_probs * (d_probs - jnp.sum(d_probs * router_probs, axis=-1, keepdims=True))
    ).astype(jnp.bfloat16)
    grad_router = jnp.einsum(
        "td,te->de", second_normalized, d_logits, preferred_element_type=jnp.float32
    )
    d_normed_two = d_normed_two + jnp.einsum(
        "te,de->td", d_logits, router_weight, preferred_element_type=jnp.float32
    )
    grad_gain_two, d_residual_norm = norm_back(d_normed_two, residual, scale_two, second_norm_scale)
    d_residual = grad_full + d_residual_norm
    d_attn_low = d_residual.astype(jnp.bfloat16)
    grad_out_w = jnp.einsum("tf,td->fd", attended, d_attn_low, preferred_element_type=jnp.float32)
    d_attended = jnp.einsum(
        "td,fd->tf", d_attn_low, output_weight, preferred_element_type=jnp.float32
    ).astype(jnp.bfloat16)
    d_attended = d_attended.reshape(seq_len, kv_dev, group_size, HEAD_DIM)
    probs_again = jnp.exp(masked_scores() - log_total)
    d_probs_att = jnp.einsum(
        "qkgd,ckd->kgqc", d_attended, values, preferred_element_type=jnp.float32
    )
    row_inner = jnp.sum(d_probs_att * probs_again, axis=-1, keepdims=True)
    d_raw = (probs_again * (d_probs_att - row_inner) * score_scale).astype(jnp.bfloat16)
    d_query = jnp.einsum(
        "kgqc,ckd->qkgd", d_raw, keys_rot, preferred_element_type=jnp.float32
    ).reshape(seq_len, heads_dev, HEAD_DIM)
    d_key = jnp.einsum("kgqc,qkgd->ckd", d_raw, queries, preferred_element_type=jnp.float32)
    d_value = jnp.einsum(
        "kgqc,qkgd->ckd",
        probs_again.astype(jnp.bfloat16),
        d_attended,
        preferred_element_type=jnp.float32,
    )
    d_query = (
        rotate_back(d_query, cosine, sine)
        .astype(jnp.bfloat16)
        .reshape(seq_len, heads_dev * HEAD_DIM)
    )
    d_key = (
        rotate_back(d_key, cosine, sine).astype(jnp.bfloat16).reshape(seq_len, kv_dev * HEAD_DIM)
    )
    d_value = d_value.astype(jnp.bfloat16).reshape(seq_len, kv_dev * HEAD_DIM)
    grad_query = jnp.einsum("td,tf->df", normed_one, d_query, preferred_element_type=jnp.float32)
    grad_key = jnp.einsum("td,tf->df", normed_one, d_key, preferred_element_type=jnp.float32)
    grad_value = jnp.einsum("td,tf->df", normed_one, d_value, preferred_element_type=jnp.float32)
    d_normed_one = jnp.einsum(
        "tf,df->td", d_query, query_weight, preferred_element_type=jnp.float32
    )
    d_normed_one = d_normed_one + jnp.einsum(
        "tf,df->td", d_key, key_weight, preferred_element_type=jnp.float32
    )
    d_normed_one = d_normed_one + jnp.einsum(
        "tf,df->td", d_value, value_weight, preferred_element_type=jnp.float32
    )
    d_normed_one = lax.psum(d_normed_one.astype(jnp.bfloat16), "tp").astype(jnp.float32)
    grad_gain_one, d_input_norm = norm_back(d_normed_one, whole, scale_one, first_norm_scale)
    d_input = d_residual + d_input_norm
    d_input_mine = lax.dynamic_slice_in_dim(d_input, tp_index * quarter, quarter, 0)
    summed = (
        lax.psum_scatter(
            grad_gain_one.astype(jnp.bfloat16), "exp", scatter_dimension=0, tiled=True
        ).astype(jnp.float32),
        lax.psum_scatter(
            grad_query.astype(jnp.bfloat16), "exp", scatter_dimension=0, tiled=True
        ).astype(jnp.float32),
        lax.psum_scatter(
            grad_key.astype(jnp.bfloat16), "exp", scatter_dimension=0, tiled=True
        ).astype(jnp.float32),
        lax.psum_scatter(
            grad_value.astype(jnp.bfloat16), "exp", scatter_dimension=0, tiled=True
        ).astype(jnp.float32),
        lax.psum_scatter(
            grad_out_w.astype(jnp.bfloat16), "exp", scatter_dimension=1, tiled=True
        ).astype(jnp.float32),
        lax.psum_scatter(
            grad_gain_two.astype(jnp.bfloat16), "exp", scatter_dimension=0, tiled=True
        ).astype(jnp.float32),
        lax.psum_scatter(
            grad_router.astype(jnp.bfloat16), "exp", scatter_dimension=0, tiled=True
        ).astype(jnp.float32),
        lax.psum_scatter(
            grad_sgate.astype(jnp.bfloat16), "exp", scatter_dimension=0, tiled=True
        ).astype(jnp.float32),
        lax.psum_scatter(
            grad_sup.astype(jnp.bfloat16), "exp", scatter_dimension=0, tiled=True
        ).astype(jnp.float32),
        lax.psum_scatter(
            grad_sdown.astype(jnp.bfloat16), "exp", scatter_dimension=1, tiled=True
        ).astype(jnp.float32),
    )
    return (
        output,
        d_input_mine,
        summed[0],
        summed[1],
        summed[2],
        summed[3],
        summed[4],
        summed[5],
        summed[6],
        summed[7],
        summed[8],
        summed[9],
        grad_egate,
        expert_up_gradient,
        grad_edown,
    )


def solution(mesh):
    placed = (
        P(("exp", "tp"), None),
        P(("exp", "tp"), None),
        P("exp"),
        P("exp", None),
        P("exp"),
        P("exp", "tp"),
        P("exp", "tp"),
        P("exp", "tp"),
        P("tp", "exp"),
        P("exp"),
        P("exp", None),
        P("exp", "tp"),
        P("exp", "tp"),
        P("tp", "exp"),
        P("exp", None, "tp"),
        P("exp", None, "tp"),
        P("exp", "tp", None),
    )
    return jax.shard_map(
        shards,
        mesh=mesh,
        in_specs=placed,
        out_specs=(
            P(("exp", "tp"), None),
            P(("exp", "tp"), None),
            P("exp"),
            P("exp", "tp"),
            P("exp", "tp"),
            P("exp", "tp"),
            P("tp", "exp"),
            P("exp"),
            P("exp", None),
            P("exp", "tp"),
            P("exp", "tp"),
            P("tp", "exp"),
            P("exp", None, "tp"),
            P("exp", None, "tp"),
            P("exp", "tp", None),
        ),
        check_vma=False,
    )
```

profile of v0, /device:TPU:0, one launch (start us, length us, event | category | flops | bytes accessed | tf_op | source)
XLA Modules:
  0.0 1813.8 jit_solution(15183513699352405257)
XLA Ops:
  65.1 21.7 %all-gather.12.cloned.1.call-done = bf16[2048,512]{1,0:T(8,128)(2,1)} async-done(((bf16[256,512]{1,0:T(8,128)(2,1)}), bf16[2048,512]{1,0:T(8,128)(2,1)}) %all-gather.12.cloned.1.call-update) | async-done | bytes 2097168 | tf_op jit(solution)/shard_map/all_gather | solution.py:96
  149.2 127.7 %all-reduce.9.cloned.1.call-done = f32[512,2048]{1,0:T(8,128)} async-done(((f32[512,2048]{1,0:T(8,128)}), f32[512,2048]{1,0:T(8,128)}) %all-reduce.9.cloned.1.call-update) | async-done | bytes 4194320 | tf_op jit(solution)/shard_map/psum | solution.py:171
  284.1 33.2 %gather_fusion = bf16[4096,2048]{1,0:T(8,128)(2,1)} fusion(bf16[513,2048]{1,0:T(8,128)(2,1)} %concatenate.47, s32[4096]{0:T(1024)S(1)} %get-tuple-element.46), kind=kCustom, calls=%fused_computation | custom fusion | bytes 33570816 | tf_op jit(solution)/shard_map/gather | solution.py:200
  323.8 186.5 %all_gather.46 = bf16[2048,16]{0,1:T(8,128)(2,1)S(1)} all-gather(bf16[256,16]{0,1:T(8,128)(2,1)S(1)} %copy-done.78), channel_id=1, replica_groups=mesh['exp'=8,'tp'=4] {'exp'}, dimensions={0}, use_global_device_ids=true | all-gather | bytes 73728 | tf_op jit(solution)/shard_map/all_gather | solution.py:100
  514.5 33.7 %gather_fusion.3 = f32[4096,2048]{1,0:T(8,128)} fusion(f32[513,2048]{1,0:T(8,128)} %concatenate.49, s32[4096]{0:T(1024)S(1)} %get-tuple-element.46), kind=kCustom, calls=%fused_computation.3 | custom fusion | bytes 67125248 | tf_op jit(solution)/shard_map/gather | solution.py:267
  552.8 23.0 %gather_fusion.2 = f32[4096]{0:T(1024)S(1)} fusion(f32[3073]{0:T(1024)S(1)} %pad_maximum_fusion.7, s32[4096]{0:T(1024)S(1)} %get-tuple-element.45), kind=kCustom, calls=%fused_computation.2 | custom fusion | bytes 49152 | tf_op jit(solution)/shard_map/gather | solution.py:267
  623.3 171.3 %all-to-all-done.2 = bf16[16,256,2048]{2,1,0:T(8,128)(2,1)} async-done(((bf16[16,256,2048]{2,1,0:T(8,128)(2,1)}), bf16[16,256,2048]{2,1,0:T(8,128)(2,1)}, u32[]{:S(2)}, u32[]{:S(2)}) %all-to-all-start.2) | async-done | bytes 16777248 | tf_op jit(solution)/shard_map/all_to_all | solution.py:268
  827.8 19.0 %fusion = bf16[8,2,256,2048]{3,2,0,1:T(8,128)(2,1)} fusion(f32[2,8,256,2048]{3,2,1,0:T(8,128)} %fusion.33, bf16[8,2,256,352]{2,3,0,1:T(8,128)(2,1)S(1)} %copy-done.18, bf16[2,2048,352]{1,2,0:T(8,128)(2,1)S(1)} %copy-done.22), kind=kOutput, calls=%fused_computation.10 | convolution fusion | flops 5922357248 | bytes 56098816 | tf_op jit(solution)/shard_map/secf,edf->secd/dot_general | solution.py:291
  873.6 108.8 %all-gather.16.cloned.1.call-done = bf16[2048,704]{0,1:T(8,128)(2,1)} async-done(((bf16[256,704]{0,1:T(8,128)(2,1)}), bf16[2048,704]{0,1:T(8,128)(2,1)}) %all-gather.16.cloned.1.call-update) | async-done | bytes 2883600 | tf_op jit(solution)/shard_map/all_gather | solution.py:101
  987.7 61.0 %all-gather.20.cloned.1.call-done = bf16[704,2048]{1,0:T(8,128)(2,1)} async-done(((bf16[704,256]{1,0:T(8,128)(2,1)}), bf16[704,2048]{1,0:T(8,128)(2,1)}) %all-gather.20.cloned.1.call-update) | async-done | bytes 2883600 | tf_op jit(solution)/shard_map/all_gather | solution.py:103
  1092.1 31.7 %gather_fusion.4 = bf16[3072,2048]{1,0:T(8,128)(2,1)} fusion(bf16[4096,2048]{1,0:T(8,128)(2,1)} %bitcast.38, s32[3072]{0:T(1024)S(1)} %broadcast_clamp_fusion), kind=kCustom, calls=%fused_computation.4 | custom fusion | bytes 25178112 | tf_op jit(solution)/shard_map/gather | solution.py:299
  1123.9 22.1 %reshape.393 = f32[512,6,2048]{2,1,0:T(8,128)} reshape(bf16[3072,2048]{1,0:T(8,128)(2,1)} %gather_fusion.4) | data formatting | bytes 37748736 | tf_op jit(solution)/shard_map/convert_element_type | solution.py:300
  1190.4 85.2 %all-to-all-done.1 = bf16[16,256,2048]{2,1,0:T(8,128)(2,1)} async-done(((bf16[16,256,2048]{2,1,0:T(8,128)(2,1)}), bf16[16,256,2048]{2,1,0:T(8,128)(2,1)}, u32[]{:S(2)}, u32[]{:S(2)}) %all-to-all-start.1) | async-done | bytes 16777248 | tf_op jit(solution)/shard_map/all_to_all | solution.py:214
  1275.6 31.9 %gather_fusion.1 = bf16[3072,2048]{1,0:T(8,128)(2,1)} fusion(bf16[4096,2048]{1,0:T(8,128)(2,1)} %bitcast.29, s32[3072]{0:T(1024)S(1)} %broadcast_clamp_fusion), kind=kCustom, calls=%fused_computation.1 | custom fusion | bytes 25178112 | tf_op jit(solution)/shard_map/gather | solution.py:222
  1307.5 22.2 %reshape.392 = f32[512,6,2048]{2,1,0:T(8,128)} reshape(bf16[3072,2048]{1,0:T(8,128)(2,1)} %gather_fusion.1) | data formatting | bytes 37748736 | tf_op jit(solution)/shard_map/convert_element_type | solution.py:223
  1329.7 20.9 %multiply_reduce_fusion = (f32[512,6]{1,0:T(8,128)S(1)}, f32[512,2048]{1,0:T(8,128)}) fusion(f32[512,6,2048]{2,1,0:T(8,128)} %reshape.392, f32[512,2048]{1,0:T(8,128)} %convert_element_type.232, f32[512,6]{1,0:T(8,128)S(1)} %copy-done.30), kind=kLoop, calls=%fused_computation.6 | loop fusion | flops 24114176 | bytes 33579008 | tf_op jit(solution)/shard_map/reduce_sum | solution.py:304
  1350.7 18.7 %psum.30 = f32[512,6]{0,1:T(8,128)S(1)} all-reduce(f32[512,6]{0,1:T(8,128)S(1)} %copy.135), channel_id=1, replica_groups=mesh['exp'=8,'tp'=4] {'tp'}, use_global_device_ids=true, to_apply=%region_18.19 | all-reduce | flops 3072 | bytes 24576 | tf_op jit(solution)/shard_map/psum | solution.py:305
  1425.9 46.3 %reduce-scatter.26.cloned.1.call-done = bf16[704,256]{1,0:T(8,128)(2,1)} async-done(((bf16[704,2048]{1,0:T(8,128)(2,1)}), bf16[704,256]{1,0:T(8,128)(2,1)}) %reduce-scatter.26.cloned.1.call-update) | async-done | bytes 360464 | tf_op jit(solution)/shard_map/reduce_scatter | solution.py:396
  1520.3 32.6 %reduce-scatter.10.cloned.1.call-done = bf16[128,2048]{1,0:T(8,128)(2,1)} async-done(((bf16[512,2048]{1,0:T(8,128)(2,1)}), bf16[128,2048]{1,0:T(8,128)(2,1)}) %reduce-scatter.10.cloned.1.call-update) | async-done | bytes 524304 | tf_op jit(solution)/shard_map/reduce_scatter | solution.py:233
  1555.2 35.0 %reduce-scatter.16.cloned.1.call-done = bf16[256,128]{1,0:T(8,128)(2,1)} async-done(((bf16[2048,128]{1,0:T(8,128)(2,1)}), bf16[256,128]{1,0:T(8,128)(2,1)}) %reduce-scatter.16.cloned.1.call-update) | async-done | bytes 65552 | tf_op jit(solution)/shard_map/reduce_scatter | solution.py:378
  1591.7 36.2 %reduce-scatter.14.cloned.1.call-done = bf16[256,128]{1,0:T(8,128)(2,1)} async-done(((bf16[2048,128]{1,0:T(8,128)(2,1)}), bf16[256,128]{1,0:T(8,128)(2,1)}) %reduce-scatter.14.cloned.1.call-update) | async-done | bytes 65552 | tf_op jit(solution)/shard_map/reduce_scatter | solution.py:375
  1629.4 87.4 %all-reduce.13.cloned.1.call-done = bf16[512,2048]{1,0:T(8,128)(2,1)} async-done(((bf16[512,2048]{1,0:T(8,128)(2,1)}), bf16[512,2048]{1,0:T(8,128)(2,1)}) %all-reduce.13.cloned.1.call-update) | async-done | bytes 2097168 | tf_op jit(solution)/shard_map/psum | solution.py:364
  1742.0 18.2 %reduce-scatter.18.cloned.1.call-done = bf16[512,256]{1,0:T(8,128)(2,1)} async-done(((bf16[512,2048]{1,0:T(8,128)(2,1)}), bf16[512,256]{1,0:T(8,128)(2,1)}) %reduce-scatter.18.cloned.1.call-update) | async-done | bytes 262160 | tf_op jit(solution)/shard_map/reduce_scatter | solution.py:381
  1761.9 43.1 %reduce-scatter.12.cloned.1.call-done = bf16[256,512]{1,0:T(8,128)(2,1)} async-done(((bf16[2048,512]{1,0:T(8,128)(2,1)}), bf16[256,512]{1,0:T(8,128)(2,1)}) %reduce-scatter.12.cloned.1.call-update) | async-done | bytes 262160 | tf_op jit(solution)/shard_map/reduce_scatter | solution.py:372
  (342 shorter events, 480.0 us)
Async XLA Ops:
  7.2 787.4 %copy-start = (bf16[2,352,2048]{2,1,0:T(8,128)(2,1)S(1)}, bf16[2,352,2048]{2,1,0:T(8,128)(2,1)}, u32[]{:S(2)}) copy-start(bf16[2,352,2048]{2,1,0:T(8,128)(2,1)} %param.33) | copy-start | bytes 8650756
  7.2 51.1 %all-gather.10.cloned.1.call-start = ((), (), s32[]{:S(2)}) async-start(), calls=%async_computation.13 | async-start | bytes 2621440 | tf_op jit(solution)/shard_map/all_gather | solution.py:118
  7.9 78.9 %all-gather.12.cloned.1.call-start = ((), (), s32[]{:S(2)}) async-start(), calls=%async_computation.14 | async-start | bytes 2359296 | tf_op jit(solution)/shard_map/all_gather | solution.py:96
  8.7 108.2 %all-gather.14.cloned.1.call-start = ((), (), s32[]{:S(2)}) async-start(), calls=%async_computation.15 | async-start | bytes 2359296 | tf_op jit(solution)/shard_map/all_gather | solution.py:99
  9.4 267.6 %all-reduce.9.cloned.1.call-start = ((), (), s32[]{:S(2)}) async-start(), calls=%async_computation.16 | async-start | bytes 8388608 | tf_op jit(solution)/shard_map/psum | solution.py:171
  317.3 276.0 %all-to-all-start = ((bf16[16,256,2048]{2,1,0:T(8,128)(2,1)}), bf16[16,256,2048]{2,1,0:T(8,128)(2,1)}, u32[]{:S(2)}, u32[]{:S(2)}) async-start(bf16[16,256,2048]{2,1,0:T(8,128)(2,1)} %bitcast.237), calls=%async_computation | async-start | bytes 33554432 | tf_op jit(solution)/shard_map/all_to_all | solution.py:201
  323.2 187.1 %all-gather.22.cloned.1.call-start = ((), (), s32[]{:S(2)}) async-start(), calls=%async_computation.21 | async-start | bytes 2621440 | tf_op jit(solution)/shard_map/all_gather | solution.py:119
  593.3 201.3 %all-to-all-start.2 = ((bf16[16,256,2048]{2,1,0:T(8,128)(2,1)}), bf16[16,256,2048]{2,1,0:T(8,128)(2,1)}, u32[]{:S(2)}, u32[]{:S(2)}) async-start(bf16[16,256,2048]{2,1,0:T(8,128)(2,1)} %multiply_convert_fusion), calls=%async_computation.3 | async-start | bytes 33554432 | tf_op jit(solution)/shard_map/all_to_all | solution.py:268
  599.1 269.3 %all-gather.18.cloned.1.call-start = ((), (), s32[]{:S(2)}) async-start(), calls=%async_computation.18 | async-start | bytes 3244032 | tf_op jit(solution)/shard_map/all_gather | solution.py:102
  861.0 224.9 %all-to-all-start.3 = ((bf16[16,256,2048]{2,1,0:T(8,128)(2,1)}), bf16[16,256,2048]{2,1,0:T(8,128)(2,1)}, u32[]{:S(2)}, u32[]{:S(2)}) async-start(bf16[16,256,2048]{2,1,0:T(8,128)(2,1)} %bitcast.239), calls=%async_computation.4 | async-start | bytes 33554432 | tf_op jit(solution)/shard_map/all_to_all | solution.py:295
  866.9 115.6 %all-gather.16.cloned.1.call-start = ((), (), s32[]{:S(2)}) async-start(), calls=%async_computation.17 | async-start | bytes 3244032 | tf_op jit(solution)/shard_map/all_gather | solution.py:101
  867.6 181.1 %all-gather.20.cloned.1.call-start = ((), (), s32[]{:S(2)}) async-start(), calls=%async_computation.19 | async-start | bytes 3244032 | tf_op jit(solution)/shard_map/all_gather | solution.py:103
  1085.9 189.7 %all-to-all-start.1 = ((bf16[16,256,2048]{2,1,0:T(8,128)(2,1)}), bf16[16,256,2048]{2,1,0:T(8,128)(2,1)}, u32[]{:S(2)}, u32[]{:S(2)}) async-start(bf16[16,256,2048]{2,1,0:T(8,128)(2,1)} %bitcast.238), calls=%async_computation.1 | async-start | bytes 33554432 | tf_op jit(solution)/shard_map/all_to_all | solution.py:214
  1091.7 285.9 %all-reduce.11.cloned.1.call-start = ((), (), s32[]{:S(2)}) async-start(), calls=%async_computation.22 | async-start | bytes 8388608 | tf_op jit(solution)/shard_map/psum | solution.py:305
  1171.6 239.4 %reduce-scatter.22.cloned.1.call-start = ((), (), s32[]{:S(2)}) async-start(), calls=%async_computation.29 | async-start | bytes 3244032 | tf_op jit(solution)/shard_map/reduce_scatter | solution.py:390
  1177.6 246.4 %reduce-scatter.24.cloned.1.call-start = ((), (), s32[]{:S(2)}) async-start(), calls=%async_computation.30 | async-start | bytes 3244032 | tf_op jit(solution)/shard_map/reduce_scatter | solution.py:393
  1180.9 291.2 %reduce-scatter.26.cloned.1.call-start = ((), (), s32[]{:S(2)}) async-start(), calls=%async_computation.31 | async-start | bytes 3244032 | tf_op jit(solution)/shard_map/reduce_scatter | solution.py:396
  1186.0 333.0 %reduce-scatter.20.cloned.1.call-start = ((), (), s32[]{:S(2)}) async-start(), calls=%async_computation.28 | async-start | bytes 73728 | tf_op jit(solution)/shard_map/reduce_scatter | solution.py:387
  1370.7 182.2 %reduce-scatter.10.cloned.1.call-start = ((), (), s32[]{:S(2)}) async-start(), calls=%async_computation.20 | async-start | bytes 2621440 | tf_op jit(solution)/shard_map/reduce_scatter | solution.py:233
  1377.3 212.9 %reduce-scatter.16.cloned.1.call-start = ((), (), s32[]{:S(2)}) async-start(), calls=%async_computation.26 | async-start | bytes 589824 | tf_op jit(solution)/shard_map/reduce_scatter | solution.py:378
  1398.6 229.3 %reduce-scatter.14.cloned.1.call-start = ((), (), s32[]{:S(2)}) async-start(), calls=%async_computation.25 | async-start | bytes 589824 | tf_op jit(solution)/shard_map/reduce_scatter | solution.py:375
  1404.8 312.0 %all-reduce.13.cloned.1.call-start = ((), (), s32[]{:S(2)}) async-start(), calls=%async_computation.23 | async-start | bytes 4194304 | tf_op jit(solution)/shard_map/psum | solution.py:364
  1409.6 350.5 %reduce-scatter.18.cloned.1.call-start = ((), (), s32[]{:S(2)}) async-start(), calls=%async_computation.27 | async-start | bytes 2359296 | tf_op jit(solution)/shard_map/reduce_scatter | solution.py:381
  1479.1 325.9 %reduce-scatter.12.cloned.1.call-start = ((), (), s32[]{:S(2)}) async-start(), calls=%async_computation.24 | async-start | bytes 2359296 | tf_op jit(solution)/shard_map/reduce_scatter | solution.py:372
  (82 other events, 1357.1 us)
Sparse Core Ops, SparseCore 0:
  9.6 48.6 all-gather.9
  60.2 26.5 all-gather.11
  88.7 28.1 all-gather.13
  122.0 154.9 all-reduce.8
  325.3 45.3 all-gather.21
  601.6 113.0 all-gather.17
  869.7 112.7 all-gather.15
  984.5 64.1 all-gather.19
  1171.8 156.2 all-reduce.10
  1331.3 43.9 reduce-scatter.21
  1379.0 44.8 reduce-scatter.23
  1427.2 44.8 reduce-scatter.25
  1475.4 31.4 reduce-scatter.19
  1509.0 43.8 reduce-scatter.9
  1556.7 33.4 reduce-scatter.15
  1593.7 34.1 reduce-scatter.13
  1630.2 86.5 all-reduce.12
  1719.9 40.1 reduce-scatter.17
  1763.8 41.2 reduce-scatter.11
where the time goes:
time: 1830 us; the launch traced here: 1810 us
  waiting for transfers between devices  915 us (50%)
  local copies, waits for them, and re-layouts  265 us (14%)
  blocking collectives  260 us (14%)
  matrix products  222 us (12%)
  other arithmetic  109 us (6%)
  starting transfers between devices  25.7 us (1%)
    all_gather x1, blocking collectives, shards(): lax.all_gather(router, 'exp', axis=0, tiled=True)  187 us
    all_to_all x1, waiting for transfers between devices, shards(): lax.all_to_all(slot_grads.reshape(experts_all, capacity, D), 'exp', split...  171 us
    psum x1, waiting for transfers between devices, shards(): lax.psum(jnp.dot(attended, output_weight, preferred_element_type=jnp.floa...  128 us
    all_gather x1, waiting for transfers between devices, shards(): lax.all_gather(shared_gate, 'exp', axis=0, tiled=True)  109 us
    psum x1, waiting for transfers between devices, shards(): lax.psum(d_normed_one.astype(jnp.bfloat16), 'tp').astype(jnp.float32)  87.4 us
    all_to_all x1, waiting for transfers between devices, shards(): lax.all_to_all(partial_rows.reshape(experts_all, capacity, D), 'exp', spl...  85.2 us
    all_gather x1, waiting for transfers between devices, shards(): lax.all_gather(shared_down, 'exp', axis=1, tiled=True)  61 us
    reduce_scatter x1, waiting for transfers between devices, shards(): lax.psum_scatter(grad_sdown.astype(jnp.bfloat16), 'exp', scatter_dimensio...  46.3 us
  transfers between devices with their start and end apart: 23, of which 16 were waited for; matrix products, arithmetic and copies ran while one was open for 30% of the time, Pallas kernels for 0%

commit v1 on v0

v1 whole, which is shorter than its diff:
```python
import functools

import jax
import jax.numpy as jnp
from jax import lax
from jax.experimental import pallas as pl
from jax.experimental.pallas import tpu as pltpu
from jax.sharding import PartitionSpec as P

D = 2048
HEAD_DIM = 128
TOP = 6


epsilon = 1e-06
rope_base = 600000.0
F32 = jnp.float32
BF16 = jnp.bfloat16


def rotary_tables(length, head_width):
    half_width = head_width // 2
    frequency = rope_base ** (-(jnp.arange(half_width, dtype=jnp.float32) * 2.0 / head_width))
    angles = jnp.arange(length, dtype=jnp.float32)[:, None] * frequency[None, :]
    return (jnp.cos(angles), jnp.sin(angles))


def rotate(values, cosine, sine):
    half_width = values.shape[-1] // 2
    first_half = values[..., :half_width]
    second_half = values[..., half_width:]
    cos_rows = cosine[:, None, :]
    sin_rows = sine[:, None, :]
    return jnp.concatenate(
        [
            first_half * cos_rows - second_half * sin_rows,
            second_half * cos_rows + first_half * sin_rows,
        ],
        axis=-1,
    )


def rotate_back(gradient, cosine, sine):
    return rotate(gradient, cosine, -sine)


def norm_back(grad_normed, input_tokens, scale_rows, gain):
    grad_gain = jnp.sum(grad_normed * input_tokens * scale_rows, axis=0)
    scaled_grad = grad_normed * gain
    grad_inputs = (
        scale_rows * scaled_grad
        - input_tokens
        * scale_rows
        * scale_rows
        * scale_rows
        * jnp.mean(scaled_grad * input_tokens, axis=-1, keepdims=True)
    )
    return (grad_gain, grad_inputs)


def dot(left, right, dims):
    return lax.dot_general(left, right, (dims, ((), ())), preferred_element_type=F32)


NN = ((1,), (0,))
NT = ((1,), (1,))
TN = ((0,), (0,))


def swap(value, axis, bit):
    size = lax.axis_size(axis)
    return lax.ppermute(value, axis, [(i, i ^ bit) for i in range(size)])


ORDER = (0, 1, 7, 6, 3, 2, 5, 4)
GROUP = len(ORDER)
LANES = 128
ROW_CHUNK = 64


def expert_kernel(sizes, *refs):
    parts, experts_all, local_experts, expert_tiles, shared_tiles = sizes
    refs = list(refs)

    def take(count):
        taken = refs[:count]
        del refs[:count]
        return taken

    rows_ref, grads_ref, mask_hbm, gate_hbm, up_hbm, down_hbm = take(6)
    shared_gate_hbm, shared_up_hbm, shared_down_hbm, router_hbm = take(4)
    all_rows, all_grads, act_hbm, wide_grad_hbm, out_even, out_odd, back_ref = take(7)
    wide_v, wide_t, down_v, rows_v, grads_v, mask_v, d_act_v, act_v, wide_grad_v = take(9)
    probs_v, gates_v, total_v, out_v, back_v, own_v, core_v, relay_v, cross_v, line_in, line_out = take(11)
    send, recv, local, weight_sem, mask_sem = take(5)
    quarter = rows_ref.shape[0]
    seq_len = parts * quarter
    half_rows = seq_len // 2
    inner = down_v.shape[0]
    wide = wide_v.shape[0]
    exp_index = lax.axis_index("exp")
    tp_index = lax.axis_index("tp")
    slot = {r: s for s, r in enumerate(ORDER)}

    def part(q):
        return pl.ds(q * quarter, quarter)

    def chip(r):
        return {"exp": exp_index ^ r}

    def line(k):
        return {"tp": tp_index ^ k}

    copies = {}
    for k in range(1, parts):
        copies["z", k] = (rows_ref, all_rows.at[slot[0], part(k)], line(k))
        copies["t", k] = (line_out.at[k - 1], line_in.at[k - 1], line(k))
    for q in range(parts):
        own = rows_ref if q == 0 else all_rows.at[slot[0], part(q)]
        copies["x", q] = (own, all_rows.at[slot[2], part(q)], chip(2))
        copies["y", q] = (own, all_rows.at[slot[4], part(q)], chip(4))
        via = 2 if 2 * q < parts else 4
        copies["d", q] = (all_rows.at[slot[via], part(q)], all_rows.at[slot[6], part(q)], chip(6 - via))
        for r in (0, 2, 4, 6):
            here = own if r == 0 else all_rows.at[slot[r], part(q)]
            copies["c", r, q] = (here, all_rows.at[slot[r + 1], part(q)], chip(1))
        for side, r in enumerate((2, 4)):
            copies["s", r, q] = (back_v.at[slot[r] % 2, part(q)], cross_v.at[side, part(q)], chip(r))
    for r in (0, 2, 4, 6):
        copies["b", r] = (back_v.at[slot[r + 1] % 2], core_v.at[r // 2], chip(1))
    for side in range(2):
        copies["r", side] = (
            back_v.at[slot[6] % 2, pl.ds(side * half_rows, half_rows)],
            relay_v.at[side],
            chip(4 - 2 * side),
        )
    for h in range(2):
        part_h = pl.ds(h * half_rows, half_rows)
        mine = grads_ref.at[part_h]
        copies["gx", h] = (mine, all_grads.at[slot[2], part_h], chip(2))
        copies["gy", h] = (mine, all_grads.at[slot[4], part_h], chip(4))
        via = 4 * h + 2 * (1 - h)
        copies["gd", h] = (all_grads.at[slot[via], part_h], all_grads.at[slot[6], part_h], chip(6 - via))
        for r in (0, 2, 4, 6):
            here = mine if r == 0 else all_grads.at[slot[r], part_h]
            copies["gc", r, h] = (here, all_grads.at[slot[r + 1], part_h], chip(1))
    number = {name: k for k, name in enumerate(copies)}

    def remote(*name):
        source, target, device = copies[name]
        return pltpu.make_async_remote_copy(
            source,
            target,
            send.at[number[name]],
            recv.at[number[name]],
            device_id=device,
            device_id_type=pl.DeviceIdType.MESH,
        )

    barrier = pltpu.get_barrier_semaphore()
    peers = [line(k) for k in range(1, parts)] + [chip(r) for r in (1, 2, 4)]
    for peer in peers:
        pl.semaphore_signal(barrier, inc=1, device_id=peer, device_id_type=pl.DeviceIdType.MESH)
    pl.semaphore_wait(barrier, len(peers))

    for k in range(1, parts):
        remote("z", k).start()

    def spread(q):
        remote("x" if 2 * q < parts else "y", q).start()
        remote("c", 0, q).start()

    def spread_rest(q):
        remote("y" if 2 * q < parts else "x", q).start()

    spread(0)
    own_copy = pltpu.make_async_copy(rows_ref, all_rows.at[slot[0], part(0)], local.at[0])
    padded = expert_tiles * LANES
    hidden = down_hbm.shape[1]
    shared_rows = shared_down_hbm.shape[0]
    weights = [(shared_down_hbm, down_v.at[pl.ds(local_experts * padded, shared_rows)])]
    weights.append((router_hbm, wide_v.at[pl.ds(wide - LANES, LANES)]))
    blanks = [(down_v, local_experts * padded + shared_rows, inner)]

    def load_tiles(source, count, first_tile, side):
        for k in range(-(-count // LANES)):
            rows = min(LANES, count - k * LANES)
            place = (2 * (first_tile + k) + side) * LANES
            weights.append((source.at[pl.ds(k * LANES, rows)], wide_v.at[pl.ds(place, rows)]))
            blanks.append((wide_v, place + rows, place + LANES))

    for e in range(local_experts):
        weights.append((down_hbm.at[e], down_v.at[pl.ds(e * padded, hidden)]))
        blanks.append((down_v, e * padded + hidden, (e + 1) * padded))
        load_tiles(gate_hbm.at[e], hidden, e * expert_tiles, 0)
        load_tiles(up_hbm.at[e], hidden, e * expert_tiles, 1)
    load_tiles(shared_gate_hbm, shared_rows, local_experts * expert_tiles, 0)
    load_tiles(shared_up_hbm, shared_rows, local_experts * expert_tiles, 1)
    weight_copies = [
        pltpu.make_async_copy(source, target, weight_sem.at[k])
        for k, (source, target) in enumerate(weights)
    ]
    own_grads = pltpu.make_async_copy(grads_ref, all_grads.at[slot[0]], local.at[1])

    def load_grads(u):
        return pltpu.make_async_copy(all_grads.at[u], grads_v, local.at[2])

    def load_rows(u):
        return pltpu.make_async_copy(all_rows.at[u], rows_v, local.at[6])

    for h in range(2):
        remote("gx", 0).start() if h == 0 else remote("gy", 1).start()
        remote("gc", 0, h).start()
    own_copy.start()
    own_grads.start()
    for copy in weight_copies:
        copy.start()
    for ref, first, last in blanks:
        if last > first:
            ref[first:last] = jnp.zeros((last - first, D), BF16)

    def arrived_x(q):
        remote("x", q).wait_recv()
        if 2 * q < parts:
            remote("d", q).start()
        remote("c", 2, q).start()

    def arrived_y(q):
        remote("y", q).wait_recv()
        if 2 * q >= parts:
            remote("d", q).start()
        remote("c", 4, q).start()

    def arrived_far(q):
        remote("d", q).wait_recv()
        remote("c", 6, q).start()

    own_grads.wait()
    load_grads(0).start()
    half_parts = parts // 2

    for copy in weight_copies:
        copy.wait()

    def turn(j, _):
        place = pl.ds(pl.multiple_of(j * LANES, LANES), LANES)
        wide_t[:, place] = wide_v[place, :].T
        return 0

    lax.fori_loop(0, wide // LANES, turn, 0)

    def arrived_grads(h):
        remote("gx" if h == 0 else "gy", h).wait_recv()
        remote("gd", h).start()
        remote("gc", 2 + 2 * h, h).start()

    for q in range(1, parts):
        remote("z", q).wait_recv()
        spread(q)
        if q == half_parts - 1:
            arrived_grads(0)
            arrived_grads(1)
        if q >= half_parts:
            arrived_x(q - half_parts)
    own_copy.wait()
    load_rows(0).start()

    def mask_loads(r):
        from_exp = (lax.rem(exp_index, GROUP) ^ r) * seq_len
        return [
            pltpu.make_async_copy(
                mask_hbm.at[pl.ds(pl.multiple_of(from_exp + (tp_index ^ q) * quarter, quarter), quarter)],
                mask_v.at[part(q)],
                mask_sem.at[q],
            )
            for q in range(parts)
        ]

    def act_store(u):
        return pltpu.make_async_copy(act_v, act_hbm.at[u], local.at[3])

    def wide_store(u):
        return pltpu.make_async_copy(wide_grad_v, wide_grad_hbm.at[u], local.at[4])

    def out_store(s):
        kept = out_odd if ORDER[s] % 2 else out_even
        return pltpu.make_async_copy(out_v, kept.at[ORDER[s] // 2], local.at[5])

    def add_into(target, others):
        def chunk(i, _):
            total = None
            for ref, first in [target] + others:
                rows = pl.ds(pl.multiple_of(first + i * ROW_CHUNK, ROW_CHUNK), ROW_CHUNK)
                value = ref[rows].astype(F32)
                total = value if total is None else total + value
            ref, first = target
            ref[pl.ds(pl.multiple_of(first + i * ROW_CHUNK, ROW_CHUNK), ROW_CHUNK)] = total.astype(BF16)
            return 0

        return chunk

    def sum_rows(count, target, others):
        lax.fori_loop(0, count // ROW_CHUNK, add_into(target, others), 0)

    def unit(u, _):
        into = lax.rem(u, 2)

        for s in range(GROUP):
            @pl.when(u == s)
            def _(s=s):
                for load in mask_loads(ORDER[s]):
                    load.start()

        load_grads(u).wait()
        grads = grads_v

        def d_act_tile(first, width):
            d_act_v[:, pl.ds(first, width)] = dot(
                grads[...], down_v[pl.ds(first, width), :], NT
            )

        for first in range(0, inner, 512):
            d_act_tile(first, min(512, inner - first))
        load_rows(u).wait()
        for load in mask_loads(0):
            load.wait()

        @pl.when(u > 0)
        def _():
            act_store(u - 1).wait()
            wide_store(u - 1).wait()

        shared_first = local_experts * expert_tiles
        linear = dot(rows_v[...], wide_t[:, shared_first * 256 :], NN)
        logits = linear[:, shared_tiles * 256 :]
        lane = lax.broadcasted_iota(jnp.int32, logits.shape, 1)
        logits = jnp.where(lane < experts_all, logits, -1e30)
        raised = jnp.exp(logits - jnp.max(logits, axis=1, keepdims=True))
        probs = raised / jnp.sum(raised, axis=1, keepdims=True)
        mask = mask_v[...].astype(F32)
        chosen = probs * mask
        chosen_sum = jnp.sum(chosen, axis=1, keepdims=True)
        probs_v[...] = probs
        gates_v[...] = chosen / chosen_sum

        def tile(linear, at, j, gate):
            one = pl.ds(j * LANES, LANES)
            for first in range(0, seq_len, ROW_CHUNK):
                last = first + ROW_CHUNK
                gate_lin = linear[first:last, at : at + LANES]
                up_lin = linear[first:last, at + LANES : at + 256]
                sigmoid = 1.0 / (1.0 + jnp.exp(-gate_lin))
                silu = gate_lin * sigmoid
                act = silu * up_lin
                d_act = d_act_v[first:last, one]
                if gate is not None:
                    total_v[first:last] += act.astype(BF16).astype(F32) * d_act
                    act = act * gate[first:last]
                    d_act = d_act * gate[first:last]
                act_v[first:last, one] = act.astype(BF16)
                d_gate = d_act * up_lin * (sigmoid * (1.0 + gate_lin * (1.0 - sigmoid)))
                wide_grad_v[first:last, pl.ds(j * 256, LANES)] = d_gate.astype(BF16)
                wide_grad_v[first:last, pl.ds(j * 256 + LANES, LANES)] = (d_act * silu).astype(BF16)

        for k in range(shared_tiles):
            tile(linear, k * 256, shared_first + k, None)
        d_gates = jnp.zeros(logits.shape, F32)
        for e in range(local_experts):
            mine = lane == exp_index * local_experts + e
            gate = jnp.sum(jnp.where(mine, gates_v[...], 0.0), axis=1, keepdims=True)
            total_v[...] = jnp.zeros(logits.shape, F32)
            first_tile = e * expert_tiles
            linear = dot(rows_v[...], wide_t[:, first_tile * 256 : (first_tile + expert_tiles) * 256], NN)
            for k in range(expert_tiles):
                tile(linear, k * 256, first_tile + k, gate)
            d_gates = jnp.where(mine, jnp.sum(total_v[...], axis=1, keepdims=True), d_gates)
        probs, gates, mask = probs_v[...], gates_v[...], mask_v[...].astype(F32)
        chosen_sum = jnp.sum(probs * mask, axis=1, keepdims=True)
        d_gates = d_gates * mask
        d_chosen = (d_gates - jnp.sum(d_gates * gates, axis=1, keepdims=True)) / chosen_sum
        d_probs = d_chosen * mask
        d_logits = probs * (d_probs - jnp.sum(d_probs * probs, axis=1, keepdims=True))
        high = d_logits.astype(BF16)
        low = pltpu.roll(d_logits - high.astype(F32), experts_all, 1)
        wide_grad_v[:, pl.ds(wide - LANES, LANES)] = jnp.where(
            lane < experts_all, high.astype(F32), low
        ).astype(BF16)
        act_store(u).start()
        wide_store(u).start()

        @pl.when(u == 0)
        def _():
            remote("gd", 0).wait_recv()
            remote("gc", 6, 0).start()

        @pl.when(u == 1)
        def _():
            remote("gd", 1).wait_recv()
            remote("gc", 6, 1).start()
            for q in range(half_parts):
                arrived_far(q)

        @pl.when(u == 3)
        def _():
            remote("gx", 1).wait_recv()
            remote("gc", 2, 1).start()
            for q in range(half_parts, parts):
                arrived_x(q)

        @pl.when(u == 4)
        def _():
            remote("gy", 0).wait_recv()
            remote("gc", 4, 0).start()
            for q in range(half_parts):
                arrived_y(q)

        @pl.when(u == 3)
        def _():
            remote("b", 0).wait_send()

        @pl.when(u == 4)
        def _():
            remote("b", 6).wait_send()

        @pl.when(u == 5)
        def _():
            remote("r", 0).wait_send()
            remote("r", 1).wait_send()

        @pl.when(u == 6)
        def _():
            remote("b", 2).wait_send()

        @pl.when(u == 7)
        def _():
            for q in range(parts):
                remote("s", 2, q).wait_send()

        back = back_v.at[into]

        def back_step(n, _):
            columns = pl.ds(pl.multiple_of(n * 512, 512), 512)
            back[:, columns] = dot(wide_grad_v[...], wide_v[:, columns], NN).astype(BF16)
            return 0

        lax.fori_loop(0, D // 512, back_step, 0)

        @pl.when(u == 0)
        def _():
            own_v[...] = back_v[0]

        @pl.when(u == slot[1])
        def _():
            remote("b", 0).start()

        @pl.when(u == slot[7])
        def _():
            remote("b", 6).start()

        @pl.when(u == slot[6])
        def _():
            remote("b", 6).wait_recv()
            sum_rows(seq_len, (back_v.at[slot[6] % 2], 0), [(core_v.at[3], 0)])
            remote("r", 0).start()
            remote("r", 1).start()

        @pl.when(u == slot[3])
        def _():
            remote("b", 2).start()

        @pl.when(u == slot[2])
        def _():
            remote("b", 2).wait_recv()
            remote("r", 0).wait_recv()
            mine = back_v.at[slot[2] % 2]
            sum_rows(half_rows, (mine, 0), [(core_v.at[1], 0), (relay_v.at[0], 0)])
            sum_rows(half_rows, (mine, half_rows), [(core_v.at[1], half_rows)])
            for q in range(parts):
                remote("s", 2, q).start()

        @pl.when(u == slot[5])
        def _():
            remote("b", 4).start()

        @pl.when(u == slot[4])
        def _():
            remote("b", 4).wait_recv()
            remote("r", 1).wait_recv()
            mine = back_v.at[slot[4] % 2]
            sum_rows(half_rows, (mine, half_rows), [(core_v.at[2], half_rows), (relay_v.at[1], 0)])
            sum_rows(half_rows, (mine, 0), [(core_v.at[2], 0)])
            for q in range(parts - 1, -1, -1):
                remote("s", 4, q).start()

        @pl.when(u == 0)
        def _():
            for q in range(half_parts, parts):
                arrived_y(q)
            remote("gy", 0).start()
            remote("gx", 1).start()
            for q in range(parts):
                spread_rest(q)
                remote("c", 0, q).wait_recv()
            for h in range(2):
                remote("gc", 0, h).wait_recv()

        for k, r in ((1, 6), (3, 2), (5, 4)):
            @pl.when(u == k)
            def _(k=k, r=r):
                if k == 1:
                    for q in range(half_parts, parts):
                        arrived_far(q)
                for q in range(parts):
                    remote("c", r, q).wait_recv()
                for h in range(2):
                    remote("gc", r, h).wait_recv()

        @pl.when(u < GROUP - 1)
        def _():
            load_grads(u + 1).start()
            load_rows(u + 1).start()

        @pl.when(u > 0)
        def _():
            out_store(0).wait()

        def out_step(n, _):
            columns = pl.ds(pl.multiple_of(n * 512, 512), 512)
            out_v[:, columns] = dot(act_v[...], down_v[:, columns], NN).astype(BF16)
            return 0

        lax.fori_loop(0, D // 512, out_step, 0)
        for s in range(GROUP):
            @pl.when(u == s)
            def _(s=s):
                out_store(s).start()

        return 0

    lax.fori_loop(0, GROUP, unit, 0)

    remote("b", 0).wait_recv()
    for q in range(parts - 1, -1, -1):
        remote("s", 2, q).wait_recv()
        remote("s", 4, q).wait_recv()
        first = q * quarter
        sources = [(own_v, first), (core_v.at[0], first), (cross_v.at[0], first), (cross_v.at[1], first)]

        def total_step(i, _, q=q, sources=sources):
            total = None
            for ref, start in sources:
                rows = pl.ds(pl.multiple_of(start + i * ROW_CHUNK, ROW_CHUNK), ROW_CHUNK)
                value = ref[rows].astype(F32)
                total = value if total is None else total + value
            rows = pl.ds(pl.multiple_of(i * ROW_CHUNK, ROW_CHUNK), ROW_CHUNK)
            if q == 0:
                back_ref[rows] = total
            else:
                line_out[q - 1, rows] = total.astype(BF16)
            return 0

        lax.fori_loop(0, quarter // ROW_CHUNK, total_step, 0)
        if q:
            remote("t", q).start()
    for k in range(parts - 1, 0, -1):
        remote("t", k).wait_recv()

    def last_step(i, _):
        rows = pl.ds(pl.multiple_of(i * ROW_CHUNK, ROW_CHUNK), ROW_CHUNK)
        total = back_ref[rows]
        for k in range(1, parts):
            total = total + line_in[k - 1, rows].astype(F32)
        back_ref[rows] = total
        return 0

    lax.fori_loop(0, quarter // ROW_CHUNK, last_step, 0)

    act_store(GROUP - 1).wait()
    wide_store(GROUP - 1).wait()
    out_store(GROUP - 1).wait()
    waited = [("b", 0), ("b", 6), ("r", 0), ("r", 1), ("b", 2)] + [("s", 2, q) for q in range(parts)]
    for name in copies:
        if name not in waited:
            remote(*name).wait_send()


def expert_layer(rows, grads, mask, weights, sizes):
    parts, _, local_experts, expert_tiles, shared_tiles = sizes
    quarter = rows.shape[0]
    seq_len = parts * quarter
    inner = (local_experts * expert_tiles + shared_tiles) * LANES
    wide = 2 * inner + LANES
    loads = 2 + local_experts * (1 + 2 * expert_tiles) + 2 * shared_tiles
    copies = 2 * (parts - 1) + 9 * parts + 6 + 14
    hbm = pl.BlockSpec(memory_space=pl.ANY)
    every = jax.ShapeDtypeStruct((GROUP, seq_len, D), BF16)
    some = jax.ShapeDtypeStruct((GROUP // 2, seq_len, D), BF16)
    flops = 2 * GROUP * seq_len * D * (2 * wide + 2 * inner)
    return pl.pallas_call(
        functools.partial(expert_kernel, sizes),
        out_shape=(
            every,
            every,
            jax.ShapeDtypeStruct((GROUP, seq_len, inner), BF16),
            jax.ShapeDtypeStruct((GROUP, seq_len, wide), BF16),
            some,
            some,
            jax.ShapeDtypeStruct((quarter, D), F32),
        ),
        in_specs=[hbm] * (3 + len(weights)),
        out_specs=(hbm,) * 6 + (pl.BlockSpec(memory_space=pltpu.VMEM),),
        scratch_shapes=[
            pltpu.VMEM((wide, D), BF16),
            pltpu.VMEM((D, wide), BF16),
            pltpu.VMEM((inner, D), BF16),
            pltpu.VMEM((seq_len, D), BF16),
            pltpu.VMEM((seq_len, D), BF16),
            pltpu.VMEM((seq_len, LANES), BF16),
            pltpu.VMEM((seq_len, inner), F32),
            pltpu.VMEM((seq_len, inner), BF16),
            pltpu.VMEM((seq_len, wide), BF16),
            pltpu.VMEM((seq_len, LANES), F32),
            pltpu.VMEM((seq_len, LANES), F32),
            pltpu.VMEM((seq_len, LANES), F32),
            pltpu.VMEM((seq_len, D), BF16),
            pltpu.VMEM((2, seq_len, D), BF16),
            pltpu.VMEM((seq_len, D), BF16),
            pltpu.VMEM((GROUP // 2, seq_len, D), BF16),
            pltpu.VMEM((2, seq_len // 2, D), BF16),
            pltpu.VMEM((2, seq_len, D), BF16),
            pltpu.VMEM((parts - 1, quarter, D), BF16),
            pltpu.VMEM((parts - 1, quarter, D), BF16),
            pltpu.SemaphoreType.DMA((copies,)),
            pltpu.SemaphoreType.DMA((copies,)),
            pltpu.SemaphoreType.DMA((8,)),
            pltpu.SemaphoreType.DMA((loads,)),
            pltpu.SemaphoreType.DMA((parts,)),
        ],
        compiler_params=pltpu.CompilerParams(
            collective_id=1, has_side_effects=True, vmem_limit_bytes=60 * 1024 * 1024
        ),
        cost_estimate=pl.CostEstimate(flops=flops, bytes_accessed=120_000_000, transcendentals=0),
        name="experts",
    )(rows, grads, mask, *weights)


def line_rows(own_rows):
    parts = lax.axis_size("tp")
    return [own_rows] + [swap(own_rows, "tp", k) for k in range(1, parts)]


def add_cores(even, odd_swapped):
    return [(e.astype(F32) + o.astype(F32)).astype(BF16) for e, o in zip(even, odd_swapped)]


def far_halves(mine):
    half = mine[3].shape[0] // 2
    return swap(mine[3][:half], "exp", 4), swap(mine[3][half:], "exp", 2)


def near_sums(mine, far):
    half = mine[3].shape[0] // 2
    first = jnp.concatenate([mine[1][:half] + far[0], mine[1][half:]], axis=0)
    second = jnp.concatenate([mine[2][:half], mine[2][half:] + far[1]], axis=0)
    return swap(first, "exp", 2), swap(second, "exp", 4)


def line_sums(mine, near):
    parts = lax.axis_size("tp")
    total = mine[0].astype(F32) + near[0].astype(F32) + near[1].astype(F32)
    total = total.reshape(parts, -1, total.shape[1])
    low = total.astype(BF16)
    result = total[0]
    for k in range(1, parts):
        result = result + swap(low[k], "tp", k).astype(F32)
    return result


def neighbours(parts):
    exp_index, tp_index = lax.axis_index("exp"), lax.axis_index("tp")
    line = [{"tp": tp_index ^ k} for k in range(1, parts)]
    return line, [{"exp": exp_index ^ r} for r in range(1, GROUP)]


def greet(peers):
    barrier = pltpu.get_barrier_semaphore()
    for peer in peers:
        pl.semaphore_signal(barrier, inc=1, device_id=peer, device_id_type=pl.DeviceIdType.MESH)
    pl.semaphore_wait(barrier, len(peers))


def remote_maker(copies, send, recv):
    number = {name: k for k, name in enumerate(copies)}

    def remote(*name):
        source, target, device = copies[name]
        return pltpu.make_async_remote_copy(
            source,
            target,
            send.at[number[name]],
            recv.at[number[name]],
            device_id=device,
            device_id_type=pl.DeviceIdType.MESH,
        )

    return remote


def gather_kernel(parts, *refs):
    tokens_ref, proj_ref, out_ref, mask_ref, gate_ref, up_ref, down_ref = refs[:7]
    tokens_all, proj_all, out_all, mask_all, gate_all, up_all, down_all = refs[7:14]
    send, recv, local = refs[14:]
    exp_index, tp_index = lax.axis_index("exp"), lax.axis_index("tp")
    line, near = neighbours(parts)
    quarter, depth, seq_len = tokens_ref.shape[0], proj_ref.shape[0], mask_ref.shape[0]
    width = down_ref.shape[2]

    def block(whole, size, r, axis=0):
        place = pl.ds(pl.multiple_of((exp_index ^ r) * size, size), size)
        return whole.at[place] if axis == 0 else whole.at[:, place]

    def arrays(r):
        return {
            "p": block(proj_all, depth, r),
            "o": block(out_all, out_ref.shape[1], r, 1),
            "m": block(mask_all, seq_len, r),
        }

    own = {"p": proj_ref, "o": out_ref, "m": mask_ref}
    my_rows = pl.ds(pl.multiple_of(tp_index * quarter, quarter), quarter)
    copies = {}
    def rows_from(s):
        return tokens_all.at[pl.ds(s * quarter, quarter)]

    for s in range(parts):
        for step in (1, -1):
            copies["z", s, step] = (rows_from(s), rows_from(s), {"tp": tp_index + step})
    for key, ref in own.items():
        mine = arrays(0)[key]
        copies["g", 2, key] = (ref, mine, near[1])
        copies["g", 4, key] = (ref, mine, near[3])
        via = 2 if key == "p" else 4
        passed = arrays(via)[key]
        copies["g", 6, key] = (passed, passed, near[5 - via])
        copies["c", 0, key] = (ref, mine, near[0])
        for r in (2, 4, 6):
            copies["c", r, key] = (arrays(r)[key], arrays(r)[key], near[0])
    for r in range(1, GROUP):
        to = exp_index ^ r
        copies["a", r, 0] = (gate_ref.at[to], block(gate_all, width, 0, 1), near[r - 1])
        copies["a", r, 1] = (up_ref.at[to], block(up_all, width, 0, 1), near[r - 1])
        copies["a", r, 2] = (down_ref.at[to], block(down_all, width, 0, 1), near[r - 1])
    remote = remote_maker(copies, send, recv)

    greet(line + near)
    for key in own:
        for r in (2, 4):
            remote("g", r, key).start()
        remote("c", 0, key).start()
    mine = pltpu.make_async_copy(tokens_ref, tokens_all.at[my_rows], local.at[6])
    mine.start()
    mine.wait()

    def at_each_place(body):
        for z in range(parts):
            pl.when(tp_index == z)(functools.partial(body, z))

    def first_hop(z):
        for step in (1, -1):
            if 0 <= z + step < parts:
                remote("z", z, step).start()

    def hop(d, z):
        for step in (1, -1):
            s = z - step * d
            if 0 <= s < parts:
                remote("z", s, step).wait_recv()
                if 0 <= z + step < parts:
                    remote("z", s, step).start()

    def sent(z):
        for step in (1, -1):
            if 0 <= z + step < parts:
                for s in range(z + 1) if step == 1 else range(z, parts):
                    remote("z", s, step).wait_send()

    at_each_place(first_hop)
    kept = [
        (proj_ref, arrays(0)["p"]),
        (out_ref, arrays(0)["o"]),
        (mask_ref, arrays(0)["m"]),
        (gate_ref.at[exp_index], block(gate_all, width, 0, 1)),
        (up_ref.at[exp_index], block(up_all, width, 0, 1)),
        (down_ref.at[exp_index], block(down_all, width, 0, 1)),
    ]
    kept = [pltpu.make_async_copy(s, t, local.at[k]) for k, (s, t) in enumerate(kept)]
    for copy in kept:
        copy.start()
    at_each_place(functools.partial(hop, 1))
    for key in own:
        for r in (2, 4):
            remote("g", r, key).wait_recv()
            if r == (2 if key == "p" else 4):
                remote("g", 6, key).start()
            remote("c", r, key).start()
    for r in range(1, GROUP):
        for k in range(3):
            remote("a", r, k).start()
    at_each_place(functools.partial(hop, 2))
    for key in own:
        remote("g", 6, key).wait_recv()
        remote("c", 6, key).start()
    for d in range(3, parts):
        at_each_place(functools.partial(hop, d))
    for copy in kept:
        copy.wait()
    for name in copies:
        if name[0] in "ca":
            remote(*name).wait_recv()
    at_each_place(sent)
    for name in copies:
        if name[0] != "z":
            remote(*name).wait_send()


def gather_inputs(tokens, proj, out, mask, gate, up, down):
    parts = lax.axis_size("tp")
    hbm = pl.BlockSpec(memory_space=pl.ANY)
    depth, seq_len = proj.shape[0], mask.shape[0]
    shapes = [
        (parts * tokens.shape[0], D),
        (GROUP * depth, proj.shape[1]),
        (out.shape[0], GROUP * out.shape[1]),
        (GROUP * seq_len, LANES),
        *((w.shape[1], GROUP * w.shape[2]) for w in (gate, up, down)),
    ]
    copies = 2 * parts + 3 * 7 + 3 * (GROUP - 1)
    return pl.pallas_call(
        functools.partial(gather_kernel, parts),
        out_shape=tuple(jax.ShapeDtypeStruct(s, BF16) for s in shapes),
        in_specs=[hbm] * 7,
        out_specs=(hbm,) * 7,
        scratch_shapes=[
            pltpu.SemaphoreType.DMA((copies,)),
            pltpu.SemaphoreType.DMA((copies,)),
            pltpu.SemaphoreType.DMA((7,)),
        ],
        compiler_params=pltpu.CompilerParams(collective_id=2, has_side_effects=True),
        name="gather_inputs",
    )(tokens, proj, out, mask, gate, up, down)


def scatter_kernel(parts, *refs):
    proj_ref, out_ref, gate_ref, up_ref, down_ref = refs[:5]
    proj_sum, out_sum, gate_back, up_back, down_back = refs[5:10]
    proj_core, out_core, proj_add, out_add, proj_relay, out_relay = refs[10:16]
    proj_cross, out_cross, narrow, narrow_in, send, recv, local = refs[16:]
    exp_index = lax.axis_index("exp")
    line, near = neighbours(parts)
    depth, width = proj_sum.shape[0], out_sum.shape[1]

    def proj_block(r):
        return proj_ref.at[pl.ds(pl.multiple_of((exp_index ^ r) * depth, depth), depth)]

    def out_block(r):
        return out_ref.at[:, pl.ds(pl.multiple_of((exp_index ^ r) * width, width), width)]

    copies = {}
    for r in (6, 2, 4, 0):
        copies["c", r, 0] = (proj_block(r + 1), proj_core.at[r // 2], near[0])
        copies["c", r, 1] = (out_block(r + 1), out_core.at[r // 2], near[0])
    copies["d", 0] = (proj_add.at[2], proj_relay, near[3])
    copies["d", 1] = (out_add.at[2], out_relay, near[1])
    for side, r in enumerate((2, 4)):
        copies["s", r, 0] = (proj_add.at[side], proj_cross.at[side], near[r - 1])
        copies["s", r, 1] = (out_add.at[side], out_cross.at[side], near[r - 1])
    for k in range(1, parts):
        copies["z", k] = (narrow, narrow_in.at[k - 1], line[k - 1])
    for r in range(1, GROUP):
        to = exp_index ^ r
        copies["a", r, 0] = (gate_ref.at[to], gate_back.at[exp_index], near[r - 1])
        copies["a", r, 1] = (up_ref.at[to], up_back.at[exp_index], near[r - 1])
        copies["a", r, 2] = (down_ref.at[to], down_back.at[exp_index], near[r - 1])
    remote = remote_maker(copies, send, recv)

    def total(target, sources):
        count = target.shape[0]

        def chunk(i, _):
            rows = pl.ds(pl.multiple_of(i * ROW_CHUNK, ROW_CHUNK), ROW_CHUNK)
            value = sum(ref[rows].astype(F32) for ref in sources[1:])
            target[rows] = (sources[0][rows].astype(F32) + value).astype(target.dtype)
            return 0

        lax.fori_loop(0, count // ROW_CHUNK, chunk, 0)

    greet(line + near)
    for r in (6, 2, 4, 0):
        for k in range(2):
            remote("c", r, k).start()
    for k in range(2):
        remote("c", 6, k).wait_recv()
    total(proj_add.at[2], [proj_block(6), proj_core.at[3]])
    remote("d", 0).start()
    total(out_add.at[2], [out_block(6), out_core.at[3]])
    remote("d", 1).start()
    for r in (2, 4):
        for k in range(2):
            remote("c", r, k).wait_recv()
    total(out_add.at[0], [out_block(2), out_core.at[1]])
    remote("s", 2, 1).start()
    total(proj_add.at[1], [proj_block(4), proj_core.at[2]])
    remote("s", 4, 0).start()
    remote("d", 0).wait_recv()
    total(proj_add.at[0], [proj_block(2), proj_core.at[1], proj_relay])
    remote("s", 2, 0).start()
    remote("d", 1).wait_recv()
    total(out_add.at[1], [out_block(4), out_core.at[2], out_relay])
    remote("s", 4, 1).start()
    kept = [
        pltpu.make_async_copy(source.at[exp_index], target.at[exp_index], local.at[k])
        for k, (source, target) in enumerate(
            ((gate_ref, gate_back), (up_ref, up_back), (down_ref, down_back))
        )
    ]
    for copy in kept:
        copy.start()
    for r in range(1, GROUP):
        for k in range(3):
            remote("a", r, k).start()
    for k in range(2):
        remote("c", 0, k).wait_recv()
        for r in (2, 4):
            remote("s", r, k).wait_recv()
        if k == 0:
            total(proj_sum, [proj_block(0), proj_core.at[0], proj_cross.at[0], proj_cross.at[1]])
            narrow[...] = proj_sum[:, proj_sum.shape[1] - LANES :]
            for j in range(1, parts):
                remote("z", j).start()
        else:
            total(out_sum, [out_block(0), out_core.at[0], out_cross.at[0], out_cross.at[1]])
    for j in range(1, parts):
        remote("z", j).wait_recv()
    value = narrow[...]
    for j in range(1, parts):
        value = value + narrow_in[j - 1]
    proj_sum[:, proj_sum.shape[1] - LANES :] = value
    for copy in kept:
        copy.wait()
    for r in range(1, GROUP):
        for k in range(3):
            remote("a", r, k).wait_recv()
    for name in copies:
        remote(*name).wait_send()


def scatter_grads(proj, out, gate, up, down):
    parts = lax.axis_size("tp")
    hbm, vmem = pl.BlockSpec(memory_space=pl.ANY), pl.BlockSpec(memory_space=pltpu.VMEM)
    one = (proj.shape[0] // GROUP, proj.shape[1])
    two = (out.shape[0], out.shape[1] // GROUP)
    narrow = (one[0], LANES)
    copies = 8 + 2 + 4 + (parts - 1) + 3 * (GROUP - 1)
    return pl.pallas_call(
        functools.partial(scatter_kernel, parts),
        out_shape=(
            jax.ShapeDtypeStruct(one, F32),
            jax.ShapeDtypeStruct(two, F32),
            *(jax.ShapeDtypeStruct(x.shape, x.dtype) for x in (gate, up, down)),
        ),
        in_specs=[vmem] * 2 + [hbm] * 3,
        out_specs=(vmem, vmem, hbm, hbm, hbm),
        scratch_shapes=[
            pltpu.VMEM((GROUP // 2, *one), BF16),
            pltpu.VMEM((GROUP // 2, *two), BF16),
            pltpu.VMEM((3, *one), BF16),
            pltpu.VMEM((3, *two), BF16),
            pltpu.VMEM(one, BF16),
            pltpu.VMEM(two, BF16),
            pltpu.VMEM((2, *one), BF16),
            pltpu.VMEM((2, *two), BF16),
            pltpu.VMEM(narrow, F32),
            pltpu.VMEM((parts - 1, *narrow), F32),
            pltpu.SemaphoreType.DMA((copies,)),
            pltpu.SemaphoreType.DMA((copies,)),
            pltpu.SemaphoreType.DMA((3,)),
        ],
        compiler_params=pltpu.CompilerParams(
            collective_id=3, has_side_effects=True, vmem_limit_bytes=40 * 1024 * 1024
        ),
        name="scatter_grads",
    )(proj, out, gate, up, down)


def pad_to(value, axis, multiple):
    widths = [(0, 0)] * value.ndim
    widths[axis] = (0, -value.shape[axis] % multiple)
    return jnp.pad(value, widths)


def shards(
    tokens,
    cotangent,
    segment_ids,
    routes,
    norm1_gain,
    attn_q,
    attn_k,
    attn_v,
    attn_o,
    norm2_gain,
    router,
    shared_gate,
    shared_up,
    shared_down,
    expert_gate,
    expert_up,
    expert_down,
):
    exp_count = lax.axis_size("exp")
    tp_count = lax.axis_size("tp")
    exp_index = lax.axis_index("exp")
    tp_index = lax.axis_index("tp")
    quarter = tokens.shape[0]
    seq_len = quarter * tp_count

    experts_all = router.shape[1]
    local_experts, _, hidden = expert_gate.shape
    shared_hidden = shared_gate.shape[1] // exp_count
    in_group = exp_count == GROUP
    qkv_widths = (attn_q.shape[1], attn_k.shape[1], attn_v.shape[1])
    gains = jnp.stack([norm1_gain, norm2_gain], axis=1)
    proj = jnp.concatenate([attn_q, attn_k, attn_v, router, gains], axis=1)
    qkv_width = sum(qkv_widths)
    proj = pad_to(proj, 1, LANES)
    member_lanes = jnp.any(
        routes[:, :, None] == jnp.arange(LANES, dtype=jnp.int32), axis=1
    ).astype(BF16)

    def cut(weight):
        return pad_to(weight.reshape(exp_count, shared_hidden, -1), 1, 16)

    cut_gate, cut_up, cut_down = cut(shared_gate.T), cut(shared_up.T), cut(shared_down)
    if in_group:
        whole, proj, output_weight, all_masks, my_gate, my_up, my_down = gather_inputs(
            tokens, proj, attn_o, member_lanes, cut_gate, cut_up, cut_down
        )
    else:
        whole = lax.all_gather(tokens, "tp", axis=0, tiled=True)
        proj = lax.all_gather(proj, "exp", axis=0, tiled=True)
        output_weight = lax.all_gather(attn_o, "exp", axis=1, tiled=True)
        all_masks = lax.all_gather(member_lanes, "exp", axis=0, tiled=True)
        my_gate, my_up, my_down = (
            lax.all_to_all(w, "exp", split_axis=0, concat_axis=2, tiled=True)
            for w in (cut_gate, cut_up, cut_down)
        )
        my_gate, my_up, my_down = my_gate[0], my_up[0], my_down[0]
    qkv_weight = proj[:, :qkv_width]
    narrow_weight = proj[:, qkv_width:].T
    first_norm_scale = narrow_weight[experts_all].astype(F32)
    second_norm_scale = narrow_weight[experts_all + 1].astype(F32)
    whole, cotangent = lax.optimization_barrier((whole, cotangent))
    grads_line = line_rows(cotangent)

    own_tokens = tokens.astype(F32)
    whole = whole.astype(F32)
    scale_one = lax.rsqrt(jnp.mean(whole * whole, axis=-1, keepdims=True) + epsilon)
    normed_one = (whole * scale_one * first_norm_scale).astype(BF16)
    heads_dev = qkv_widths[0] // HEAD_DIM
    kv_dev = qkv_widths[1] // HEAD_DIM
    group_size = heads_dev // kv_dev
    score_scale = HEAD_DIM ** (-0.5)
    cosine, sine = rotary_tables(seq_len, HEAD_DIM)
    qkv_lin = dot(normed_one, qkv_weight, NN).reshape(seq_len, -1, HEAD_DIM)
    turned = rotate(qkv_lin[:, : heads_dev + kv_dev], cosine, sine).astype(BF16)
    queries = turned[:, :heads_dev].reshape(seq_len, kv_dev, group_size, HEAD_DIM)
    keys_rot = turned[:, heads_dev:]
    values = qkv_lin[:, heads_dev + kv_dev :].astype(BF16)
    positions = jnp.arange(seq_len, dtype=jnp.int32)
    allowed = (positions[None, :] <= positions[:, None]) & (
        segment_ids[:, None] == segment_ids[None, :]
    )
    raw_scores = jnp.einsum("qkgd,ckd->kgqc", queries, keys_rot, preferred_element_type=F32)
    scores = jnp.where(allowed, raw_scores * score_scale, -1e30)
    exponent = jnp.exp(scores - jnp.max(scores, axis=-1, keepdims=True))
    probs = exponent / jnp.sum(exponent, axis=-1, keepdims=True)
    probs_low = probs.astype(BF16)
    attended = jnp.einsum("kgqc,ckd->qkgd", probs_low, values, preferred_element_type=F32)
    attended = attended.reshape(seq_len, heads_dev * HEAD_DIM).astype(BF16)
    attended, *grads_line[1:-1] = lax.optimization_barrier((attended, *grads_line[1:-1]))
    attn_mine = lax.psum_scatter(
        dot(attended, output_weight, NN).astype(BF16), "tp", scatter_dimension=0, tiled=True
    )

    residual = own_tokens + attn_mine.astype(F32)
    scale_two = lax.rsqrt(jnp.mean(residual * residual, axis=-1, keepdims=True) + epsilon)
    normed_two = (residual * scale_two * second_norm_scale).astype(BF16)
    expert_tiles, shared_tiles = -(-hidden // LANES), -(-my_gate.shape[0] // LANES)
    router_rows = narrow_weight[:experts_all]
    router_pad = jnp.zeros((LANES - 2 * experts_all, D), BF16)
    weights = (
        expert_gate.transpose(0, 2, 1),
        expert_up.transpose(0, 2, 1),
        expert_down,
        my_gate,
        my_up,
        my_down,
        jnp.concatenate([router_rows, router_rows, router_pad], axis=0),
    )
    inner = (local_experts * expert_tiles + shared_tiles) * LANES
    wide = 2 * inner + LANES
    sizes = (tp_count, experts_all, local_experts, expert_tiles, shared_tiles)
    all_masks = all_masks.reshape(exp_count // GROUP, -1, LANES)

    output = residual
    d_normed_two, wide_sum, down_sum = 0.0, 0.0, 0.0
    for base in range(0, exp_count, GROUP):
        rows_b = normed_two
        if base:
            rows_b, grads_line = swap(rows_b, "exp", base), line_rows(swap(cotangent, "exp", base))
        masks = lax.dynamic_index_in_dim(
            all_masks, (exp_index // GROUP) ^ (base // GROUP), keepdims=False
        )
        all_rows, all_grads, act, wide_grads, out_even, out_odd, back = expert_layer(
            rows_b, jnp.concatenate(grads_line, axis=0), masks, weights, sizes
        )
        swapped = swap(out_odd, "exp", 1)
        d_normed_two = d_normed_two + (swap(back, "exp", base) if base else back)
        count = GROUP * seq_len
        grads_seen, act = all_grads.reshape(count, D), act.reshape(count, -1)
        rows_seen, wide_grads = all_rows.reshape(count, D), wide_grads.reshape(count, wide)
        if base + GROUP < exp_count:
            wide_sum = wide_sum + dot(wide_grads, rows_seen, TN)
            down_sum = down_sum + dot(act, grads_seen, TN)
            mine = add_cores(out_even, swapped)
            part_out = line_sums(mine, near_sums(mine, far_halves(mine)))
            output = output + (swap(part_out, "exp", base) if base else part_out)
            cotangent, normed_two, wide_sum, down_sum, output = lax.optimization_barrier(
                (cotangent, normed_two, wide_sum, down_sum, output)
            )
    down_sum = down_sum + dot(act, grads_seen, TN)
    swapped, down_sum = lax.optimization_barrier((swapped, down_sum))

    grad_gain_two, d_residual = norm_back(d_normed_two, residual, scale_two, second_norm_scale)
    d_residual = cotangent.astype(F32) + d_residual

    d_attn_low = lax.all_gather(d_residual.astype(BF16), "tp", axis=0, tiled=True)
    mine = add_cores(out_even, swapped)
    d_attn_low, *far = lax.optimization_barrier((d_attn_low, *far_halves(mine)))
    near = near_sums(mine, far)
    grad_out_w = dot(attended, d_attn_low, TN)
    d_attended = dot(d_attn_low, output_weight, NT).astype(BF16)
    d_attended = d_attended.reshape(seq_len, kv_dev, group_size, HEAD_DIM)
    d_probs_att = jnp.einsum("qkgd,ckd->kgqc", d_attended, values, preferred_element_type=F32)
    row_inner = jnp.sum(d_probs_att * probs, axis=-1, keepdims=True)
    d_raw = (probs * (d_probs_att - row_inner) * score_scale).astype(BF16)
    d_query = jnp.einsum("kgqc,ckd->qkgd", d_raw, keys_rot, preferred_element_type=F32).reshape(
        seq_len, heads_dev, HEAD_DIM
    )
    d_key = jnp.einsum("kgqc,qkgd->ckd", d_raw, queries, preferred_element_type=F32)
    d_value = jnp.einsum("kgqc,qkgd->ckd", probs_low, d_attended, preferred_element_type=F32)
    d_qkv = jnp.concatenate(
        [
            rotate_back(jnp.concatenate([d_query, d_key], axis=1), cosine, sine).astype(BF16),
            d_value.astype(BF16),
        ],
        axis=1,
    ).reshape(seq_len, -1)
    d_normed_one = dot(d_qkv, qkv_weight, NT).astype(BF16)
    d_normed_one, wide_grads = lax.optimization_barrier((d_normed_one, wide_grads))
    d_normed_one = lax.psum_scatter(
        d_normed_one, "tp", scatter_dimension=0, tiled=True
    ).astype(F32)
    grad_qkv = dot(normed_one, d_qkv, TN)
    wide_sum = wide_sum + dot(wide_grads, rows_seen, TN)
    d_normed_one, *near = lax.optimization_barrier((d_normed_one, *near))

    def rows_of(first, count, height):
        tiles = [wide_sum[(first + 2 * k) * LANES : (first + 2 * k + 1) * LANES] for k in range(count)]
        return jnp.concatenate(tiles, axis=0)[:height]

    def both(side):
        experts = [
            rows_of(2 * e * expert_tiles + side, expert_tiles, hidden) for e in range(local_experts)
        ]
        return jnp.stack(experts).transpose(0, 2, 1)

    grad_egate, grad_eup = both(0), both(1)
    padded = expert_tiles * LANES
    grad_edown = jnp.stack(
        [down_sum[e * padded : e * padded + hidden] for e in range(local_experts)]
    )
    start = local_experts * padded
    first_shared = 2 * local_experts * expert_tiles
    grad_router = wide_sum[wide - LANES : wide - LANES + experts_all]
    grad_router = grad_router + wide_sum[wide - LANES + experts_all : wide - LANES + 2 * experts_all]
    output = output + (swap(line_sums(mine, near), "exp", base) if base else line_sums(mine, near))
    output = output.astype(BF16)
    own_scale = lax.rsqrt(jnp.mean(own_tokens * own_tokens, axis=-1, keepdims=True) + epsilon)
    grad_gain_one, d_input = norm_back(d_normed_one, own_tokens, own_scale, first_norm_scale)
    d_input = d_residual + d_input

    def uncut(grad):
        return grad.astype(BF16).reshape(grad.shape[0], exp_count, -1).transpose(1, 0, 2)

    narrow = jnp.concatenate(
        [grad_router.T, grad_gain_one[:, None], grad_gain_two[:, None]], axis=1
    )
    grad_proj = jnp.concatenate([grad_qkv, pad_to(narrow, 1, LANES)], axis=1).astype(BF16)
    grad_out_w = grad_out_w.astype(BF16)
    shared_rows = my_gate.shape[0]
    back_gate = uncut(rows_of(first_shared, shared_tiles, shared_rows))
    back_up = uncut(rows_of(first_shared + 1, shared_tiles, shared_rows))
    back_down = uncut(down_sum[start : start + shared_rows])
    if in_group:
        grad_proj, grad_out_w, back_gate, back_up, back_down = scatter_grads(
            grad_proj, grad_out_w, back_gate, back_up, back_down
        )
        narrow = grad_proj[:, qkv_width:]
    else:
        grad_proj = lax.psum_scatter(grad_proj, "exp", scatter_dimension=0, tiled=True).astype(F32)
        narrow = lax.psum(grad_proj[:, qkv_width:], "tp")
        grad_out_w = lax.psum_scatter(
            grad_out_w, "exp", scatter_dimension=1, tiled=True
        ).astype(F32)
        back_gate, back_up, back_down = (
            lax.all_to_all(x, "exp", split_axis=0, concat_axis=0, tiled=True)
            for x in (back_gate, back_up, back_down)
        )

    def joined(pieces):
        return pieces[:, :shared_hidden].reshape(-1, pieces.shape[2]).astype(F32)

    grad_sgate, grad_sup, grad_sdown = joined(back_gate).T, joined(back_up).T, joined(back_down)
    cuts = (qkv_widths[0], qkv_widths[0] + qkv_widths[1])
    return (
        output,
        d_input,
        narrow[:, experts_all],
        grad_proj[:, : cuts[0]],
        grad_proj[:, cuts[0] : cuts[1]],
        grad_proj[:, cuts[1] : qkv_width],
        grad_out_w,
        narrow[:, experts_all + 1],
        narrow[:, :experts_all],
        grad_sgate,
        grad_sup,
        grad_sdown,
        grad_egate,
        grad_eup,
        grad_edown,
    )


def solution(mesh):
    placed = (
        P(("exp", "tp"), None),
        P(("exp", "tp"), None),
        P("exp"),
        P("exp", None),
        P("exp"),
        P("exp", "tp"),
        P("exp", "tp"),
        P("exp", "tp"),
        P("tp", "exp"),
        P("exp"),
        P("exp", None),
        P("exp", "tp"),
        P("exp", "tp"),
        P("tp", "exp"),
        P("exp", None, "tp"),
        P("exp", None, "tp"),
        P("exp", "tp", None),
    )
    return jax.shard_map(
        shards,
        mesh=mesh,
        in_specs=placed,
        out_specs=(
            P(("exp", "tp"), None),
            P(("exp", "tp"), None),
            P("exp"),
            P("exp", "tp"),
            P("exp", "tp"),
            P("exp", "tp"),
            P("tp", "exp"),
            P("exp"),
            P("exp", None),
            P("exp", "tp"),
            P("exp", "tp"),
            P("tp", "exp"),
            P("exp", None, "tp"),
            P("exp", None, "tp"),
            P("exp", "tp", None),
        ),
        check_vma=False,
    )
```

time: 1830 us -> 778 us (0.43)
  waiting for transfers between devices: 915 us -> 67.8 us
  Pallas kernels: 0 us -> 462 us
  blocking collectives: 260 us -> 0 us
  local copies, waits for them, and re-layouts: 265 us -> 43.9 us
  matrix products: 222 us -> 93.1 us
  other arithmetic: 109 us -> 73.9 us
    pallas_call x0 -> x3, Pallas kernels: none -> 462 us  [the longest x1 348 us: expert_layer(): pl.pallas_call(functools.partial(expert_kernel, sizes), out_shape=(every,...]
    all_to_all x4 -> x0, waiting for transfers between devices: 257 us -> none  [the longest x1 171 us: shards(): lax.all_to_all(slot_grads.reshape(experts_all, capacity, D), 'exp', split...]
    all_gather x5 -> x0, blocking collectives: 227 us -> none  [the longest x1 187 us: shards(): lax.all_gather(router, 'exp', axis=0, tiled=True)]
    all_gather x7 -> x1, waiting for transfers between devices: 217 us -> 1.22 us  [shards(): lax.all_gather(d_residual.astype(BF16), 'tp', axis=0, tiled=True)]
    psum x3 -> x0, waiting for transfers between devices: 215 us -> none  [the longest x1 128 us: shards(): lax.psum(jnp.dot(attended, output_weight, preferred_element_type=jnp.floa...]
    reduce_scatter x9 -> x2, waiting for transfers between devices: 222 us -> 30.5 us  [the longest x1 30.5 us: shards(): lax.psum_scatter(dot(attended, output_weight, NN).astype(BF16), 'tp', sca...]
    gather x5 -> x0, local copies, waits for them, and re-layouts: 154 us -> none  [the longest x1 33.7 us: shards(): grad_padded[slot_token]]
    dot_general x39 -> x14, matrix products: 222 us -> 93.1 us  [the longest x8 83.5 us: dot(): lax.dot_general(left, right, (dims, ((), ())), preferred_element_type=F32)]
  transfers between devices with their start and end apart: 23 -> 14, of which waited for: 16 -> 5; matrix products, arithmetic and copies ran while one was open for 30% -> 21% of each run, Pallas kernels for 0% -> 7%
where the time goes in v1:
time: 778 us; the launch traced here: 769 us
  Pallas kernels  462 us (59%)
  matrix products  93.1 us (12%)
  other arithmetic  73.9 us (9%)
  waiting for transfers between devices  67.8 us (9%)
  local copies, waits for them, and re-layouts  43.9 us (6%)
  between operations  15.2 us (2%)
  starting transfers between devices  13 us (2%)
    pallas_call x1, Pallas kernels, expert_layer(): pl.pallas_call(functools.partial(expert_kernel, sizes), out_shape=(every,...  348 us
    dot_general x8, matrix products, dot(): lax.dot_general(left, right, (dims, ((), ())), preferred_element_type=F32)  83.5 us
    pallas_call x1, Pallas kernels, gather_inputs(): pl.pallas_call(functools.partial(gather_kernel, parts), out_shape=tuple((...  62.7 us
    pallas_call x1, Pallas kernels, scatter_grads(): pl.pallas_call(functools.partial(scatter_kernel, parts), out_shape=(jax.S...  51.5 us
    ppermute x11, waiting for transfers between devices, swap(): return lax.ppermute(value, axis, [(i, i ^ bit) for i in range(size)])  36 us
    reduce_scatter x1, waiting for transfers between devices, shards(): lax.psum_scatter(dot(attended, output_weight, NN).astype(BF16), 'tp', sca...  30.5 us
  transfers between devices with their start and end apart: 14, of which 5 were waited for; matrix products, arithmetic and copies ran while one was open for 21% of the time, Pallas kernels for 7%

profile of v1, /device:TPU:0, one launch (start us, length us, event | category | flops | bytes accessed | tf_op | source)
XLA Modules:
  0.0 769.1 jit_solution(11567901657890792999)
XLA Ops:
  17.9 62.7 %gather_inputs.1 = (bf16[512,2048]{1,0:T(8,128)(2,1)}, bf16[2048,896]{1,0:T(8,128)(2,1)}, bf16[512,2048]{1,0:T(8,128)(2,1)}, bf16[4096,128]{1,0:T(8,128)(2,1)}, ...) custom-call(bf16[128,2048]{1,0:T(8,128)(2,1)} %refs_0_.1, ...), custom_call_target="tpu_custom_call" | custom-call | tf_op jit(solution)/shard_map/gather_inputs/pallas_call | solution.py:838
  84.9 6.2 copy.114
  92.2 4.0 fusion.18
  103.2 2.8 fusion.28
  109.0 4.4 collective-permute-start.2
  114.4 19.3 %collective-permute-done.2 = bf16[128,2048]{1,0:T(8,128)(2,1)S(1)} collective-permute-done((bf16[128,2048]{1,0:T(8,128)(2,1)S(1)}, bf16[128,2048]{1,0:T(8,128)(2,1)S(1)}, u32[]{:S(2)}, u32[]{:S(2)}) %collective-permute-start.2) | collective-permute-done | bytes 524320 | tf_op jit(solution)/shard_map/ppermute | solution.py:72
  136.4 30.5 %reduce-scatter.3.cloned.1.call-done = bf16[128,2048]{1,0:T(8,128)(2,1)} async-done(((bf16[512,2048]{1,0:T(8,128)(2,1)}), bf16[128,2048]{1,0:T(8,128)(2,1)}) %reduce-scatter.3.cloned.1.call-update) | async-done | bytes 524304 | tf_op jit(solution)/shard_map/reduce_scatter | solution.py:1091
  170.2 348.1 %experts.1 = (bf16[8,512,2048]{2,1,0:T(8,128)(2,1)}, bf16[8,512,2048]{2,1,0:T(8,128)(2,1)}, bf16[8,512,896]{2,1,0:T(8,128)(2,1)}, bf16[8,512,1920]{2,1,0:T(8,128...) custom-call(bf16[128,2048]{1,0:T(8,128)(2,1)} %multiply_convert_fusion.refs_0_, ...), custom_call_target="tpu_custom_call" | custom-call | flops 94489280512 | bytes 120000000 | tf_op jit(solution)/shard_map/experts/pallas_call | solution.py:599
  522.7 19.9 %convolution_bitcast_fusion = f32[896,2048]{1,0:T(8,128)S(1)} fusion(bf16[8,512,896]{2,1,0:T(8,128)(2,1)} %get-tuple-element.63, bf16[8,512,2048]{2,1,0:T(8,128)(2,1)} %get-tuple-element.64), kind=kOutput, calls=%fused_computation.24 | convolution fusion | flops 15032385536 | bytes 31457280 | tf_op jit(solution)/shard_map/dot_general | solution.py:62
  542.6 13.3 %add_convert_fusion = (bf16[1,512,2048]{2,1,0:T(8,128)(2,1)S(1)}, bf16[1,512,2048]{2,1,0:T(8,128)(2,1)S(1)}, bf16[1,512,2048]{2,1,0:T(8,128)(2,1)S(1)}) fusion(bf16[4,512,2048]{2,1,0:T(8,128)(2,1)} %collective-permute-done.3, bf16[4,512,2048]{2,1,0:T(8,128)(2,1)S(1)} %bitcast.202), kind=kLoop, calls=%fused_computation.19 | loop fusion | flops 12582912 | bytes 18874368 | tf_op jit(solution)/shard_map/convert_element_type | solution.py:653
  560.7 2.9 pad_maximum_fusion
  567.8 15.4 %collective-permute-done.5 = bf16[256,2048]{1,0:T(8,128)(2,1)S(1)} collective-permute-done((bf16[256,2048]{1,0:T(8,128)(2,1)}, bf16[256,2048]{1,0:T(8,128)(2,1)S(1)}, u32[]{:S(2)}, u32[]{:S(2)}) %collective-permute-start.5) | collective-permute-done | bytes 1048608 | tf_op jit(solution)/shard_map/ppermute | solution.py:72
  584.5 3.5 convolution_convert_fusion.4
  599.8 5.1 convolution_convert_fusion.2
  605.0 2.8 pad_maximum_fusion.11
  611.5 43.3 %fusion.78 = (bf16[1920,2048]{1,0:T(8,128)(2,1)}, f32[1920,2048]{1,0:T(8,128)}) fusion(bf16[4096,1920]{1,0:T(8,128)(2,1)} %bitcast.225, bf16[4096,2048]{1,0:T(8,128)(2,1)} %bitcast.224), kind=kOutput, calls=%fused_computation.150 | convolution fusion | flops 32216186880 | bytes 56098816 | tf_op jit(solution)/shard_map/dot_general | solution.py:62
  656.2 8.3 %fusion.73 = (f32[128,2048]{1,0:T(8,128)S(1)}, f32[128,2048]{1,0:T(8,128)}, f32[128,2048]{1,0:T(8,128)}, f32[128,2048]{1,0:T(8,128)}, f32[128,2048]{1,0:T(8,128)...) fusion(f32[1920,2048]{1,0:T(8,128)} %get-tuple-element.196), kind=kLoop, calls=%fused_computation.145 | loop fusion | bytes 25165824 | tf_op jit(solution)/shard_map/slice | solution.py:1179
  664.5 2.8 fusion.13
  668.6 2.9 maximum_bitcast_fusion.1
  672.4 2.9 maximum_bitcast_fusion
  675.3 3.8 convolution_convert_fusion
  681.3 7.9 %fusion.71 = (bf16[512,2048]{1,0:T(8,128)(2,1)S(1)}, f32[512,2048]{1,0:T(8,128)}) fusion(bf16[512,2048]{1,0:T(8,128)(2,1)} %collective-permute-done.7, bf16[512,2048]{1,0:T(8,128)(2,1)} %collective-permute-done.6, bf16[4,512,2048]{2,1,0:T(8,128)(2,1)} %collective-permute-done.3, bf16[4,512,2048]{2,1,0:T(8,128)(2,1)} %get-tuple-element.61), kind=kLoop, calls=%fused_computation.144 | loop fusion | flops 10485760 | bytes 14680064 | tf_op jit(solution)/shard_map/convert_element_type | solution.py:672
  697.7 51.5 %scatter_grads.1 = (f32[256,896]{1,0:T(8,128)S(1)}, f32[512,256]{1,0:T(8,128)S(1)}, bf16[8,96,256]{2,1,0:T(8,128)(2,1)S(1)}, bf16[8,96,256]{2,1,0:T(8,128)(2,1)S(1)}, bf16[8,96,256]{2,1,0:T(8,128)(2,1)S(1)}) custom-call(bf16[2048,896]{1,0:T(8,128)(2,1)S(1)} %fusion.11.refs_0_, bf16[512,2048]{1,0:T(8,128)(2,1)S(1)} %convolution_convert_fusion.1.refs_1_, ...), custom_call_target="tpu_custom_call" | custom-call | tf_op jit(solution)/shard_map/scatter_grads/pallas_call | solution.py:964
  757.4 4.0 fusion.45
  (209 shorter events, 85.7 us)
Async XLA Ops:
  7.2 9.9 %copy-start.38 = (bf16[704,256]{1,0:T(8,128)(2,1)S(1)}, bf16[704,256]{1,0:T(8,128)(2,1)}, u32[]{:S(2)}) copy-start(bf16[704,256]{1,0:T(8,128)(2,1)} %param.30) | copy-start | bytes 1081348
  7.2 73.4 %copy-start.20 = (bf16[128,2048]{1,0:T(8,128)(2,1)S(1)}, bf16[128,2048]{1,0:T(8,128)(2,1)}, u32[]{:S(2)}) copy-start(bf16[128,2048]{1,0:T(8,128)(2,1)} %param.18) | copy-start | bytes 1572868
  7.2 73.6 %copy-start.41 = (s32[512]{0:T(512)S(1)}, s32[512]{0:T(512)}, u32[]{:S(2)}) copy-start(s32[512]{0:T(512)} %param.19) | copy-start | bytes 6148
  7.2 159.6 %reduce-scatter.3.cloned.1.call-start = ((), (), s32[]{:S(2)}) async-start(), calls=%async_computation.2 | async-start | bytes 2621440 | tf_op jit(solution)/shard_map/reduce_scatter | solution.py:1091
  80.6 25.4 %collective-permute-start.1 = (bf16[128,2048]{1,0:T(8,128)(2,1)S(1)}, bf16[128,2048]{1,0:T(8,128)(2,1)}, u32[]{:S(2)}, u32[]{:S(2)}) collective-permute-start(bf16[128,2048]{1,0:T(8,128)(2,1)S(1)} %copy-done.20), channel_id=1, source_target_pairs={{0,2},{1,3},{2,0},{3,1},{4,6},{5,7},{6,4},{7,5},{8,10},{9,11},{10,... | collective-permute-start | bytes 1572872 | tf_op jit(solution)/shard_map/ppermute | solution.py:72
  80.7 25.3 %collective-permute-start = (bf16[128,2048]{1,0:T(8,128)(2,1)S(1)}, bf16[128,2048]{1,0:T(8,128)(2,1)}, u32[]{:S(2)}, u32[]{:S(2)}) collective-permute-start(bf16[128,2048]{1,0:T(8,128)(2,1)S(1)} %copy-done.20), channel_id=1, source_target_pairs={{0,1},{1,0},{2,3},{3,2},{4,5},{5,4},{6,7},{7,6},{8,9},{9,8},{10,11... | collective-permute-start | bytes 1572872 | tf_op jit(solution)/shard_map/ppermute | solution.py:72
  108.7 58.2 %copy-start.6 = (bf16[128,2048]{1,0:T(8,128)(2,1)S(1)}, bf16[128,2048]{1,0:T(8,128)(2,1)}, u32[]{:S(2)}) copy-start(bf16[128,2048]{1,0:T(8,128)(2,1)} %refs_0_.1) | copy-start | bytes 1572868
  108.7 459.1 %all-gather.2.cloned.1.call-start = ((), (), s32[]{:S(2)}) async-start(), calls=%async_computation.3 | async-start | bytes 2621440 | tf_op jit(solution)/shard_map/all_gather | solution.py:1147
  109.0 24.6 %collective-permute-start.2 = (bf16[128,2048]{1,0:T(8,128)(2,1)S(1)}, bf16[128,2048]{1,0:T(8,128)(2,1)S(1)}, u32[]{:S(2)}, u32[]{:S(2)}) collective-permute-start(bf16[128,2048]{1,0:T(8,128)(2,1)S(1)} %copy-done.20), channel_id=1, source_target_pairs={{0,3},{1,2},{2,1},{3,0},{4,7},{5,6},{6,5},{7,4},{8,11},{9,10},{10,... | collective-permute-start | bytes 1572872 | tf_op jit(solution)/shard_map/ppermute | solution.py:72
  170.2 348.2 %copy-start.9 = (bf16[128,2048]{1,0:T(8,128)(2,1)S(1)}, bf16[128,2048]{1,0:T(8,128)(2,1)}, u32[]{:S(2)}) copy-start(bf16[128,2048]{1,0:T(8,128)(2,1)} %reduce-scatter.3.cloned.1.call-done) | copy-start | bytes 1572868
  518.3 24.3 %collective-permute-start.3 = (bf16[4,512,2048]{2,1,0:T(8,128)(2,1)}, bf16[4,512,2048]{2,1,0:T(8,128)(2,1)}, u32[]{:S(2)}, u32[]{:S(2)}) collective-permute-start(bf16[4,512,2048]{2,1,0:T(8,128)(2,1)} %get-tuple-element.62), channel_id=1, source_target_pairs={{0,4},{4,0},{8,12},{12,8},{16,20},{20,16},{24,28},{28,24},{1,5},{5... | collective-permute-start | bytes 25165832 | tf_op jit(solution)/shard_map/ppermute | solution.py:72
  522.6 157.5 %reduce-scatter.5.cloned.1.call-start = ((), (), s32[]{:S(2)}) async-start(), calls=%async_computation.4 | async-start | bytes 2621440 | tf_op jit(solution)/shard_map/reduce_scatter | solution.py:1171
  522.6 20.0 %slice-start = ((s8[8388608]{0:T(1024)(128)(4,1)}), s8[4194304]{0:T(1024)(128)(4,1)S(1)}, s32[]{:S(2)}) async-start(s8[8388608]{0:T(1024)(128)(4,1)} %bitcast.201), calls=%async_computation.5 | async-start | bytes 8388608
  522.6 20.0 %slice-start.1 = ((s8[8388608]{0:T(1024)(128)(4,1)}), s8[4194304]{0:T(1024)(128)(4,1)S(1)}, s32[]{:S(2)}) async-start(s8[8388608]{0:T(1024)(128)(4,1)} %bitcast.201), calls=%async_computation.6 | async-start | bytes 8388608
  557.5 25.7 %collective-permute-start.5 = (bf16[256,2048]{1,0:T(8,128)(2,1)}, bf16[256,2048]{1,0:T(8,128)(2,1)S(1)}, u32[]{:S(2)}, u32[]{:S(2)}) collective-permute-start(bf16[256,2048]{1,0:T(8,128)(2,1)} %get-tuple-element.176), channel_id=1, source_target_pairs={{0,8},{4,12},{8,0},{12,4},{16,24},{20,28},{24,16},{28,20},{1,9},{5... | collective-permute-start | bytes 3145736 | tf_op jit(solution)/shard_map/ppermute | solution.py:72
  559.0 25.6 %collective-permute-start.4 = (bf16[256,2048]{1,0:T(8,128)(2,1)}, bf16[256,2048]{1,0:T(8,128)(2,1)}, u32[]{:S(2)}, u32[]{:S(2)}) collective-permute-start(bf16[256,2048]{1,0:T(8,128)(2,1)} %get-tuple-element.177), channel_id=1, source_target_pairs={{0,16},{4,20},{8,24},{12,28},{16,0},{20,4},{24,8},{28,12},{1,17},{... | collective-permute-start | bytes 3145736 | tf_op jit(solution)/shard_map/ppermute | solution.py:72
  567.8 20.2 %copy-start.5 = (f32[512,512,4]{1,0,2:T(8,128)S(1)}, f32[512,512,4]{1,0,2:T(8,128)}, u32[]{:S(2)}) copy-start(f32[512,512,4]{1,0,2:T(8,128)} %copy-done.4) | copy-start | bytes 12582916
  607.8 73.5 %collective-permute-start.7 = (bf16[512,2048]{1,0:T(8,128)(2,1)}, bf16[512,2048]{1,0:T(8,128)(2,1)}, u32[]{:S(2)}, u32[]{:S(2)}) collective-permute-start(bf16[512,2048]{1,0:T(8,128)(2,1)} %pad_maximum_fusion.11), channel_id=1, source_target_pairs={{0,16},{4,20},{8,24},{12,28},{16,0},{20,4},{24,8},{28,12},{1,17},{... | collective-permute-start | bytes 6291464 | tf_op jit(solution)/shard_map/ppermute | solution.py:72
  610.5 70.8 %collective-permute-start.6 = (bf16[512,2048]{1,0:T(8,128)(2,1)}, bf16[512,2048]{1,0:T(8,128)(2,1)}, u32[]{:S(2)}, u32[]{:S(2)}) collective-permute-start(bf16[512,2048]{1,0:T(8,128)(2,1)} %pad_maximum_fusion.10), channel_id=1, source_target_pairs={{0,8},{4,12},{8,0},{12,4},{16,24},{20,28},{24,16},{28,20},{1,9},{5... | collective-permute-start | bytes 6291464 | tf_op jit(solution)/shard_map/ppermute | solution.py:72
  611.5 43.3 %copy-start.45 = (bf16[512,2048]{1,0:T(8,128)(2,1)S(1)}, bf16[512,2048]{1,0:T(8,128)(2,1)}, u32[]{:S(2)}) copy-start(bf16[512,2048]{1,0:T(8,128)(2,1)} %all-gather.2.cloned.1.call-done) | copy-start | bytes 6291460
  611.5 43.4 %copy-start.47 = (bf16[128,4,512]{2,0,1:T(8,128)(2,1)S(1)}, bf16[128,4,512]{2,0,1:T(8,128)(2,1)}, u32[]{:S(2)}) copy-start(bf16[128,4,512]{2,0,1:T(8,128)(2,1)} %copy-done.46) | copy-start | bytes 1572868
  690.7 66.7 %collective-permute-start.8 = (bf16[128,2048]{1,0:T(8,128)(2,1)}, bf16[128,2048]{1,0:T(8,128)(2,1)}, u32[]{:S(2)}, u32[]{:S(2)}) collective-permute-start(bf16[128,2048]{1,0:T(8,128)(2,1)} %get-tuple-element.173), channel_id=1, source_target_pairs={{0,1},{1,0},{2,3},{3,2},{4,5},{5,4},{6,7},{7,6},{8,9},{9,8},{10,11... | collective-permute-start | bytes 1572872 | tf_op jit(solution)/shard_map/ppermute | solution.py:72
  690.8 66.6 %collective-permute-start.10 = (bf16[128,2048]{1,0:T(8,128)(2,1)}, bf16[128,2048]{1,0:T(8,128)(2,1)}, u32[]{:S(2)}, u32[]{:S(2)}) collective-permute-start(bf16[128,2048]{1,0:T(8,128)(2,1)} %get-tuple-element.174), channel_id=1, source_target_pairs={{0,3},{1,2},{2,1},{3,0},{4,7},{5,6},{6,5},{7,4},{8,11},{9,10},{10,... | collective-permute-start | bytes 1572872 | tf_op jit(solution)/shard_map/ppermute | solution.py:72
  692.4 64.9 %collective-permute-start.9 = (bf16[128,2048]{1,0:T(8,128)(2,1)}, bf16[128,2048]{1,0:T(8,128)(2,1)}, u32[]{:S(2)}, u32[]{:S(2)}) collective-permute-start(bf16[128,2048]{1,0:T(8,128)(2,1)} %get-tuple-element.175), channel_id=1, source_target_pairs={{0,2},{1,3},{2,0},{3,1},{4,6},{5,7},{6,4},{7,5},{8,10},{9,11},{10,... | collective-permute-start | bytes 1572872 | tf_op jit(solution)/shard_map/ppermute | solution.py:72
  (41 other events, 164.7 us)
Sparse Core Ops, SparseCore 0:
  108.8 57.9 reduce-scatter.2
  522.7 45.0 all-gather.1
  605.1 42.0 reduce-scatter.4

commit v2 on v1

--- a/solution.py
+++ b/solution.py
@@ -76,6 +76,7 @@
 GROUP = len(ORDER)
 LANES = 128
 ROW_CHUNK = 64
+SUM_CHUNK = 16
 
 
 def expert_kernel(sizes, *refs):
@@ -87,17 +88,23 @@
         del refs[:count]
         return taken
 
-    rows_ref, grads_ref, mask_hbm, gate_hbm, up_hbm, down_hbm = take(6)
+    rows_ref, grads_ref, grads_x, grads_y, mask_hbm, gate_hbm, up_hbm, down_hbm = take(8)
     shared_gate_hbm, shared_up_hbm, shared_down_hbm, router_hbm = take(4)
-    all_rows, all_grads, act_hbm, wide_grad_hbm, out_even, out_odd, back_ref = take(7)
-    wide_v, wide_t, down_v, rows_v, grads_v, mask_v, d_act_v, act_v, wide_grad_v = take(9)
+    all_rows, all_grads, act_hbm, gate_grad_hbm, up_grad_hbm = take(5)
+    out_even, out_odd, d_act_hbm, back_ref = take(4)
+    wide_v, down_v, rows_v, grads_v, mask_v, d_act_v, act_v, wide_grad_v = take(8)
     probs_v, gates_v, total_v, out_v, back_v, own_v, core_v, relay_v, cross_v, line_in, line_out = take(11)
-    send, recv, local, weight_sem, mask_sem = take(5)
+    send, recv, local, weight_sem, mask_sem, d_act_sem, act_sem, out_sem = take(8)
     quarter = rows_ref.shape[0]
     seq_len = parts * quarter
     half_rows = seq_len // 2
     inner = down_v.shape[0]
     wide = wide_v.shape[0]
+    padded = expert_tiles * LANES
+    shared_padded = shared_tiles * LANES
+    first_part = 2 * padded
+    shared_place = 2 * local_experts * padded
+    router_place = shared_place + shared_padded
     exp_index = lax.axis_index("exp")
     tp_index = lax.axis_index("tp")
     slot = {r: s for s, r in enumerate(ORDER)}
@@ -134,16 +141,14 @@
             relay_v.at[side],
             chip(4 - 2 * side),
         )
+    kept_grads = {0: grads_ref, 2: grads_x, 4: grads_y}
     for h in range(2):
         part_h = pl.ds(h * half_rows, half_rows)
-        mine = grads_ref.at[part_h]
-        copies["gx", h] = (mine, all_grads.at[slot[2], part_h], chip(2))
-        copies["gy", h] = (mine, all_grads.at[slot[4], part_h], chip(4))
         via = 4 * h + 2 * (1 - h)
-        copies["gd", h] = (all_grads.at[slot[via], part_h], all_grads.at[slot[6], part_h], chip(6 - via))
-        for r in (0, 2, 4, 6):
-            here = mine if r == 0 else all_grads.at[slot[r], part_h]
-            copies["gc", r, h] = (here, all_grads.at[slot[r + 1], part_h], chip(1))
+        copies["gd", h] = (kept_grads[via].at[part_h], all_grads.at[slot[6], part_h], chip(6 - via))
+        copies["gc", 6, h] = (all_grads.at[slot[6], part_h], all_grads.at[slot[7], part_h], chip(1))
+    for r, ref in kept_grads.items():
+        copies["gc", r, 0] = (ref, all_grads.at[slot[r + 1]], chip(1))
     number = {name: k for k, name in enumerate(copies)}
 
     def remote(*name):
@@ -163,8 +168,8 @@
         pl.semaphore_signal(barrier, inc=1, device_id=peer, device_id_type=pl.DeviceIdType.MESH)
     pl.semaphore_wait(barrier, len(peers))
 
-    for k in range(1, parts):
-        remote("z", k).start()
+    own_copy = pltpu.make_async_copy(rows_ref, all_rows.at[slot[0], part(0)], local.at[0])
+    own_copy.start()
 
     def spread(q):
         remote("x" if 2 * q < parts else "y", q).start()
@@ -173,46 +178,44 @@
     def spread_rest(q):
         remote("y" if 2 * q < parts else "x", q).start()
 
+    for k in range(1, parts):
+        remote("z", k).start()
     spread(0)
-    own_copy = pltpu.make_async_copy(rows_ref, all_rows.at[slot[0], part(0)], local.at[0])
-    padded = expert_tiles * LANES
     hidden = down_hbm.shape[1]
     shared_rows = shared_down_hbm.shape[0]
     weights = [(shared_down_hbm, down_v.at[pl.ds(local_experts * padded, shared_rows)])]
-    weights.append((router_hbm, wide_v.at[pl.ds(wide - LANES, LANES)]))
+    weights.append((router_hbm, wide_v.at[pl.ds(router_place, LANES)]))
     blanks = [(down_v, local_experts * padded + shared_rows, inner)]
 
-    def load_tiles(source, count, first_tile, side):
-        for k in range(-(-count // LANES)):
-            rows = min(LANES, count - k * LANES)
-            place = (2 * (first_tile + k) + side) * LANES
-            weights.append((source.at[pl.ds(k * LANES, rows)], wide_v.at[pl.ds(place, rows)]))
-            blanks.append((wide_v, place + rows, place + LANES))
+    def load_part(source, count, place):
+        weights.append((source, wide_v.at[pl.ds(place, count)]))
+        blanks.append((wide_v, place + count, place + -(-count // LANES) * LANES))
 
     for e in range(local_experts):
         weights.append((down_hbm.at[e], down_v.at[pl.ds(e * padded, hidden)]))
         blanks.append((down_v, e * padded + hidden, (e + 1) * padded))
-        load_tiles(gate_hbm.at[e], hidden, e * expert_tiles, 0)
-        load_tiles(up_hbm.at[e], hidden, e * expert_tiles, 1)
-    load_tiles(shared_gate_hbm, shared_rows, local_experts * expert_tiles, 0)
-    load_tiles(shared_up_hbm, shared_rows, local_experts * expert_tiles, 1)
+        load_part(gate_hbm.at[e], hidden, 2 * e * padded)
+        load_part(up_hbm.at[e], hidden, (2 * e + 1) * padded)
+    load_part(shared_gate_hbm, shared_rows, shared_place)
+    load_part(shared_up_hbm, shared_rows, router_place + LANES)
     weight_copies = [
         pltpu.make_async_copy(source, target, weight_sem.at[k])
         for k, (source, target) in enumerate(weights)
     ]
-    own_grads = pltpu.make_async_copy(grads_ref, all_grads.at[slot[0]], local.at[1])
-
-    def load_grads(u):
-        return pltpu.make_async_copy(all_grads.at[u], grads_v, local.at[2])
+    grads_copies = [
+        pltpu.make_async_copy(ref, all_grads.at[slot[r]], local.at[1 + k])
+        for k, (r, ref) in enumerate(kept_grads.items())
+    ]
 
     def load_rows(u):
         return pltpu.make_async_copy(all_rows.at[u], rows_v, local.at[6])
 
+    for r in kept_grads:
+        remote("gc", r, 0).start()
     for h in range(2):
-        remote("gx", 0).start() if h == 0 else remote("gy", 1).start()
-        remote("gc", 0, h).start()
-    own_copy.start()
-    own_grads.start()
+        remote("gd", h).start()
+    for copy in grads_copies:
+        copy.start()
     for copy in weight_copies:
         copy.start()
     for ref, first, last in blanks:
@@ -235,35 +238,52 @@
         remote("d", q).wait_recv()
         remote("c", 6, q).start()
 
-    own_grads.wait()
-    load_grads(0).start()
     half_parts = parts // 2
+
+    def d_act_store(s, into):
+        return pltpu.make_async_copy(d_act_v.at[into], d_act_hbm.at[s], d_act_sem.at[into])
+
+    def d_act_load(u, into):
+        return pltpu.make_async_copy(d_act_hbm.at[u], d_act_v.at[into], d_act_sem.at[into])
 
     for copy in weight_copies:
         copy.wait()
 
-    def turn(j, _):
-        place = pl.ds(pl.multiple_of(j * LANES, LANES), LANES)
-        wide_t[:, place] = wide_v[place, :].T
-        return 0
-
-    lax.fori_loop(0, wide // LANES, turn, 0)
-
-    def arrived_grads(h):
-        remote("gx" if h == 0 else "gy", h).wait_recv()
-        remote("gd", h).start()
-        remote("gc", 2 + 2 * h, h).start()
-
-    for q in range(1, parts):
-        remote("z", q).wait_recv()
-        spread(q)
-        if q == half_parts - 1:
-            arrived_grads(0)
-            arrived_grads(1)
-        if q >= half_parts:
-            arrived_x(q - half_parts)
+    def first_product(k, r):
+        if r == 6:
+            for h in range(2):
+                remote("gd", h).wait_recv()
+                remote("gc", 6, h).start()
+        elif r == 7:
+            for h in range(2):
+                remote("gc", 6, h).wait_recv()
+        elif r % 2:
+            remote("gc", r - 1, 0).wait_recv()
+        source = kept_grads.get(r, all_grads.at[slot[r]])
+        load = pltpu.make_async_copy(source, grads_v, local.at[5])
+        load.start()
+        if k >= 2:
+            d_act_store(0, k % 2).wait()
+        load.wait()
+        for first in range(0, inner, 512):
+            columns = pl.ds(first, min(512, inner - first))
+            d_act_v[k % 2, :, columns] = dot(grads_v[...], down_v[columns, :], NT)
+        d_act_store(slot[r], k % 2).start()
+
+    arrivals = {2: 1, 5: 2, 7: 3}
+    for k, r in enumerate((0, 1, 2, 3, 4, 5, 6, 7)):
+        first_product(k, r)
+        q = arrivals.get(k, parts)
+        if q < parts:
+            remote("z", q).wait_recv()
+            spread(q)
+            if q >= half_parts:
+                arrived_x(q - half_parts)
     own_copy.wait()
     load_rows(0).start()
+    for k in range(2):
+        d_act_store(0, k).wait()
+    d_act_load(0, 0).start()
 
     def mask_loads(r):
         from_exp = (lax.rem(exp_index, GROUP) ^ r) * seq_len
@@ -277,30 +297,42 @@
         ]
 
     def act_store(u):
-        return pltpu.make_async_copy(act_v, act_hbm.at[u], local.at[3])
-
-    def wide_store(u):
-        return pltpu.make_async_copy(wide_grad_v, wide_grad_hbm.at[u], local.at[4])
+        into = u % 2
+        return pltpu.make_async_copy(act_v.at[into], act_hbm.at[u], act_sem.at[into])
+
+    def act_load(u):
+        into = u % 2
+        return pltpu.make_async_copy(act_hbm.at[u], act_v.at[into], act_sem.at[into])
+
+    def wide_stores(u):
+        return [
+            pltpu.make_async_copy(
+                wide_grad_v.at[:, pl.ds(0, first_part)], gate_grad_hbm.at[u], local.at[4]
+            ),
+            pltpu.make_async_copy(
+                wide_grad_v.at[:, pl.ds(first_part, wide - first_part)], up_grad_hbm.at[u], local.at[7]
+            ),
+        ]
 
     def out_store(s):
         kept = out_odd if ORDER[s] % 2 else out_even
-        return pltpu.make_async_copy(out_v, kept.at[ORDER[s] // 2], local.at[5])
+        return pltpu.make_async_copy(out_v.at[s % 2], kept.at[ORDER[s] // 2], out_sem.at[s % 2])
 
     def add_into(target, others):
         def chunk(i, _):
             total = None
             for ref, first in [target] + others:
-                rows = pl.ds(pl.multiple_of(first + i * ROW_CHUNK, ROW_CHUNK), ROW_CHUNK)
+                rows = pl.ds(pl.multiple_of(first + i * SUM_CHUNK, SUM_CHUNK), SUM_CHUNK)
                 value = ref[rows].astype(F32)
                 total = value if total is None else total + value
             ref, first = target
-            ref[pl.ds(pl.multiple_of(first + i * ROW_CHUNK, ROW_CHUNK), ROW_CHUNK)] = total.astype(BF16)
+            ref[pl.ds(pl.multiple_of(first + i * SUM_CHUNK, SUM_CHUNK), SUM_CHUNK)] = total.astype(BF16)
             return 0
 
         return chunk
 
     def sum_rows(count, target, others):
-        lax.fori_loop(0, count // ROW_CHUNK, add_into(target, others), 0)
+        lax.fori_loop(0, count // SUM_CHUNK, add_into(target, others), 0)
 
     def unit(u, _):
         into = lax.rem(u, 2)
@@ -311,28 +343,23 @@
                 for load in mask_loads(ORDER[s]):
                     load.start()
 
-        load_grads(u).wait()
-        grads = grads_v
-
-        def d_act_tile(first, width):
-            d_act_v[:, pl.ds(first, width)] = dot(
-                grads[...], down_v[pl.ds(first, width), :], NT
-            )
-
-        for first in range(0, inner, 512):
-            d_act_tile(first, min(512, inner - first))
         load_rows(u).wait()
         for load in mask_loads(0):
             load.wait()
 
+        d_act_load(u, into).wait()
+
+        @pl.when(u > 1)
+        def _():
+            act_store(u - 2).wait()
+
         @pl.when(u > 0)
         def _():
-            act_store(u - 1).wait()
-            wide_store(u - 1).wait()
-
-        shared_first = local_experts * expert_tiles
-        linear = dot(rows_v[...], wide_t[:, shared_first * 256 :], NN)
-        logits = linear[:, shared_tiles * 256 :]
+            for store in wide_stores(u - 1):
+                store.wait()
+
+        linear = dot(rows_v[...], wide_v[shared_place:, :], NT)
+        logits = linear[:, shared_padded : shared_padded + LANES]
         lane = lax.broadcasted_iota(jnp.int32, logits.shape, 1)
         logits = jnp.where(lane < experts_all, logits, -1e30)
         raised = jnp.exp(logits - jnp.max(logits, axis=1, keepdims=True))
@@ -343,36 +370,38 @@
         probs_v[...] = probs
         gates_v[...] = chosen / chosen_sum
 
-        def tile(linear, at, j, gate):
+        def tile(linear, at_gate, at_up, place, j, gate):
             one = pl.ds(j * LANES, LANES)
             for first in range(0, seq_len, ROW_CHUNK):
                 last = first + ROW_CHUNK
-                gate_lin = linear[first:last, at : at + LANES]
-                up_lin = linear[first:last, at + LANES : at + 256]
-                sigmoid = 1.0 / (1.0 + jnp.exp(-gate_lin))
+                gate_lin = linear[first:last, at_gate : at_gate + LANES]
+                up_lin = linear[first:last, at_up : at_up + LANES]
+                sigmoid = 0.5 * jnp.tanh(0.5 * gate_lin) + 0.5
                 silu = gate_lin * sigmoid
                 act = silu * up_lin
-                d_act = d_act_v[first:last, one]
+                d_act = d_act_v[into, first:last, one]
                 if gate is not None:
-                    total_v[first:last] += act.astype(BF16).astype(F32) * d_act
+                    total_v[first:last] += act * d_act
                     act = act * gate[first:last]
                     d_act = d_act * gate[first:last]
-                act_v[first:last, one] = act.astype(BF16)
-                d_gate = d_act * up_lin * (sigmoid * (1.0 + gate_lin * (1.0 - sigmoid)))
-                wide_grad_v[first:last, pl.ds(j * 256, LANES)] = d_gate.astype(BF16)
-                wide_grad_v[first:last, pl.ds(j * 256 + LANES, LANES)] = (d_act * silu).astype(BF16)
+                act_v[into, first:last, one] = act.astype(BF16)
+                d_up = d_act * silu
+                d_gate = d_act * up_lin * (sigmoid + silu * (1.0 - sigmoid))
+                wide_grad_v[first:last, pl.ds(place + at_gate, LANES)] = d_gate.astype(BF16)
+                wide_grad_v[first:last, pl.ds(place + at_up, LANES)] = d_up.astype(BF16)
 
         for k in range(shared_tiles):
-            tile(linear, k * 256, shared_first + k, None)
+            at_up = shared_padded + LANES + k * LANES
+            tile(linear, k * LANES, at_up, shared_place, local_experts * expert_tiles + k, None)
         d_gates = jnp.zeros(logits.shape, F32)
         for e in range(local_experts):
             mine = lane == exp_index * local_experts + e
             gate = jnp.sum(jnp.where(mine, gates_v[...], 0.0), axis=1, keepdims=True)
             total_v[...] = jnp.zeros(logits.shape, F32)
-            first_tile = e * expert_tiles
-            linear = dot(rows_v[...], wide_t[:, first_tile * 256 : (first_tile + expert_tiles) * 256], NN)
+            place = 2 * e * padded
+            linear = dot(rows_v[...], wide_v[place : place + 2 * padded, :], NT)
             for k in range(expert_tiles):
-                tile(linear, k * 256, first_tile + k, gate)
+                tile(linear, k * LANES, padded + k * LANES, place, e * expert_tiles + k, gate)
             d_gates = jnp.where(mine, jnp.sum(total_v[...], axis=1, keepdims=True), d_gates)
         probs, gates, mask = probs_v[...], gates_v[...], mask_v[...].astype(F32)
         chosen_sum = jnp.sum(probs * mask, axis=1, keepdims=True)
@@ -382,35 +411,36 @@
         d_logits = probs * (d_probs - jnp.sum(d_probs * probs, axis=1, keepdims=True))
         high = d_logits.astype(BF16)
         low = pltpu.roll(d_logits - high.astype(F32), experts_all, 1)
-        wide_grad_v[:, pl.ds(wide - LANES, LANES)] = jnp.where(
+        wide_grad_v[:, pl.ds(router_place, LANES)] = jnp.where(
             lane < experts_all, high.astype(F32), low
         ).astype(BF16)
         act_store(u).start()
-        wide_store(u).start()
+        for store in wide_stores(u):
+            store.start()
+
+        @pl.when(u < GROUP - 1)
+        def _():
+            d_act_load(u + 1, 1 - into).start()
 
         @pl.when(u == 0)
         def _():
-            remote("gd", 0).wait_recv()
-            remote("gc", 6, 0).start()
+            for q in range(half_parts, parts):
+                arrived_y(q)
+            for q in range(parts):
+                spread_rest(q)
 
         @pl.when(u == 1)
         def _():
-            remote("gd", 1).wait_recv()
-            remote("gc", 6, 1).start()
             for q in range(half_parts):
                 arrived_far(q)
 
         @pl.when(u == 3)
         def _():
-            remote("gx", 1).wait_recv()
-            remote("gc", 2, 1).start()
             for q in range(half_parts, parts):
                 arrived_x(q)
 
         @pl.when(u == 4)
         def _():
-            remote("gy", 0).wait_recv()
-            remote("gc", 4, 0).start()
             for q in range(half_parts):
                 arrived_y(q)
 
@@ -492,19 +522,7 @@
             for q in range(parts - 1, -1, -1):
                 remote("s", 4, q).start()
 
-        @pl.when(u == 0)
-        def _():
-            for q in range(half_parts, parts):
-                arrived_y(q)
-            remote("gy", 0).start()
-            remote("gx", 1).start()
-            for q in range(parts):
-                spread_rest(q)
-                remote("c", 0, q).wait_recv()
-            for h in range(2):
-                remote("gc", 0, h).wait_recv()
-
-        for k, r in ((1, 6), (3, 2), (5, 4)):
+        for k, r in ((0, 0), (1, 6), (3, 2), (5, 4)):
             @pl.when(u == k)
             def _(k=k, r=r):
                 if k == 1:
@@ -512,21 +530,62 @@
                         arrived_far(q)
                 for q in range(parts):
                     remote("c", r, q).wait_recv()
-                for h in range(2):
-                    remote("gc", r, h).wait_recv()
 
         @pl.when(u < GROUP - 1)
         def _():
-            load_grads(u + 1).start()
             load_rows(u + 1).start()
 
-        @pl.when(u > 0)
-        def _():
-            out_store(0).wait()
+        return 0
+
+    lax.fori_loop(0, GROUP, unit, 0)
+
+    remote("b", 0).wait_recv()
+
+    def finish(q):
+        remote("s", 2, q).wait_recv()
+        remote("s", 4, q).wait_recv()
+        first = q * quarter
+        sources = [(own_v, first), (core_v.at[0], first), (cross_v.at[0], first), (cross_v.at[1], first)]
+
+        def total_step(i, _):
+            total = None
+            for ref, start in sources:
+                rows = pl.ds(pl.multiple_of(start + i * SUM_CHUNK, SUM_CHUNK), SUM_CHUNK)
+                value = ref[rows].astype(F32)
+                total = value if total is None else total + value
+            rows = pl.ds(pl.multiple_of(i * SUM_CHUNK, SUM_CHUNK), SUM_CHUNK)
+            if q == 0:
+                back_ref[rows] = total
+            else:
+                line_out[q - 1, rows] = total.astype(BF16)
+            return 0
+
+        lax.fori_loop(0, quarter // SUM_CHUNK, total_step, 0)
+        if q:
+            remote("t", q).start()
+
+    for u in (GROUP - 2, GROUP - 1):
+        act_store(u).wait()
+    for store in wide_stores(GROUP - 1):
+        store.wait()
+    act_load(0).start()
+
+    def out_unit(u, _):
+        into = lax.rem(u, 2)
+
+        @pl.when(u < GROUP - 1)
+        def _():
+            act_load(u + 1).start()
+
+        act_load(u).wait()
+        for s in range(2, GROUP):
+            @pl.when(u == s)
+            def _(s=s):
+                out_store(s - 2).wait()
 
         def out_step(n, _):
             columns = pl.ds(pl.multiple_of(n * 512, 512), 512)
-            out_v[:, columns] = dot(act_v[...], down_v[:, columns], NN).astype(BF16)
+            out_v[into, :, columns] = dot(act_v[into], down_v[:, columns], NN).astype(BF16)
             return 0
 
         lax.fori_loop(0, D // 512, out_step, 0)
@@ -535,33 +594,17 @@
             def _(s=s):
                 out_store(s).start()
 
+        for q in range(1, parts):
+            @pl.when(u == GROUP - 1 - 2 * (q - 1))
+            def _(q=q):
+                finish(q)
+
         return 0
 
-    lax.fori_loop(0, GROUP, unit, 0)
-
-    remote("b", 0).wait_recv()
-    for q in range(parts - 1, -1, -1):
-        remote("s", 2, q).wait_recv()
-        remote("s", 4, q).wait_recv()
-        first = q * quarter
-        sources = [(own_v, first), (core_v.at[0], first), (cross_v.at[0], first), (cross_v.at[1], first)]
-
-        def total_step(i, _, q=q, sources=sources):
-            total = None
-            for ref, start in sources:
-                rows = pl.ds(pl.multiple_of(start + i * ROW_CHUNK, ROW_CHUNK), ROW_CHUNK)
-                value = ref[rows].astype(F32)
-                total = value if total is None else total + value
-            rows = pl.ds(pl.multiple_of(i * ROW_CHUNK, ROW_CHUNK), ROW_CHUNK)
-            if q == 0:
-                back_ref[rows] = total
-            else:
-                line_out[q - 1, rows] = total.astype(BF16)
-            return 0
-
-        lax.fori_loop(0, quarter // ROW_CHUNK, total_step, 0)
-        if q:
-            remote("t", q).start()
+    lax.fori_loop(0, GROUP, out_unit, 0)
+    finish(0)
+    for s in (GROUP - 2, GROUP - 1):
+        out_store(s).wait()
     for k in range(parts - 1, 0, -1):
         remote("t", k).wait_recv()
 
@@ -575,9 +618,8 @@
 
     lax.fori_loop(0, quarter // ROW_CHUNK, last_step, 0)
 
-    act_store(GROUP - 1).wait()
-    wide_store(GROUP - 1).wait()
-    out_store(GROUP - 1).wait()
+    for copy in grads_copies:
+        copy.wait()
     waited = [("b", 0), ("b", 6), ("r", 0), ("r", 1), ("b", 2)] + [("s", 2, q) for q in range(parts)]
     for name in copies:
         if name not in waited:
@@ -590,8 +632,9 @@
     seq_len = parts * quarter
     inner = (local_experts * expert_tiles + shared_tiles) * LANES
     wide = 2 * inner + LANES
-    loads = 2 + local_experts * (1 + 2 * expert_tiles) + 2 * shared_tiles
-    copies = 2 * (parts - 1) + 9 * parts + 6 + 14
+    first_part = 2 * expert_tiles * LANES
+    loads = 4 + 3 * local_experts
+    copies = 2 * (parts - 1) + 9 * parts + 6 + 7
     hbm = pl.BlockSpec(memory_space=pl.ANY)
     every = jax.ShapeDtypeStruct((GROUP, seq_len, D), BF16)
     some = jax.ShapeDtypeStruct((GROUP // 2, seq_len, D), BF16)
@@ -602,27 +645,28 @@
             every,
             every,
             jax.ShapeDtypeStruct((GROUP, seq_len, inner), BF16),
-            jax.ShapeDtypeStruct((GROUP, seq_len, wide), BF16),
+            jax.ShapeDtypeStruct((GROUP, seq_len, first_part), BF16),
+            jax.ShapeDtypeStruct((GROUP, seq_len, wide - first_part), BF16),
             some,
             some,
+            jax.ShapeDtypeStruct((GROUP, seq_len, inner), F32),
             jax.ShapeDtypeStruct((quarter, D), F32),
         ),
-        in_specs=[hbm] * (3 + len(weights)),
-        out_specs=(hbm,) * 6 + (pl.BlockSpec(memory_space=pltpu.VMEM),),
+        in_specs=[hbm] * (5 + len(weights)),
+        out_specs=(hbm,) * 8 + (pl.BlockSpec(memory_space=pltpu.VMEM),),
         scratch_shapes=[
             pltpu.VMEM((wide, D), BF16),
-            pltpu.VMEM((D, wide), BF16),
             pltpu.VMEM((inner, D), BF16),
             pltpu.VMEM((seq_len, D), BF16),
             pltpu.VMEM((seq_len, D), BF16),
             pltpu.VMEM((seq_len, LANES), BF16),
-            pltpu.VMEM((seq_len, inner), F32),
-            pltpu.VMEM((seq_len, inner), BF16),
+            pltpu.VMEM((2, seq_len, inner), F32),
+            pltpu.VMEM((2, seq_len, inner), BF16),
             pltpu.VMEM((seq_len, wide), BF16),
             pltpu.VMEM((seq_len, LANES), F32),
             pltpu.VMEM((seq_len, LANES), F32),
             pltpu.VMEM((seq_len, LANES), F32),
-            pltpu.VMEM((seq_len, D), BF16),
+            pltpu.VMEM((2, seq_len, D), BF16),
             pltpu.VMEM((2, seq_len, D), BF16),
             pltpu.VMEM((seq_len, D), BF16),
             pltpu.VMEM((GROUP // 2, seq_len, D), BF16),
@@ -635,13 +679,16 @@
             pltpu.SemaphoreType.DMA((8,)),
             pltpu.SemaphoreType.DMA((loads,)),
             pltpu.SemaphoreType.DMA((parts,)),
+            pltpu.SemaphoreType.DMA((2,)),
+            pltpu.SemaphoreType.DMA((2,)),
+            pltpu.SemaphoreType.DMA((2,)),
         ],
         compiler_params=pltpu.CompilerParams(
             collective_id=1, has_side_effects=True, vmem_limit_bytes=60 * 1024 * 1024
         ),
         cost_estimate=pl.CostEstimate(flops=flops, bytes_accessed=120_000_000, transcendentals=0),
         name="experts",
-    )(rows, grads, mask, *weights)
+    )(rows, *grads, mask, *weights)
 
 
 def line_rows(own_rows):
@@ -665,13 +712,15 @@
     return swap(first, "exp", 2), swap(second, "exp", 4)
 
 
+def chip_sums(mine, near):
+    total = mine[0].astype(F32) + near[0].astype(F32) + near[1].astype(F32)
+    total = total.reshape(lax.axis_size("tp"), -1, total.shape[1])
+    return total[0], total.astype(BF16)
+
+
 def line_sums(mine, near):
-    parts = lax.axis_size("tp")
-    total = mine[0].astype(F32) + near[0].astype(F32) + near[1].astype(F32)
-    total = total.reshape(parts, -1, total.shape[1])
-    low = total.astype(BF16)
-    result = total[0]
-    for k in range(1, parts):
+    result, low = chip_sums(mine, near)
+    for k in range(1, low.shape[0]):
         result = result + swap(low[k], "tp", k).astype(F32)
     return result
 
@@ -707,9 +756,9 @@
 
 
 def gather_kernel(parts, *refs):
-    tokens_ref, proj_ref, out_ref, mask_ref, gate_ref, up_ref, down_ref = refs[:7]
-    tokens_all, proj_all, out_all, mask_all, gate_all, up_all, down_all = refs[7:14]
-    send, recv, local = refs[14:]
+    tokens_ref, proj_ref, narrow_ref, out_ref, mask_ref, gate_ref, up_ref, down_ref = refs[:8]
+    tokens_all, proj_all, narrow_all, out_all, mask_all, gate_all, up_all, down_all = refs[8:16]
+    send, recv, local = refs[16:]
     exp_index, tp_index = lax.axis_index("exp"), lax.axis_index("tp")
     line, near = neighbours(parts)
     quarter, depth, seq_len = tokens_ref.shape[0], proj_ref.shape[0], mask_ref.shape[0]
@@ -722,24 +771,21 @@
     def arrays(r):
         return {
             "p": block(proj_all, depth, r),
+            "n": block(narrow_all, narrow_ref.shape[1], r, 1),
             "o": block(out_all, out_ref.shape[1], r, 1),
             "m": block(mask_all, seq_len, r),
         }
 
-    own = {"p": proj_ref, "o": out_ref, "m": mask_ref}
+    own = {"p": proj_ref, "n": narrow_ref, "o": out_ref, "m": mask_ref}
     my_rows = pl.ds(pl.multiple_of(tp_index * quarter, quarter), quarter)
     copies = {}
-    def rows_from(s):
-        return tokens_all.at[pl.ds(s * quarter, quarter)]
-
-    for s in range(parts):
-        for step in (1, -1):
-            copies["z", s, step] = (rows_from(s), rows_from(s), {"tp": tp_index + step})
+    for k in range(1, parts):
+        copies["z", k] = (tokens_ref, tokens_all.at[my_rows], line[k - 1])
     for key, ref in own.items():
         mine = arrays(0)[key]
         copies["g", 2, key] = (ref, mine, near[1])
         copies["g", 4, key] = (ref, mine, near[3])
-        via = 2 if key == "p" else 4
+        via = 2 if key in "pn" else 4
         passed = arrays(via)[key]
         copies["g", 6, key] = (passed, passed, near[5 - via])
         copies["c", 0, key] = (ref, mine, near[0])
@@ -753,40 +799,16 @@
     remote = remote_maker(copies, send, recv)
 
     greet(line + near)
+    for k in range(1, parts):
+        remote("z", k).start()
     for key in own:
         for r in (2, 4):
             remote("g", r, key).start()
         remote("c", 0, key).start()
-    mine = pltpu.make_async_copy(tokens_ref, tokens_all.at[my_rows], local.at[6])
-    mine.start()
-    mine.wait()
-
-    def at_each_place(body):
-        for z in range(parts):
-            pl.when(tp_index == z)(functools.partial(body, z))
-
-    def first_hop(z):
-        for step in (1, -1):
-            if 0 <= z + step < parts:
-                remote("z", z, step).start()
-
-    def hop(d, z):
-        for step in (1, -1):
-            s = z - step * d
-            if 0 <= s < parts:
-                remote("z", s, step).wait_recv()
-                if 0 <= z + step < parts:
-                    remote("z", s, step).start()
-
-    def sent(z):
-        for step in (1, -1):
-            if 0 <= z + step < parts:
-                for s in range(z + 1) if step == 1 else range(z, parts):
-                    remote("z", s, step).wait_send()
-
-    at_each_place(first_hop)
     kept = [
+        (tokens_ref, tokens_all.at[my_rows]),
         (proj_ref, arrays(0)["p"]),
+        (narrow_ref, arrays(0)["n"]),
         (out_ref, arrays(0)["o"]),
         (mask_ref, arrays(0)["m"]),
         (gate_ref.at[exp_index], block(gate_all, width, 0, 1)),
@@ -796,65 +818,60 @@
     kept = [pltpu.make_async_copy(s, t, local.at[k]) for k, (s, t) in enumerate(kept)]
     for copy in kept:
         copy.start()
-    at_each_place(functools.partial(hop, 1))
     for key in own:
         for r in (2, 4):
             remote("g", r, key).wait_recv()
-            if r == (2 if key == "p" else 4):
+            if r == (2 if key in "pn" else 4):
                 remote("g", 6, key).start()
             remote("c", r, key).start()
     for r in range(1, GROUP):
         for k in range(3):
             remote("a", r, k).start()
-    at_each_place(functools.partial(hop, 2))
     for key in own:
         remote("g", 6, key).wait_recv()
         remote("c", 6, key).start()
-    for d in range(3, parts):
-        at_each_place(functools.partial(hop, d))
     for copy in kept:
         copy.wait()
     for name in copies:
-        if name[0] in "ca":
+        if name[0] != "g":
             remote(*name).wait_recv()
-    at_each_place(sent)
     for name in copies:
-        if name[0] != "z":
-            remote(*name).wait_send()
-
-
-def gather_inputs(tokens, proj, out, mask, gate, up, down):
+        remote(*name).wait_send()
+
+
+def gather_inputs(tokens, proj, narrow, out, mask, gate, up, down):
     parts = lax.axis_size("tp")
     hbm = pl.BlockSpec(memory_space=pl.ANY)
     depth, seq_len = proj.shape[0], mask.shape[0]
     shapes = [
         (parts * tokens.shape[0], D),
         (GROUP * depth, proj.shape[1]),
+        (narrow.shape[0], GROUP * narrow.shape[1]),
         (out.shape[0], GROUP * out.shape[1]),
         (GROUP * seq_len, LANES),
         *((w.shape[1], GROUP * w.shape[2]) for w in (gate, up, down)),
     ]
-    copies = 2 * parts + 3 * 7 + 3 * (GROUP - 1)
+    copies = (parts - 1) + 4 * 7 + 3 * (GROUP - 1)
     return pl.pallas_call(
         functools.partial(gather_kernel, parts),
         out_shape=tuple(jax.ShapeDtypeStruct(s, BF16) for s in shapes),
-        in_specs=[hbm] * 7,
-        out_specs=(hbm,) * 7,
+        in_specs=[hbm] * 8,
+        out_specs=(hbm,) * 8,
         scratch_shapes=[
             pltpu.SemaphoreType.DMA((copies,)),
             pltpu.SemaphoreType.DMA((copies,)),
-            pltpu.SemaphoreType.DMA((7,)),
+            pltpu.SemaphoreType.DMA((8,)),
         ],
         compiler_params=pltpu.CompilerParams(collective_id=2, has_side_effects=True),
         name="gather_inputs",
-    )(tokens, proj, out, mask, gate, up, down)
+    )(tokens, proj, narrow, out, mask, gate, up, down)
 
 
 def scatter_kernel(parts, *refs):
-    proj_ref, out_ref, gate_ref, up_ref, down_ref = refs[:5]
-    proj_sum, out_sum, gate_back, up_back, down_back = refs[5:10]
-    proj_core, out_core, proj_add, out_add, proj_relay, out_relay = refs[10:16]
-    proj_cross, out_cross, narrow, narrow_in, send, recv, local = refs[16:]
+    proj_ref, out_ref, mine_ref, line_ref, gate_ref, up_ref, down_ref = refs[:7]
+    proj_sum, out_sum, output_ref, gate_back, up_back, down_back = refs[7:13]
+    proj_core, out_core, proj_add, out_add, proj_relay, out_relay = refs[13:19]
+    proj_cross, out_cross, narrow, narrow_in, line_in, send, recv, local = refs[19:]
     exp_index = lax.axis_index("exp")
     line, near = neighbours(parts)
     depth, width = proj_sum.shape[0], out_sum.shape[1]
@@ -876,6 +893,7 @@
         copies["s", r, 1] = (out_add.at[side], out_cross.at[side], near[r - 1])
     for k in range(1, parts):
         copies["z", k] = (narrow, narrow_in.at[k - 1], line[k - 1])
+        copies["t", k] = (line_ref.at[k], line_in.at[k - 1], line[k - 1])
     for r in range(1, GROUP):
         to = exp_index ^ r
         copies["a", r, 0] = (gate_ref.at[to], gate_back.at[exp_index], near[r - 1])
@@ -887,14 +905,16 @@
         count = target.shape[0]
 
         def chunk(i, _):
-            rows = pl.ds(pl.multiple_of(i * ROW_CHUNK, ROW_CHUNK), ROW_CHUNK)
+            rows = pl.ds(pl.multiple_of(i * 32, 32), 32)
             value = sum(ref[rows].astype(F32) for ref in sources[1:])
             target[rows] = (sources[0][rows].astype(F32) + value).astype(target.dtype)
             return 0
 
-        lax.fori_loop(0, count // ROW_CHUNK, chunk, 0)
+        lax.fori_loop(0, count // 32, chunk, 0)
 
     greet(line + near)
+    for k in range(1, parts):
+        remote("t", k).start()
     for r in (6, 2, 4, 0):
         for k in range(2):
             remote("c", r, k).start()
@@ -917,6 +937,9 @@
     remote("d", 1).wait_recv()
     total(out_add.at[1], [out_block(4), out_core.at[2], out_relay])
     remote("s", 4, 1).start()
+    for r in range(1, GROUP):
+        for k in range(3):
+            remote("a", r, k).start()
     kept = [
         pltpu.make_async_copy(source.at[exp_index], target.at[exp_index], local.at[k])
         for k, (source, target) in enumerate(
@@ -925,9 +948,6 @@
     ]
     for copy in kept:
         copy.start()
-    for r in range(1, GROUP):
-        for k in range(3):
-            remote("a", r, k).start()
     for k in range(2):
         remote("c", 0, k).wait_recv()
         for r in (2, 4):
@@ -945,6 +965,9 @@
     for j in range(1, parts):
         value = value + narrow_in[j - 1]
     proj_sum[:, proj_sum.shape[1] - LANES :] = value
+    for j in range(1, parts):
+        remote("t", j).wait_recv()
+    total(output_ref, [mine_ref] + [line_in.at[j - 1] for j in range(1, parts)])
     for copy in kept:
         copy.wait()
     for r in range(1, GROUP):
@@ -954,22 +977,23 @@
         remote(*name).wait_send()
 
 
-def scatter_grads(proj, out, gate, up, down):
+def scatter_grads(proj, out, mine, line, gate, up, down):
     parts = lax.axis_size("tp")
     hbm, vmem = pl.BlockSpec(memory_space=pl.ANY), pl.BlockSpec(memory_space=pltpu.VMEM)
     one = (proj.shape[0] // GROUP, proj.shape[1])
     two = (out.shape[0], out.shape[1] // GROUP)
     narrow = (one[0], LANES)
-    copies = 8 + 2 + 4 + (parts - 1) + 3 * (GROUP - 1)
+    copies = 8 + 2 + 4 + 2 * (parts - 1) + 3 * (GROUP - 1)
     return pl.pallas_call(
         functools.partial(scatter_kernel, parts),
         out_shape=(
             jax.ShapeDtypeStruct(one, F32),
             jax.ShapeDtypeStruct(two, F32),
+            jax.ShapeDtypeStruct(mine.shape, BF16),
             *(jax.ShapeDtypeStruct(x.shape, x.dtype) for x in (gate, up, down)),
         ),
-        in_specs=[vmem] * 2 + [hbm] * 3,
-        out_specs=(vmem, vmem, hbm, hbm, hbm),
+        in_specs=[vmem] * 3 + [hbm] * 4,
+        out_specs=(vmem, vmem, vmem, hbm, hbm, hbm),
         scratch_shapes=[
             pltpu.VMEM((GROUP // 2, *one), BF16),
             pltpu.VMEM((GROUP // 2, *two), BF16),
@@ -981,6 +1005,7 @@
             pltpu.VMEM((2, *two), BF16),
             pltpu.VMEM(narrow, F32),
             pltpu.VMEM((parts - 1, *narrow), F32),
+            pltpu.VMEM((parts - 1, *mine.shape), BF16),
             pltpu.SemaphoreType.DMA((copies,)),
             pltpu.SemaphoreType.DMA((copies,)),
             pltpu.SemaphoreType.DMA((3,)),
@@ -989,7 +1014,7 @@
             collective_id=3, has_side_effects=True, vmem_limit_bytes=40 * 1024 * 1024
         ),
         name="scatter_grads",
-    )(proj, out, gate, up, down)
+    )(proj, out, mine, line, gate, up, down)
 
 
 def pad_to(value, axis, multiple):
@@ -1029,10 +1054,10 @@
     shared_hidden = shared_gate.shape[1] // exp_count
     in_group = exp_count == GROUP
     qkv_widths = (attn_q.shape[1], attn_k.shape[1], attn_v.shape[1])
-    gains = jnp.stack([norm1_gain, norm2_gain], axis=1)
-    proj = jnp.concatenate([attn_q, attn_k, attn_v, router, gains], axis=1)
+    gains = jnp.stack([norm1_gain, norm2_gain], axis=0)
+    proj = jnp.concatenate([attn_q, attn_k, attn_v], axis=1)
     qkv_width = sum(qkv_widths)
-    proj = pad_to(proj, 1, LANES)
+    narrow_weight = pad_to(jnp.concatenate([router.T, gains], axis=0), 0, 16)
     member_lanes = jnp.any(
         routes[:, :, None] == jnp.arange(LANES, dtype=jnp.int32), axis=1
     ).astype(BF16)
@@ -1042,12 +1067,22 @@
 
     cut_gate, cut_up, cut_down = cut(shared_gate.T), cut(shared_up.T), cut(shared_down)
     if in_group:
-        whole, proj, output_weight, all_masks, my_gate, my_up, my_down = gather_inputs(
-            tokens, proj, attn_o, member_lanes, cut_gate, cut_up, cut_down
+        (
+            whole,
+            qkv_weight,
+            narrow_weight,
+            output_weight,
+            all_masks,
+            my_gate,
+            my_up,
+            my_down,
+        ) = gather_inputs(
+            tokens, proj, narrow_weight, attn_o, member_lanes, cut_gate, cut_up, cut_down
         )
     else:
         whole = lax.all_gather(tokens, "tp", axis=0, tiled=True)
-        proj = lax.all_gather(proj, "exp", axis=0, tiled=True)
+        qkv_weight = lax.all_gather(proj, "exp", axis=0, tiled=True)
+        narrow_weight = lax.all_gather(narrow_weight, "exp", axis=1, tiled=True)
         output_weight = lax.all_gather(attn_o, "exp", axis=1, tiled=True)
         all_masks = lax.all_gather(member_lanes, "exp", axis=0, tiled=True)
         my_gate, my_up, my_down = (
@@ -1055,12 +1090,10 @@
             for w in (cut_gate, cut_up, cut_down)
         )
         my_gate, my_up, my_down = my_gate[0], my_up[0], my_down[0]
-    qkv_weight = proj[:, :qkv_width]
-    narrow_weight = proj[:, qkv_width:].T
     first_norm_scale = narrow_weight[experts_all].astype(F32)
     second_norm_scale = narrow_weight[experts_all + 1].astype(F32)
     whole, cotangent = lax.optimization_barrier((whole, cotangent))
-    grads_line = line_rows(cotangent)
+    line_grads = line_rows(cotangent)
 
     own_tokens = tokens.astype(F32)
     whole = whole.astype(F32)
@@ -1087,7 +1120,9 @@
     probs_low = probs.astype(BF16)
     attended = jnp.einsum("kgqc,ckd->qkgd", probs_low, values, preferred_element_type=F32)
     attended = attended.reshape(seq_len, heads_dev * HEAD_DIM).astype(BF16)
-    attended, *grads_line[1:-1] = lax.optimization_barrier((attended, *grads_line[1:-1]))
+    attended, *line_grads[1:-1] = lax.optimization_barrier((attended, *line_grads[1:-1]))
+    own_grads = jnp.concatenate(line_grads, axis=0)
+    grads_line = [own_grads, swap(own_grads, "exp", 2), swap(own_grads, "exp", 4)]
     attn_mine = lax.psum_scatter(
         dot(attended, output_weight, NN).astype(BF16), "tp", scatter_dimension=0, tiled=True
     )
@@ -1108,35 +1143,37 @@
         jnp.concatenate([router_rows, router_rows, router_pad], axis=0),
     )
     inner = (local_experts * expert_tiles + shared_tiles) * LANES
-    wide = 2 * inner + LANES
     sizes = (tp_count, experts_all, local_experts, expert_tiles, shared_tiles)
     all_masks = all_masks.reshape(exp_count // GROUP, -1, LANES)
 
     output = residual
-    d_normed_two, wide_sum, down_sum = 0.0, 0.0, 0.0
+    d_normed_two, rest_sum, first_sum, down_sum = 0.0, 0.0, 0.0, 0.0
     for base in range(0, exp_count, GROUP):
         rows_b = normed_two
         if base:
-            rows_b, grads_line = swap(rows_b, "exp", base), line_rows(swap(cotangent, "exp", base))
+            rows_b, own_b = swap(rows_b, "exp", base), swap(own_grads, "exp", base)
+            grads_line = [own_b, swap(own_b, "exp", 2), swap(own_b, "exp", 4)]
         masks = lax.dynamic_index_in_dim(
             all_masks, (exp_index // GROUP) ^ (base // GROUP), keepdims=False
         )
-        all_rows, all_grads, act, wide_grads, out_even, out_odd, back = expert_layer(
-            rows_b, jnp.concatenate(grads_line, axis=0), masks, weights, sizes
+        all_rows, all_grads, act, first_grads, rest_grads, out_even, out_odd, _, back = expert_layer(
+            rows_b, grads_line, masks, weights, sizes
         )
         swapped = swap(out_odd, "exp", 1)
         d_normed_two = d_normed_two + (swap(back, "exp", base) if base else back)
         count = GROUP * seq_len
         grads_seen, act = all_grads.reshape(count, D), act.reshape(count, -1)
-        rows_seen, wide_grads = all_rows.reshape(count, D), wide_grads.reshape(count, wide)
+        rows_seen = all_rows.reshape(count, D)
+        rest_grads, first_grads = rest_grads.reshape(count, -1), first_grads.reshape(count, -1)
         if base + GROUP < exp_count:
-            wide_sum = wide_sum + dot(wide_grads, rows_seen, TN)
+            rest_sum = rest_sum + dot(rest_grads, rows_seen, TN)
+            first_sum = first_sum + dot(first_grads, rows_seen, TN)
             down_sum = down_sum + dot(act, grads_seen, TN)
             mine = add_cores(out_even, swapped)
             part_out = line_sums(mine, near_sums(mine, far_halves(mine)))
             output = output + (swap(part_out, "exp", base) if base else part_out)
-            cotangent, normed_two, wide_sum, down_sum, output = lax.optimization_barrier(
-                (cotangent, normed_two, wide_sum, down_sum, output)
+            own_grads, normed_two, rest_sum, first_sum, down_sum, output = lax.optimization_barrier(
+                (own_grads, normed_two, rest_sum, first_sum, down_sum, output)
             )
     down_sum = down_sum + dot(act, grads_seen, TN)
     swapped, down_sum = lax.optimization_barrier((swapped, down_sum))
@@ -1146,7 +1183,9 @@
 
     d_attn_low = lax.all_gather(d_residual.astype(BF16), "tp", axis=0, tiled=True)
     mine = add_cores(out_even, swapped)
-    d_attn_low, *far = lax.optimization_barrier((d_attn_low, *far_halves(mine)))
+    mine, first_grads = lax.optimization_barrier((mine, first_grads))
+    first_sum = first_sum + dot(first_grads, rows_seen, TN)
+    d_attn_low, first_sum, *far = lax.optimization_barrier((d_attn_low, first_sum, *far_halves(mine)))
     near = near_sums(mine, far)
     grad_out_w = dot(attended, d_attn_low, TN)
     d_attended = dot(d_attn_low, output_weight, NT).astype(BF16)
@@ -1167,35 +1206,37 @@
         axis=1,
     ).reshape(seq_len, -1)
     d_normed_one = dot(d_qkv, qkv_weight, NT).astype(BF16)
-    d_normed_one, wide_grads = lax.optimization_barrier((d_normed_one, wide_grads))
+    d_normed_one, rest_grads, first_sum, down_sum = lax.optimization_barrier(
+        (d_normed_one, rest_grads, first_sum, down_sum)
+    )
     d_normed_one = lax.psum_scatter(
         d_normed_one, "tp", scatter_dimension=0, tiled=True
     ).astype(F32)
     grad_qkv = dot(normed_one, d_qkv, TN)
-    wide_sum = wide_sum + dot(wide_grads, rows_seen, TN)
+    rest_sum = rest_sum + dot(rest_grads, rows_seen, TN)
     d_normed_one, *near = lax.optimization_barrier((d_normed_one, *near))
 
-    def rows_of(first, count, height):
-        tiles = [wide_sum[(first + 2 * k) * LANES : (first + 2 * k + 1) * LANES] for k in range(count)]
-        return jnp.concatenate(tiles, axis=0)[:height]
-
-    def both(side):
-        experts = [
-            rows_of(2 * e * expert_tiles + side, expert_tiles, hidden) for e in range(local_experts)
-        ]
-        return jnp.stack(experts).transpose(0, 2, 1)
-
-    grad_egate, grad_eup = both(0), both(1)
     padded = expert_tiles * LANES
+
+    spans = [first_sum] + [
+        rest_sum[2 * e * padded : 2 * (e + 1) * padded] for e in range(local_experts - 1)
+    ]
+    grad_egate = jnp.stack([s[:hidden] for s in spans]).transpose(0, 2, 1)
+    grad_eup = jnp.stack([s[padded : padded + hidden] for s in spans]).transpose(0, 2, 1)
     grad_edown = jnp.stack(
         [down_sum[e * padded : e * padded + hidden] for e in range(local_experts)]
     )
+    shared_sum = rest_sum[2 * (local_experts - 1) * padded :]
     start = local_experts * padded
-    first_shared = 2 * local_experts * expert_tiles
-    grad_router = wide_sum[wide - LANES : wide - LANES + experts_all]
-    grad_router = grad_router + wide_sum[wide - LANES + experts_all : wide - LANES + 2 * experts_all]
-    output = output + (swap(line_sums(mine, near), "exp", base) if base else line_sums(mine, near))
-    output = output.astype(BF16)
+    shared_rows = my_gate.shape[0]
+    place = shared_tiles * LANES
+    grad_router = shared_sum[place : place + experts_all]
+    grad_router = grad_router + shared_sum[place + experts_all : place + 2 * experts_all]
+    if in_group:
+        own_sum, line_parts = chip_sums(mine, near)
+    else:
+        own_sum = line_sums(mine, near)
+    output = output + (swap(own_sum, "exp", base) if base else own_sum)
     own_scale = lax.rsqrt(jnp.mean(own_tokens * own_tokens, axis=-1, keepdims=True) + epsilon)
     grad_gain_one, d_input = norm_back(d_normed_one, own_tokens, own_scale, first_norm_scale)
     d_input = d_residual + d_input
@@ -1208,16 +1249,17 @@
     )
     grad_proj = jnp.concatenate([grad_qkv, pad_to(narrow, 1, LANES)], axis=1).astype(BF16)
     grad_out_w = grad_out_w.astype(BF16)
-    shared_rows = my_gate.shape[0]
-    back_gate = uncut(rows_of(first_shared, shared_tiles, shared_rows))
-    back_up = uncut(rows_of(first_shared + 1, shared_tiles, shared_rows))
-    back_down = uncut(down_sum[start : start + shared_rows])
+    back_gate, back_up, back_down = (
+        uncut(sums[:shared_rows])
+        for sums in (shared_sum, shared_sum[place + LANES :], down_sum[start:])
+    )
     if in_group:
-        grad_proj, grad_out_w, back_gate, back_up, back_down = scatter_grads(
-            grad_proj, grad_out_w, back_gate, back_up, back_down
+        grad_proj, grad_out_w, output, back_gate, back_up, back_down = scatter_grads(
+            grad_proj, grad_out_w, output, line_parts, back_gate, back_up, back_down
         )
         narrow = grad_proj[:, qkv_width:]
     else:
+        output = output.astype(BF16)
         grad_proj = lax.psum_scatter(grad_proj, "exp", scatter_dimension=0, tiled=True).astype(F32)
         narrow = lax.psum(grad_proj[:, qkv_width:], "tp")
         grad_out_w = lax.psum_scatter(

time: 778 us -> 712 us (0.915)
  Pallas kernels: 462 us -> 389 us
  waiting for transfers between devices: 67.8 us -> 79.2 us
  other arithmetic: 73.9 us -> 63 us
    pallas_call x1, Pallas kernels: 348 us -> 279 us  [expert_layer(): pl.pallas_call(functools.partial(expert_kernel, sizes), out_shape=(every,...]
    slice x6 -> x2, local copies, waits for them, and re-layouts: 13.6 us -> 2.11 us  [shards(): sums[:shared_rows]]
    pallas_call x1, Pallas kernels: 62.7 us -> 52 us  [gather_inputs(): pl.pallas_call(functools.partial(gather_kernel, parts), out_shape=tuple((...]
    ppermute x11 -> x10, waiting for transfers between devices: 36 us -> 45.7 us  [swap(): return lax.ppermute(value, axis, [(i, i ^ bit) for i in range(size)])]
    another operation x1, local copies, waits for them, and re-layouts: 0.71 us -> 9.37 us  [shards(): jnp.stack([down_sum[e * padded:e * padded + hidden] for e in range(local_...]
    dot_general x8 -> x9, matrix products: 83.5 us -> 88.7 us  [dot(): lax.dot_general(left, right, (dims, ((), ())), preferred_element_type=F32)]
    ppermute x11 -> x10, starting transfers between devices: 12.6 us -> 16.8 us  [swap(): return lax.ppermute(value, axis, [(i, i ^ bit) for i in range(size)])]
  transfers between devices with their start and end apart: 14 -> 13, of which waited for: 5 -> 10; matrix products, arithmetic and copies ran while one was open for 21% -> 17% of each run, Pallas kernels for 7% -> 0%
where the time goes in v2:
time: 712 us; the launch traced here: 702 us
  Pallas kernels  389 us (55%)
  matrix products  98.3 us (14%)
  waiting for transfers between devices  79.2 us (11%)
  other arithmetic  63 us (9%)
  local copies, waits for them, and re-layouts  40.3 us (6%)
  starting transfers between devices  17.3 us (2%)
  between operations  15.1 us (2%)
    pallas_call x1, Pallas kernels, expert_layer(): pl.pallas_call(functools.partial(expert_kernel, sizes), out_shape=(every,...  279 us
    dot_general x9, matrix products, dot(): lax.dot_general(left, right, (dims, ((), ())), preferred_element_type=F32)  88.7 us
    pallas_call x1, Pallas kernels, scatter_grads(): pl.pallas_call(functools.partial(scatter_kernel, parts), out_shape=(jax.S...  58.1 us
    pallas_call x1, Pallas kernels, gather_inputs(): pl.pallas_call(functools.partial(gather_kernel, parts), out_shape=tuple((...  52 us
    ppermute x10, waiting for transfers between devices, swap(): return lax.ppermute(value, axis, [(i, i ^ bit) for i in range(size)])  45.7 us
    reduce_scatter x1, waiting for transfers between devices, shards(): lax.psum_scatter(dot(attended, output_weight, NN).astype(BF16), 'tp', sca...  28.7 us
    ppermute x10, starting transfers between devices, swap(): return lax.ppermute(value, axis, [(i, i ^ bit) for i in range(size)])  16.8 us
  transfers between devices with their start and end apart: 13, of which 10 were waited for; matrix products, arithmetic and copies ran while one was open for 17% of the time, Pallas kernels for 0%

profile of v2, /device:TPU:0, one launch (start us, length us, event | category | flops | bytes accessed | tf_op | source)
XLA Modules:
  0.0 702.4 jit_solution(18207182069615960620)
XLA Ops:
  19.0 52.0 %gather_inputs.1 = (bf16[512,2048]{1,0:T(8,128)(2,1)}, bf16[2048,768]{1,0:T(8,128)(2,1)}, bf16[32,2048]{1,0:T(8,128)(2,1)}, bf16[512,2048]{1,0:T(8,128)(2,1)}, b...) custom-call(bf16[128,2048]{1,0:T(8,128)(2,1)} %refs_0_.1, ...), custom_call_target="tpu_custom_call" | custom-call | tf_op jit(solution)/shard_map/gather_inputs/pallas_call | solution.py:855
  79.0 4.4 fusion.46
  93.3 3.4 collective-permute-done.1
  99.6 3.6 collective-permute-start.2
  107.8 17.1 %collective-permute-done.2 = bf16[128,2048]{1,0:T(8,128)(2,1)S(1)} collective-permute-done((bf16[128,2048]{1,0:T(8,128)(2,1)S(1)}, bf16[128,2048]{1,0:T(8,128)(2,1)S(1)}, u32[]{:S(2)}, u32[]{:S(2)}) %collective-permute-start.2) | collective-permute-done | bytes 524320 | tf_op jit(solution)/shard_map/ppermute | solution.py:72
  128.1 28.7 %reduce-scatter.3.cloned.1.call-done = bf16[128,2048]{1,0:T(8,128)(2,1)} async-done(((bf16[512,2048]{1,0:T(8,128)(2,1)}), bf16[128,2048]{1,0:T(8,128)(2,1)}) %reduce-scatter.3.cloned.1.call-update) | async-done | bytes 524304 | tf_op jit(solution)/shard_map/reduce_scatter | solution.py:1126
  160.1 8.7 %collective-permute-done.4.refs_3_ = bf16[512,2048]{1,0:T(8,128)(2,1)} collective-permute-done((bf16[512,2048]{1,0:T(8,128)(2,1)}, bf16[512,2048]{1,0:T(8,128)(2,1)}, u32[]{:S(2)}, u32[]{:S(2)}) %collective-permute-start.4) | collective-permute-done | bytes 2097184 | tf_op jit(solution)/shard_map/ppermute | solution.py:72
  169.7 279.2 %experts.1 = (bf16[8,512,2048]{2,1,0:T(8,128)(2,1)}, bf16[8,512,2048]{2,1,0:T(8,128)(2,1)}, bf16[8,512,896]{2,1,0:T(8,128)(2,1)}, bf16[8,512,768]{2,1,0:T(8,128)...) custom-call(bf16[128,2048]{1,0:T(8,128)(2,1)} %multiply_convert_fusi, ...), custom_call_target="tpu_custom_call" | custom-call | flops 94489280512 | bytes 120000000 | tf_op jit(solution)/shard_map/experts/pallas_call | solution.py:642
  453.9 21.7 %convolution_bitcast_fusion = f32[896,2048]{1,0:T(8,128)} fusion(bf16[8,512,896]{2,1,0:T(8,128)(2,1)} %get-tuple-element.76, bf16[8,512,2048]{2,1,0:T(8,128)(2,1)} %get-tuple-element.77), kind=kOutput, calls=%fused_computation.23 | convolution fusion | flops 15032385536 | bytes 31457280 | tf_op jit(solution)/shard_map/dot_general | solution.py:62
  475.6 7.4 %fusion.15 = (bf16[512,2048]{1,0:T(8,128)(2,1)S(1)}, bf16[512,2048]{1,0:T(8,128)(2,1)S(1)}, bf16[512,2048]{1,0:T(8,128)(2,1)}, bf16[512,2048]{1,0:T(8,128)(2,1)}) fusion(bf16[4,512,2048]{2,1,0:T(8,128)(2,1)} %collective-permute-done.5, bf16[4,512,2048]{2,1,0:T(8,128)(2,1)S(1)} %bitcast.194), kind=kLoop, calls=%fused_computation.41 | loop fusion | flops 16777216 | bytes 25165824 | tf_op jit(solution)/shard_map/convert_element_type | solution.py:700
  484.5 4.8 collective-permute-start.6
  489.3 19.0 %fusion.73 = f32[768,2048]{1,0:T(8,128)} fusion(bf16[4096,768]{1,0:T(8,128)(2,1)S(1)} %bitcast.224, bf16[4096,2048]{1,0:T(8,128)(2,1)} %bitcast.219), kind=kOutput, calls=%fused_computation.142 | convolution fusion | flops 12884901888 | bytes 29360128 | tf_op jit(solution)/shard_map/dot_general | solution.py:62
  509.9 3.5 collective-permute-done.6
  513.4 3.5 convolution_convert_fusion.4
  526.3 5.3 convolution_convert_fusion.2
  531.6 27.1 %fusion.72 = (bf16[1152,2048]{1,0:T(8,128)(2,1)S(1)}, f32[1152,2048]{1,0:T(8,128)}) fusion(bf16[4096,1152]{1,0:T(8,128)(2,1)} %bitcast.221, bf16[4096,2048]{1,0:T(8,128)(2,1)} %bitcast.220), kind=kOutput, calls=%fused_computation.141 | convolution fusion | flops 19329712128 | bytes 40370176 | tf_op jit(solution)/shard_map/dot_general | solution.py:62
  571.8 9.4 %slice_bitcast_fusion.3 = (f32[1,352,2048]{2,1,0:T(8,128)}, f32[1,352,2048]{2,1,0:T(8,128)}, f32[1,352,2048]{2,1,0:T(8,128)}, f32[1,352,2048]{2,1,0:T(8,128)}) fusion(f32[896,2048]{1,0:T(8,128)} %convolution_bitcast_fusion, f32[768,2048]{1,0:T(8,128)} %fusion.73), kind=kLoop, calls=%fused_computation.35 | loop fusion | bytes 23068672 | tf_op jit(solution)/shard_map/stack | solution.py:1226
  582.3 6.1 pad_maximum_fusion
  591.6 3.1 maximum_bitcast_fusion.1
  594.7 3.7 convolution_convert_fusion
  599.4 4.8 reduce-scatter.5.cloned.1.call-done
  605.4 7.7 %collective-permute-done.9 = bf16[512,2048]{1,0:T(8,128)(2,1)} collective-permute-done((bf16[512,2048]{1,0:T(8,128)(2,1)}, bf16[512,2048]{1,0:T(8,128)(2,1)}, u32[]{:S(2)}, u32[]{:S(2)}) %collective-permute-start.9) | collective-permute-done | bytes 2097184 | tf_op jit(solution)/shard_map/ppermute | solution.py:72
  621.1 3.8 fusion.66
  626.9 58.1 %scatter_grads.1 = (f32[256,896]{1,0:T(8,128)S(1)}, f32[512,256]{1,0:T(8,128)S(1)}, bf16[128,2048]{1,0:T(8,128)(2,1)S(1)}, bf16[8,96,256]{2,1,0:T(8,128)(2,1)S(1...) custom-call(bf16[2048,896]{1,0:T(8,128)(2,1)S(1)} %fusion.10.refs_0_, ...), custom_call_target="tpu_custom_call" | custom-call | tf_op jit(solution)/shard_map/scatter_grads/pallas_call | solution.py:987
  (220 shorter events, 101.2 us)
Async XLA Ops:
  7.2 63.8 %copy-start.24 = (bf16[128,2048]{1,0:T(8,128)(2,1)S(1)}, bf16[128,2048]{1,0:T(8,128)(2,1)}, u32[]{:S(2)}) copy-start(bf16[128,2048]{1,0:T(8,128)(2,1)} %param.18) | copy-start | bytes 1572868
  7.2 66.9 %copy-start.44 = (s32[512]{0:T(512)S(1)}, s32[512]{0:T(512)}, u32[]{:S(2)}) copy-start(s32[512]{0:T(512)} %param.19) | copy-start | bytes 6148
  7.2 149.6 %reduce-scatter.3.cloned.1.call-start = ((), (), s32[]{:S(2)}) async-start(), calls=%async_computation.2 | async-start | bytes 2621440 | tf_op jit(solution)/shard_map/reduce_scatter | solution.py:1126
  71.0 25.7 %collective-permute-start.1 = (bf16[128,2048]{1,0:T(8,128)(2,1)S(1)}, bf16[128,2048]{1,0:T(8,128)(2,1)}, u32[]{:S(2)}, u32[]{:S(2)}) collective-permute-start(bf16[128,2048]{1,0:T(8,128)(2,1)S(1)} %copy-done.24), channel_id=1, source_target_pairs={{0,2},{1,3},{2,0},{3,1},{4,6},{5,7},{6,4},{7,5},{8,10},{9,11},{10,... | collective-permute-start | bytes 1572872 | tf_op jit(solution)/shard_map/ppermute | solution.py:72
  73.5 23.2 %collective-permute-start = (bf16[128,2048]{1,0:T(8,128)(2,1)S(1)}, bf16[128,2048]{1,0:T(8,128)(2,1)}, u32[]{:S(2)}, u32[]{:S(2)}) collective-permute-start(bf16[128,2048]{1,0:T(8,128)(2,1)S(1)} %copy-done.24), channel_id=1, source_target_pairs={{0,1},{1,0},{2,3},{3,2},{4,5},{5,4},{6,7},{7,6},{8,9},{9,8},{10,11... | collective-permute-start | bytes 1572872 | tf_op jit(solution)/shard_map/ppermute | solution.py:72
  74.3 16.1 %copy-start.26 = (pred[512,512]{0,1:T(8,128)(4,1)}, pred[512,512]{0,1:T(8,128)(4,1)S(1)}, u32[]{:S(2)}) copy-start(pred[512,512]{0,1:T(8,128)(4,1)S(1)} %fusion.44) | copy-start | bytes 786436
  99.3 27.9 %copy-start.41 = (bf16[32,2048]{1,0:T(8,128)(2,1)S(1)}, bf16[32,2048]{1,0:T(8,128)(2,1)}, u32[]{:S(2)}) copy-start(bf16[32,2048]{1,0:T(8,128)(2,1)} %get-tuple-element.62) | copy-start | bytes 393220
  99.3 57.5 %copy-start.10 = (bf16[128,2048]{1,0:T(8,128)(2,1)S(1)}, bf16[128,2048]{1,0:T(8,128)(2,1)}, u32[]{:S(2)}) copy-start(bf16[128,2048]{1,0:T(8,128)(2,1)} %refs_0_.1) | copy-start | bytes 1572868
  99.3 409.1 %all-gather.2.cloned.1.call-start = ((), (), s32[]{:S(2)}) async-start(), calls=%async_computation.3 | async-start | bytes 2621440 | tf_op jit(solution)/shard_map/all_gather | solution.py:1184
  99.6 25.3 %collective-permute-start.2 = (bf16[128,2048]{1,0:T(8,128)(2,1)S(1)}, bf16[128,2048]{1,0:T(8,128)(2,1)S(1)}, u32[]{:S(2)}, u32[]{:S(2)}) collective-permute-start(bf16[128,2048]{1,0:T(8,128)(2,1)S(1)} %copy-done.24), channel_id=1, source_target_pairs={{0,3},{1,2},{2,1},{3,0},{4,7},{5,6},{6,5},{7,4},{8,11},{9,10},{10,... | collective-permute-start | bytes 1572872 | tf_op jit(solution)/shard_map/ppermute | solution.py:72
  125.7 43.1 %collective-permute-start.4 = (bf16[512,2048]{1,0:T(8,128)(2,1)}, bf16[512,2048]{1,0:T(8,128)(2,1)}, u32[]{:S(2)}, u32[]{:S(2)}) collective-permute-start(bf16[512,2048]{1,0:T(8,128)(2,1)} %constant_dynamic-update-slice_fusion.refs_1_), channel_id=1, source_target_pairs={{0,16},{4,20},{8,24},{12,28},{16,0},{20,4},{24,8},{28,12},{1,17},{... | collective-permute-start | bytes 6291464 | tf_op jit(solution)/shard_map/ppermute | solution.py:72
  125.7 44.0 %collective-permute-start.3 = (bf16[512,2048]{1,0:T(8,128)(2,1)}, bf16[512,2048]{1,0:T(8,128)(2,1)}, u32[]{:S(2)}, u32[]{:S(2)}) collective-permute-start(bf16[512,2048]{1,0:T(8,128)(2,1)} %constant_dynamic-update-slice_fusion.refs_1_), channel_id=1, source_target_pairs={{0,8},{4,12},{8,0},{12,4},{16,24},{20,28},{24,16},{28,20},{1,9},{5... | collective-permute-start | bytes 6291464 | tf_op jit(solution)/shard_map/ppermute | solution.py:72
  169.7 279.7 %copy-start.12 = (bf16[128,2048]{1,0:T(8,128)(2,1)S(1)}, bf16[128,2048]{1,0:T(8,128)(2,1)}, u32[]{:S(2)}) copy-start(bf16[128,2048]{1,0:T(8,128)(2,1)} %reduce-scatter.3.cloned.1.call-done) | copy-start | bytes 1572868
  448.9 26.7 %collective-permute-start.5 = (bf16[4,512,2048]{2,1,0:T(8,128)(2,1)}, bf16[4,512,2048]{2,1,0:T(8,128)(2,1)}, u32[]{:S(2)}, u32[]{:S(2)}) collective-permute-start(bf16[4,512,2048]{2,1,0:T(8,128)(2,1)} %get-tuple-element.75), channel_id=1, source_target_pairs={{0,4},{4,0},{8,12},{12,8},{16,20},{20,16},{24,28},{28,24},{1,5},{5... | collective-permute-start | bytes 25165832 | tf_op jit(solution)/shard_map/ppermute | solution.py:72
  453.6 150.6 %reduce-scatter.5.cloned.1.call-start = ((), (), s32[]{:S(2)}) async-start(), calls=%async_computation.4 | async-start | bytes 2621440 | tf_op jit(solution)/shard_map/reduce_scatter | solution.py:1212
  453.9 21.7 %slice-start = ((s8[8388608]{0:T(1024)(128)(4,1)}), s8[4194304]{0:T(1024)(128)(4,1)S(1)}, s32[]{:S(2)}) async-start(s8[8388608]{0:T(1024)(128)(4,1)} %bitcast.193), calls=%async_computation.5 | async-start | bytes 8388608
  453.9 21.7 %slice-start.1 = ((s8[8388608]{0:T(1024)(128)(4,1)}), s8[4194304]{0:T(1024)(128)(4,1)S(1)}, s32[]{:S(2)}) async-start(s8[8388608]{0:T(1024)(128)(4,1)} %bitcast.193), calls=%async_computation.6 | async-start | bytes 8388608
  475.6 13.7 %slice-start.5 = ((s8[6291456]{0:T(1024)(128)(4,1)}), s8[4194304]{0:T(1024)(128)(4,1)S(1)}, s32[]{:S(2)}) async-start(s8[6291456]{0:T(1024)(128)(4,1)} %bitcast.222), calls=%async_computation.10 | async-start | bytes 8388608
  475.6 13.7 %slice-start.6 = ((s8[6291456]{0:T(1024)(128)(4,1)}), s8[2097152]{0:T(1024)(128)(4,1)S(1)}, s32[]{:S(2)}) async-start(s8[6291456]{0:T(1024)(128)(4,1)} %bitcast.222), calls=%async_computation.11 | async-start | bytes 4194304
  484.5 25.4 %collective-permute-start.7 = (bf16[256,2048]{1,0:T(8,128)(2,1)}, bf16[256,2048]{1,0:T(8,128)(2,1)S(1)}, u32[]{:S(2)}, u32[]{:S(2)}) collective-permute-start(bf16[256,2048]{1,0:T(8,128)(2,1)} %get-tuple-element.192), channel_id=1, source_target_pairs={{0,8},{4,12},{8,0},{12,4},{16,24},{20,28},{24,16},{28,20},{1,9},{5... | collective-permute-start | bytes 3145736 | tf_op jit(solution)/shard_map/ppermute | solution.py:72
  484.5 28.9 %collective-permute-start.6 = (bf16[256,2048]{1,0:T(8,128)(2,1)}, bf16[256,2048]{1,0:T(8,128)(2,1)}, u32[]{:S(2)}, u32[]{:S(2)}) collective-permute-start(bf16[256,2048]{1,0:T(8,128)(2,1)} %get-tuple-element.193), channel_id=1, source_target_pairs={{0,16},{4,20},{8,24},{12,28},{16,0},{20,4},{24,8},{28,12},{1,17},{... | collective-permute-start | bytes 3145736 | tf_op jit(solution)/shard_map/ppermute | solution.py:72
  565.1 48.0 %collective-permute-start.9 = (bf16[512,2048]{1,0:T(8,128)(2,1)}, bf16[512,2048]{1,0:T(8,128)(2,1)}, u32[]{:S(2)}, u32[]{:S(2)}) collective-permute-start(bf16[512,2048]{1,0:T(8,128)(2,1)} %pad_maximum_fusion.2), channel_id=1, source_target_pairs={{0,16},{4,20},{8,24},{12,28},{16,0},{20,4},{24,8},{28,12},{1,17},{... | collective-permute-start | bytes 6291464 | tf_op jit(solution)/shard_map/ppermute | solution.py:72
  568.6 47.4 %collective-permute-start.8 = (bf16[512,2048]{1,0:T(8,128)(2,1)}, bf16[512,2048]{1,0:T(8,128)(2,1)}, u32[]{:S(2)}, u32[]{:S(2)}) collective-permute-start(bf16[512,2048]{1,0:T(8,128)(2,1)} %pad_maximum_fusion.1), channel_id=1, source_target_pairs={{0,8},{4,12},{8,0},{12,4},{16,24},{20,28},{24,16},{28,20},{1,9},{5... | collective-permute-start | bytes 6291464 | tf_op jit(solution)/shard_map/ppermute | solution.py:72
  605.4 10.6 %copy-start.21 = (f32[128,2048]{1,0:T(8,128)}, f32[128,2048]{1,0:T(8,128)S(1)}, u32[]{:S(2)}) copy-start(f32[128,2048]{1,0:T(8,128)S(1)} %convert_element_type.205) | copy-start | bytes 3145732
  (47 other events, 204.0 us)
Sparse Core Ops, SparseCore 0:
  99.4 57.3 reduce-scatter.2
  453.7 48.3 all-gather.1
  559.8 44.3 reduce-scatter.4

commit v3 on v2

--- a/solution.py
+++ b/solution.py
@@ -80,7 +80,7 @@
 
 
 def expert_kernel(sizes, *refs):
-    parts, experts_all, local_experts, expert_tiles, shared_tiles = sizes
+    parts, experts_all, local_experts, expert_tiles, shared_tiles, summed = sizes
     refs = list(refs)
 
     def take(count):
@@ -88,12 +88,12 @@
         del refs[:count]
         return taken
 
-    rows_ref, grads_ref, grads_x, grads_y, mask_hbm, gate_hbm, up_hbm, down_hbm = take(8)
+    attn_hbm, tokens_hbm, gain_ref, grads_ref, mask_hbm, gate_hbm, up_hbm, down_hbm = take(8)
     shared_gate_hbm, shared_up_hbm, shared_down_hbm, router_hbm = take(4)
     all_rows, all_grads, act_hbm, gate_grad_hbm, up_grad_hbm = take(5)
-    out_even, out_odd, d_act_hbm, back_ref = take(4)
+    out_even, out_odd, d_act_hbm, back_ref, rows_ref, residual_ref = take(6)
     wide_v, down_v, rows_v, grads_v, mask_v, d_act_v, act_v, wide_grad_v = take(8)
-    probs_v, gates_v, total_v, out_v, back_v, own_v, core_v, relay_v, cross_v, line_in, line_out = take(11)
+    probs_v, gates_v, total_v, out_v, back_v, own_v, core_v, relay_v, cross_v, line_in, line_out, attn_in, attn_relay = take(13)
     send, recv, local, weight_sem, mask_sem, d_act_sem, act_sem, out_sem = take(8)
     quarter = rows_ref.shape[0]
     seq_len = parts * quarter
@@ -121,7 +121,14 @@
     copies = {}
     for k in range(1, parts):
         copies["z", k] = (rows_ref, all_rows.at[slot[0], part(k)], line(k))
+        there = pl.ds(pl.multiple_of((tp_index ^ k) * quarter, quarter), quarter)
+        if not summed:
+            copies["n", k] = (attn_hbm.at[there], attn_in.at[k - 1], line(k))
         copies["t", k] = (line_out.at[k - 1], line_in.at[k - 1], line(k))
+    copies["zr",] = (all_rows.at[slot[0], part(2)], all_rows.at[slot[0], part(3)], line(1))
+    if not summed:
+        copies["nr",] = (attn_hbm.at[there], attn_relay, line(1))
+        copies["nm",] = (line_out.at[2], attn_in.at[1], line(2))
     for q in range(parts):
         own = rows_ref if q == 0 else all_rows.at[slot[0], part(q)]
         copies["x", q] = (own, all_rows.at[slot[2], part(q)], chip(2))
@@ -141,14 +148,16 @@
             relay_v.at[side],
             chip(4 - 2 * side),
         )
-    kept_grads = {0: grads_ref, 2: grads_x, 4: grads_y}
+    copies["gc", 0, 0] = (grads_ref, all_grads.at[slot[1]], chip(1))
     for h in range(2):
         part_h = pl.ds(h * half_rows, half_rows)
         via = 4 * h + 2 * (1 - h)
-        copies["gd", h] = (kept_grads[via].at[part_h], all_grads.at[slot[6], part_h], chip(6 - via))
-        copies["gc", 6, h] = (all_grads.at[slot[6], part_h], all_grads.at[slot[7], part_h], chip(1))
-    for r, ref in kept_grads.items():
-        copies["gc", r, 0] = (ref, all_grads.at[slot[r + 1]], chip(1))
+        copies["gx", h] = (grads_ref.at[part_h], all_grads.at[slot[2], part_h], chip(2))
+        copies["gy", h] = (grads_ref.at[part_h], all_grads.at[slot[4], part_h], chip(4))
+        copies["gd", h] = (all_grads.at[slot[via], part_h], all_grads.at[slot[6], part_h], chip(6 - via))
+        for r in (2, 4, 6):
+            here = all_grads.at[slot[r], part_h]
+            copies["gc", r, h] = (here, all_grads.at[slot[r + 1], part_h], chip(1))
     number = {name: k for k, name in enumerate(copies)}
 
     def remote(*name):
@@ -168,8 +177,36 @@
         pl.semaphore_signal(barrier, inc=1, device_id=peer, device_id_type=pl.DeviceIdType.MESH)
     pl.semaphore_wait(barrier, len(peers))
 
-    own_copy = pltpu.make_async_copy(rows_ref, all_rows.at[slot[0], part(0)], local.at[0])
-    own_copy.start()
+    middle = inside(tp_index)
+    outside = jnp.logical_not(middle)
+
+    def rows_at(k):
+        return pl.ds(pl.multiple_of((tp_index ^ k) * quarter, quarter), quarter)
+
+    if summed:
+        loads = [pltpu.make_async_copy(attn_hbm, rows_ref, local.at[0])]
+    else:
+        remote("n", 1).start()
+
+        @pl.when(outside)
+        def _():
+            remote("nr").start()
+            remote("n", 2).start()
+
+        pl.when(middle)(remote("n", 3).start)
+        loads = [
+            pltpu.make_async_copy(source, line_out.at[k], local.at[k])
+            for k, source in enumerate(
+                (tokens_hbm, attn_hbm.at[rows_at(0)], attn_hbm.at[rows_at(2)])
+            )
+        ]
+    for load in loads:
+        load.start()
+    remote("gx", 0).start()
+    remote("gy", 1).start()
+    remote("gc", 0, 0).start()
+    remote("gx", 1).start()
+    remote("gy", 0).start()
 
     def spread(q):
         remote("x" if 2 * q < parts else "y", q).start()
@@ -178,9 +215,6 @@
     def spread_rest(q):
         remote("y" if 2 * q < parts else "x", q).start()
 
-    for k in range(1, parts):
-        remote("z", k).start()
-    spread(0)
     hidden = down_hbm.shape[1]
     shared_rows = shared_down_hbm.shape[0]
     weights = [(shared_down_hbm, down_v.at[pl.ds(local_experts * padded, shared_rows)])]
@@ -202,26 +236,34 @@
         pltpu.make_async_copy(source, target, weight_sem.at[k])
         for k, (source, target) in enumerate(weights)
     ]
-    grads_copies = [
-        pltpu.make_async_copy(ref, all_grads.at[slot[r]], local.at[1 + k])
-        for k, (r, ref) in enumerate(kept_grads.items())
-    ]
+    grads_copy = pltpu.make_async_copy(grads_ref, all_grads.at[slot[0]], local.at[3])
 
     def load_rows(u):
         return pltpu.make_async_copy(all_rows.at[u], rows_v, local.at[6])
 
-    for r in kept_grads:
-        remote("gc", r, 0).start()
-    for h in range(2):
-        remote("gd", h).start()
-    for copy in grads_copies:
-        copy.start()
+    grads_copy.start()
     for copy in weight_copies:
         copy.start()
     for ref, first, last in blanks:
         if last > first:
             ref[first:last] = jnp.zeros((last - first, D), BF16)
 
+    def add_into(target, others):
+        def chunk(i, _):
+            total = None
+            for ref, first in [target] + others:
+                rows = pl.ds(pl.multiple_of(first + i * SUM_CHUNK, SUM_CHUNK), SUM_CHUNK)
+                value = ref[rows].astype(F32)
+                total = value if total is None else total + value
+            ref, first = target
+            ref[pl.ds(pl.multiple_of(first + i * SUM_CHUNK, SUM_CHUNK), SUM_CHUNK)] = total.astype(BF16)
+            return 0
+
+        return chunk
+
+    def sum_rows(count, target, others):
+        lax.fori_loop(0, count // SUM_CHUNK, add_into(target, others), 0)
+
     def arrived_x(q):
         remote("x", q).wait_recv()
         if 2 * q < parts:
@@ -254,12 +296,10 @@
             for h in range(2):
                 remote("gd", h).wait_recv()
                 remote("gc", 6, h).start()
-        elif r == 7:
-            for h in range(2):
-                remote("gc", 6, h).wait_recv()
         elif r % 2:
-            remote("gc", r - 1, 0).wait_recv()
-        source = kept_grads.get(r, all_grads.at[slot[r]])
+            for h in range(2 if r > 1 else 1):
+                remote("gc", r - 1, h).wait_recv()
+        source = grads_ref if r == 0 else all_grads.at[slot[r]]
         load = pltpu.make_async_copy(source, grads_v, local.at[5])
         load.start()
         if k >= 2:
@@ -270,15 +310,73 @@
             d_act_v[k % 2, :, columns] = dot(grads_v[...], down_v[columns, :], NT)
         d_act_store(slot[r], k % 2).start()
 
-    arrivals = {2: 1, 5: 2, 7: 3}
-    for k, r in enumerate((0, 1, 2, 3, 4, 5, 6, 7)):
-        first_product(k, r)
-        q = arrivals.get(k, parts)
-        if q < parts:
-            remote("z", q).wait_recv()
-            spread(q)
-            if q >= half_parts:
-                arrived_x(q - half_parts)
+    first_product(0, 0)
+    first_product(1, 1)
+    for load in loads:
+        load.wait()
+    if summed:
+        residual_ref[...] = jnp.zeros_like(residual_ref)
+    else:
+        @pl.when(middle)
+        def _():
+            remote("nr").wait_recv()
+            sum_rows(quarter, (line_out.at[2], 0), [(attn_relay, 0)])
+            remote("nm").start()
+
+        remote("n", 1).wait_recv()
+
+        def normed(arrived):
+            def step(i, _):
+                rows = pl.ds(pl.multiple_of(i * SUM_CHUNK, SUM_CHUNK), SUM_CHUNK)
+                value = line_out[1, rows].astype(F32)
+                for k in arrived:
+                    value = value + attn_in[k, rows].astype(F32)
+                value = value + line_out[0, rows].astype(F32)
+                residual_ref[rows] = value
+                mean = jnp.sum(value * value, axis=1, keepdims=True) * (1.0 / D)
+                rows_ref[rows] = (value * lax.rsqrt(mean + epsilon) * gain_ref[...]).astype(BF16)
+                return 0
+
+            lax.fori_loop(0, quarter // SUM_CHUNK, step, 0)
+
+        @pl.when(outside)
+        def _():
+            remote("nm").wait_recv()
+            normed((0, 1))
+
+        @pl.when(middle)
+        def _():
+            remote("n", 2).wait_recv()
+            remote("n", 3).wait_recv()
+            normed((0, 1, 2))
+
+    remote("z", 2).start()
+    remote("z", 1).start()
+    pl.when(middle)(remote("z", 3).start)
+    own_copy = pltpu.make_async_copy(rows_ref, all_rows.at[slot[0], part(0)], local.at[0])
+    own_copy.start()
+    spread(0)
+    for h, r in ((0, 2), (1, 4), (1, 2), (0, 4)):
+        remote("gx" if r == 2 else "gy", h).wait_recv()
+        if r == 2 + 2 * h:
+            remote("gd", h).start()
+        remote("gc", r, h).start()
+    first_product(2, 2)
+    first_product(3, 3)
+    remote("z", 1).wait_recv()
+    spread(1)
+    first_product(4, 4)
+    first_product(5, 5)
+    remote("z", 2).wait_recv()
+    pl.when(middle)(remote("zr").start)
+    spread(2)
+    arrived_x(0)
+    first_product(6, 6)
+    first_product(7, 7)
+    pl.when(middle)(remote("z", 3).wait_recv)
+    pl.when(outside)(remote("zr").wait_recv)
+    spread(3)
+    arrived_x(1)
     own_copy.wait()
     load_rows(0).start()
     for k in range(2):
@@ -317,22 +415,6 @@
     def out_store(s):
         kept = out_odd if ORDER[s] % 2 else out_even
         return pltpu.make_async_copy(out_v.at[s % 2], kept.at[ORDER[s] // 2], out_sem.at[s % 2])
-
-    def add_into(target, others):
-        def chunk(i, _):
-            total = None
-            for ref, first in [target] + others:
-                rows = pl.ds(pl.multiple_of(first + i * SUM_CHUNK, SUM_CHUNK), SUM_CHUNK)
-                value = ref[rows].astype(F32)
-                total = value if total is None else total + value
-            ref, first = target
-            ref[pl.ds(pl.multiple_of(first + i * SUM_CHUNK, SUM_CHUNK), SUM_CHUNK)] = total.astype(BF16)
-            return 0
-
-        return chunk
-
-    def sum_rows(count, target, others):
-        lax.fori_loop(0, count // SUM_CHUNK, add_into(target, others), 0)
 
     def unit(u, _):
         into = lax.rem(u, 2)
@@ -564,6 +646,9 @@
         if q:
             remote("t", q).start()
 
+    if not summed:
+        pl.when(middle)(remote("nm").wait_send)
+
     for u in (GROUP - 2, GROUP - 1):
         act_store(u).wait()
     for store in wide_stores(GROUP - 1):
@@ -618,23 +703,37 @@
 
     lax.fori_loop(0, quarter // ROW_CHUNK, last_step, 0)
 
-    for copy in grads_copies:
-        copy.wait()
+    grads_copy.wait()
+
+    @pl.when(middle)
+    def _():
+        remote("z", 3).wait_send()
+        remote("zr").wait_send()
+        if not summed:
+            remote("n", 3).wait_send()
+
+    if not summed:
+        @pl.when(outside)
+        def _():
+            remote("n", 2).wait_send()
+            remote("nr").wait_send()
+
     waited = [("b", 0), ("b", 6), ("r", 0), ("r", 1), ("b", 2)] + [("s", 2, q) for q in range(parts)]
+    waited += [("z", 3), ("zr",), ("n", 2), ("n", 3), ("nr",), ("nm",)]
     for name in copies:
         if name not in waited:
             remote(*name).wait_send()
 
 
-def expert_layer(rows, grads, mask, weights, sizes):
-    parts, _, local_experts, expert_tiles, shared_tiles = sizes
-    quarter = rows.shape[0]
+def expert_layer(attn, tokens, gain, grads, mask, weights, sizes):
+    parts, _, local_experts, expert_tiles, shared_tiles, summed = sizes
+    quarter = tokens.shape[0]
     seq_len = parts * quarter
     inner = (local_experts * expert_tiles + shared_tiles) * LANES
     wide = 2 * inner + LANES
     first_part = 2 * expert_tiles * LANES
     loads = 4 + 3 * local_experts
-    copies = 2 * (parts - 1) + 9 * parts + 6 + 7
+    copies = 3 * (parts - 1) + 9 * parts + 6 + 13 + 3
     hbm = pl.BlockSpec(memory_space=pl.ANY)
     every = jax.ShapeDtypeStruct((GROUP, seq_len, D), BF16)
     some = jax.ShapeDtypeStruct((GROUP // 2, seq_len, D), BF16)
@@ -651,9 +750,11 @@
             some,
             jax.ShapeDtypeStruct((GROUP, seq_len, inner), F32),
             jax.ShapeDtypeStruct((quarter, D), F32),
+            jax.ShapeDtypeStruct((quarter, D), BF16),
+            jax.ShapeDtypeStruct((quarter, D), F32),
         ),
-        in_specs=[hbm] * (5 + len(weights)),
-        out_specs=(hbm,) * 8 + (pl.BlockSpec(memory_space=pltpu.VMEM),),
+        in_specs=[hbm] * 2 + [pl.BlockSpec(memory_space=pltpu.VMEM)] + [hbm] * (2 + len(weights)),
+        out_specs=(hbm,) * 8 + (pl.BlockSpec(memory_space=pltpu.VMEM),) * 3,
         scratch_shapes=[
             pltpu.VMEM((wide, D), BF16),
             pltpu.VMEM((inner, D), BF16),
@@ -674,6 +775,8 @@
             pltpu.VMEM((2, seq_len, D), BF16),
             pltpu.VMEM((parts - 1, quarter, D), BF16),
             pltpu.VMEM((parts - 1, quarter, D), BF16),
+            pltpu.VMEM((parts - 1, quarter, D), BF16),
+            pltpu.VMEM((quarter, D), BF16),
             pltpu.SemaphoreType.DMA((copies,)),
             pltpu.SemaphoreType.DMA((copies,)),
             pltpu.SemaphoreType.DMA((8,)),
@@ -684,16 +787,18 @@
             pltpu.SemaphoreType.DMA((2,)),
         ],
         compiler_params=pltpu.CompilerParams(
-            collective_id=1, has_side_effects=True, vmem_limit_bytes=60 * 1024 * 1024
+            collective_id=4 if summed else 1,
+            has_side_effects=True,
+            vmem_limit_bytes=60 * 1024 * 1024,
         ),
         cost_estimate=pl.CostEstimate(flops=flops, bytes_accessed=120_000_000, transcendentals=0),
         name="experts",
-    )(rows, *grads, mask, *weights)
+    )(attn, tokens, gain, grads, mask, *weights)
 
 
 def line_rows(own_rows):
     parts = lax.axis_size("tp")
-    return [own_rows] + [swap(own_rows, "tp", k) for k in range(1, parts)]
+    return jnp.concatenate([own_rows] + [swap(own_rows, "tp", k) for k in range(1, parts)], axis=0)
 
 
 def add_cores(even, odd_swapped):
@@ -755,10 +860,15 @@
     return remote
 
 
+def inside(place):
+    return (place == 1) | (place == 2)
+
+
 def gather_kernel(parts, *refs):
-    tokens_ref, proj_ref, narrow_ref, out_ref, mask_ref, gate_ref, up_ref, down_ref = refs[:8]
-    tokens_all, proj_all, narrow_all, out_all, mask_all, gate_all, up_all, down_all = refs[8:16]
-    send, recv, local = refs[16:]
+    tokens_ref, grads_ref, proj_ref, narrow_ref, out_ref, mask_ref = refs[:6]
+    gate_ref, up_ref, down_ref, tokens_all, grads_all, proj_all = refs[6:12]
+    narrow_all, out_all, mask_all, gate_all, up_all, down_all = refs[12:18]
+    send, recv, local = refs[18:]
     exp_index, tp_index = lax.axis_index("exp"), lax.axis_index("tp")
     line, near = neighbours(parts)
     quarter, depth, seq_len = tokens_ref.shape[0], proj_ref.shape[0], mask_ref.shape[0]
@@ -780,7 +890,15 @@
     my_rows = pl.ds(pl.multiple_of(tp_index * quarter, quarter), quarter)
     copies = {}
     for k in range(1, parts):
-        copies["z", k] = (tokens_ref, tokens_all.at[my_rows], line[k - 1])
+        copies["z", 0, k] = (tokens_ref, tokens_all.at[my_rows], line[k - 1])
+        copies["z", 1, k] = (grads_ref, grads_all.at[pl.ds(k * quarter, quarter)], line[k - 1])
+    passed = pl.ds(pl.multiple_of((tp_index ^ 2) * quarter, quarter), quarter)
+    copies["zr", 0] = (tokens_all.at[passed], tokens_all.at[passed], line[0])
+    copies["zr", 1] = (
+        grads_all.at[pl.ds(2 * quarter, quarter)],
+        grads_all.at[pl.ds(3 * quarter, quarter)],
+        line[0],
+    )
     for key, ref in own.items():
         mine = arrays(0)[key]
         copies["g", 2, key] = (ref, mine, near[1])
@@ -799,14 +917,17 @@
     remote = remote_maker(copies, send, recv)
 
     greet(line + near)
-    for k in range(1, parts):
-        remote("z", k).start()
+    for kind in range(2):
+        remote("z", kind, 2).start()
+        remote("z", kind, 1).start()
+        pl.when(inside(tp_index))(remote("z", kind, 3).start)
     for key in own:
         for r in (2, 4):
             remote("g", r, key).start()
         remote("c", 0, key).start()
     kept = [
         (tokens_ref, tokens_all.at[my_rows]),
+        (grads_ref, grads_all.at[pl.ds(0, quarter)]),
         (proj_ref, arrays(0)["p"]),
         (narrow_ref, arrays(0)["n"]),
         (out_ref, arrays(0)["o"]),
@@ -827,23 +948,40 @@
     for r in range(1, GROUP):
         for k in range(3):
             remote("a", r, k).start()
+    for kind in range(2):
+        remote("z", kind, 2).wait_recv()
+        pl.when(inside(tp_index))(remote("zr", kind).start)
     for key in own:
         remote("g", 6, key).wait_recv()
         remote("c", 6, key).start()
     for copy in kept:
         copy.wait()
     for name in copies:
-        if name[0] != "g":
+        if name[0] in "ca":
             remote(*name).wait_recv()
+    for kind in range(2):
+        remote("z", kind, 1).wait_recv()
+
+        @pl.when(inside(tp_index))
+        def _(kind=kind):
+            remote("z", kind, 3).wait_recv()
+            remote("z", kind, 3).wait_send()
+            remote("zr", kind).wait_send()
+
+        pl.when(jnp.logical_not(inside(tp_index)))(remote("zr", kind).wait_recv)
+        for k in (1, 2):
+            remote("z", kind, k).wait_send()
     for name in copies:
-        remote(*name).wait_send()
-
-
-def gather_inputs(tokens, proj, narrow, out, mask, gate, up, down):
+        if name[0] not in ("z", "zr"):
+            remote(*name).wait_send()
+
+
+def gather_inputs(tokens, grads, proj, narrow, out, mask, gate, up, down):
     parts = lax.axis_size("tp")
     hbm = pl.BlockSpec(memory_space=pl.ANY)
     depth, seq_len = proj.shape[0], mask.shape[0]
     shapes = [
+        (parts * tokens.shape[0], D),
         (parts * tokens.shape[0], D),
         (GROUP * depth, proj.shape[1]),
         (narrow.shape[0], GROUP * narrow.shape[1]),
@@ -851,20 +989,20 @@
         (GROUP * seq_len, LANES),
         *((w.shape[1], GROUP * w.shape[2]) for w in (gate, up, down)),
     ]
-    copies = (parts - 1) + 4 * 7 + 3 * (GROUP - 1)
+    copies = 2 * parts + 4 * 7 + 3 * (GROUP - 1)
     return pl.pallas_call(
         functools.partial(gather_kernel, parts),
         out_shape=tuple(jax.ShapeDtypeStruct(s, BF16) for s in shapes),
-        in_specs=[hbm] * 8,
-        out_specs=(hbm,) * 8,
+        in_specs=[hbm] * 9,
+        out_specs=(hbm,) * 9,
         scratch_shapes=[
             pltpu.SemaphoreType.DMA((copies,)),
             pltpu.SemaphoreType.DMA((copies,)),
-            pltpu.SemaphoreType.DMA((8,)),
+            pltpu.SemaphoreType.DMA((9,)),
         ],
         compiler_params=pltpu.CompilerParams(collective_id=2, has_side_effects=True),
         name="gather_inputs",
-    )(tokens, proj, narrow, out, mask, gate, up, down)
+    )(tokens, grads, proj, narrow, out, mask, gate, up, down)
 
 
 def scatter_kernel(parts, *refs):
@@ -1069,6 +1207,7 @@
     if in_group:
         (
             whole,
+            own_grads,
             qkv_weight,
             narrow_weight,
             output_weight,
@@ -1077,10 +1216,11 @@
             my_up,
             my_down,
         ) = gather_inputs(
-            tokens, proj, narrow_weight, attn_o, member_lanes, cut_gate, cut_up, cut_down
+            tokens, cotangent, proj, narrow_weight, attn_o, member_lanes, cut_gate, cut_up, cut_down
         )
     else:
         whole = lax.all_gather(tokens, "tp", axis=0, tiled=True)
+        own_grads = line_rows(cotangent)
         qkv_weight = lax.all_gather(proj, "exp", axis=0, tiled=True)
         narrow_weight = lax.all_gather(narrow_weight, "exp", axis=1, tiled=True)
         output_weight = lax.all_gather(attn_o, "exp", axis=1, tiled=True)
@@ -1092,9 +1232,6 @@
         my_gate, my_up, my_down = my_gate[0], my_up[0], my_down[0]
     first_norm_scale = narrow_weight[experts_all].astype(F32)
     second_norm_scale = narrow_weight[experts_all + 1].astype(F32)
-    whole, cotangent = lax.optimization_barrier((whole, cotangent))
-    line_grads = line_rows(cotangent)
-
     own_tokens = tokens.astype(F32)
     whole = whole.astype(F32)
     scale_one = lax.rsqrt(jnp.mean(whole * whole, axis=-1, keepdims=True) + epsilon)
@@ -1120,16 +1257,8 @@
     probs_low = probs.astype(BF16)
     attended = jnp.einsum("kgqc,ckd->qkgd", probs_low, values, preferred_element_type=F32)
     attended = attended.reshape(seq_len, heads_dev * HEAD_DIM).astype(BF16)
-    attended, *line_grads[1:-1] = lax.optimization_barrier((attended, *line_grads[1:-1]))
-    own_grads = jnp.concatenate(line_grads, axis=0)
-    grads_line = [own_grads, swap(own_grads, "exp", 2), swap(own_grads, "exp", 4)]
-    attn_mine = lax.psum_scatter(
-        dot(attended, output_weight, NN).astype(BF16), "tp", scatter_dimension=0, tiled=True
-    )
-
-    residual = own_tokens + attn_mine.astype(F32)
-    scale_two = lax.rsqrt(jnp.mean(residual * residual, axis=-1, keepdims=True) + epsilon)
-    normed_two = (residual * scale_two * second_norm_scale).astype(BF16)
+    attn_part = dot(attended, output_weight, NN).astype(BF16)
+
     expert_tiles, shared_tiles = -(-hidden // LANES), -(-my_gate.shape[0] // LANES)
     router_rows = narrow_weight[:experts_all]
     router_pad = jnp.zeros((LANES - 2 * experts_all, D), BF16)
@@ -1144,21 +1273,24 @@
     )
     inner = (local_experts * expert_tiles + shared_tiles) * LANES
     sizes = (tp_count, experts_all, local_experts, expert_tiles, shared_tiles)
+    gain_row = second_norm_scale[None, :]
     all_masks = all_masks.reshape(exp_count // GROUP, -1, LANES)
 
-    output = residual
     d_normed_two, rest_sum, first_sum, down_sum = 0.0, 0.0, 0.0, 0.0
     for base in range(0, exp_count, GROUP):
-        rows_b = normed_two
+        rows_b, own_b = attn_part, own_grads
         if base:
-            rows_b, own_b = swap(rows_b, "exp", base), swap(own_grads, "exp", base)
-            grads_line = [own_b, swap(own_b, "exp", 2), swap(own_b, "exp", 4)]
+            rows_b, own_b = swap(normed_two, "exp", base), swap(own_grads, "exp", base)
         masks = lax.dynamic_index_in_dim(
             all_masks, (exp_index // GROUP) ^ (base // GROUP), keepdims=False
         )
-        all_rows, all_grads, act, first_grads, rest_grads, out_even, out_odd, _, back = expert_layer(
-            rows_b, grads_line, masks, weights, sizes
+        *results, back, rows_b, residual_b = expert_layer(
+            rows_b, tokens, gain_row, own_b, masks, weights, (*sizes, base > 0)
         )
+        all_rows, all_grads, act, first_grads, rest_grads, out_even, out_odd, _ = results
+        if not base:
+            normed_two, residual = rows_b, residual_b
+            output = residual
         swapped = swap(out_odd, "exp", 1)
         d_normed_two = d_normed_two + (swap(back, "exp", base) if base else back)
         count = GROUP * seq_len
@@ -1178,6 +1310,7 @@
     down_sum = down_sum + dot(act, grads_seen, TN)
     swapped, down_sum = lax.optimization_barrier((swapped, down_sum))
 
+    scale_two = lax.rsqrt(jnp.mean(residual * residual, axis=-1, keepdims=True) + epsilon)
     grad_gain_two, d_residual = norm_back(d_normed_two, residual, scale_two, second_norm_scale)
     d_residual = cotangent.astype(F32) + d_residual
 

time: 712 us -> 674 us (0.947)
  waiting for transfers between devices: 79.2 us -> 17.9 us
  Pallas kernels: 389 us -> 436 us
  starting transfers between devices: 17.3 us -> 2.59 us
    ppermute x10 -> x5, waiting for transfers between devices: 45.7 us -> 12.1 us  [swap(): return lax.ppermute(value, axis, [(i, i ^ bit) for i in range(size)])]
    reduce_scatter x1 -> x0, waiting for transfers between devices: 28.7 us -> none  [shards(): lax.psum_scatter(dot(attended, output_weight, NN).astype(BF16), 'tp', sca...]
    pallas_call x1, Pallas kernels: 279 us -> 303 us  [expert_layer(): pl.pallas_call(functools.partial(expert_kernel, sizes), out_shape=(every,...]
    pallas_call x1, Pallas kernels: 52 us -> 75.4 us  [gather_inputs(): pl.pallas_call(functools.partial(gather_kernel, parts), out_shape=tuple((...]
    ppermute x10 -> x5, starting transfers between devices: 16.8 us -> 2.51 us  [swap(): return lax.ppermute(value, axis, [(i, i ^ bit) for i in range(size)])]
  transfers between devices with their start and end apart: 13 -> 7, of which waited for: 10 -> 5; matrix products, arithmetic and copies ran while one was open for 17% -> 14% of each run, Pallas kernels for 0% -> 0%
where the time goes in v3:
time: 674 us; the launch traced here: 668 us
  Pallas kernels  436 us (65%)
  matrix products  99.9 us (15%)
  other arithmetic  60.1 us (9%)
  local copies, waits for them, and re-layouts  36.4 us (5%)
  waiting for transfers between devices  17.9 us (3%)
  between operations  15.4 us (2%)
    pallas_call x1, Pallas kernels, expert_layer(): pl.pallas_call(functools.partial(expert_kernel, sizes), out_shape=(every,...  303 us
    dot_general x9, matrix products, dot(): lax.dot_general(left, right, (dims, ((), ())), preferred_element_type=F32)  90.4 us
    pallas_call x1, Pallas kernels, gather_inputs(): pl.pallas_call(functools.partial(gather_kernel, parts), out_shape=tuple((...  75.4 us
    pallas_call x1, Pallas kernels, scatter_grads(): pl.pallas_call(functools.partial(scatter_kernel, parts), out_shape=(jax.S...  57.7 us
  transfers between devices with their start and end apart: 7, of which 5 were waited for; matrix products, arithmetic and copies ran while one was open for 14% of the time, Pallas kernels for 0%

profile of v3, /device:TPU:0, one launch (start us, length us, event | category | flops | bytes accessed | tf_op | source)
XLA Modules:
  0.0 668.4 jit_solution(6271181196098693110)
XLA Ops:
  18.9 75.4 %gather_inputs.1 = (bf16[512,2048]{1,0:T(8,128)(2,1)}, bf16[512,2048]{1,0:T(8,128)(2,1)}, bf16[2048,768]{1,0:T(8,128)(2,1)}, bf16[32,2048]{1,0:T(8,128)(2,1)}, b...) custom-call(bf16[128,2048]{1,0:T(8,128)(2,1)} %refs_1_.3, ...), custom_call_target="tpu_custom_call" | custom-call | tf_op jit(solution)/shard_map/gather_inputs/pallas_call | solution.py:993
  98.7 4.4 fusion.46
  110.7 2.8 fusion.23
  113.5 2.6 convolution_convert_fusion.3.refs_0_
  117.1 302.9 %experts.1 = (bf16[8,512,2048]{2,1,0:T(8,128)(2,1)}, bf16[8,512,2048]{2,1,0:T(8,128)(2,1)}, bf16[8,512,896]{2,1,0:T(8,128)(2,1)}, bf16[8,512,768]{2,1,0:T(8,128)...) custom-call(bf16[512,2048]{1,0:T(8,128)(2,1)} %convolution_convert_f, ...), custom_call_target="tpu_custom_call" | custom-call | flops 94489280512 | bytes 120000000 | tf_op jit(solution)/shard_map/experts/pallas_call | solution.py:741
  424.0 2.7 fusion.65
  427.5 22.1 %convolution_bitcast_fusion = f32[896,2048]{1,0:T(8,128)} fusion(bf16[8,512,896]{2,1,0:T(8,128)(2,1)} %get-tuple-element.70, bf16[8,512,2048]{2,1,0:T(8,128)(2,1)} %get-tuple-element.71), kind=kOutput, calls=%fused_computation.23 | convolution fusion | flops 15032385536 | bytes 31457280 | tf_op jit(solution)/shard_map/dot_general | solution.py:62
  449.7 7.4 %fusion.15 = (bf16[512,2048]{1,0:T(8,128)(2,1)S(1)}, bf16[512,2048]{1,0:T(8,128)(2,1)S(1)}, bf16[512,2048]{1,0:T(8,128)(2,1)}, bf16[512,2048]{1,0:T(8,128)(2,1)}) fusion(bf16[4,512,2048]{2,1,0:T(8,128)(2,1)} %collective-permute-done, bf16[4,512,2048]{2,1,0:T(8,128)(2,1)S(1)} %bitcast.194), kind=kLoop, calls=%fused_computation.41 | loop fusion | flops 16777216 | bytes 25165824 | tf_op jit(solution)/shard_map/convert_element_type | solution.py:805
  459.2 19.1 %fusion.73 = f32[768,2048]{1,0:T(8,128)} fusion(bf16[4096,768]{1,0:T(8,128)(2,1)S(1)} %bitcast.221, bf16[4096,2048]{1,0:T(8,128)(2,1)} %bitcast.216), kind=kOutput, calls=%fused_computation.136 | convolution fusion | flops 12884901888 | bytes 29360128 | tf_op jit(solution)/shard_map/dot_general | solution.py:62
  478.5 5.8 collective-permute-done.1
  484.8 3.5 convolution_convert_fusion.4
  488.3 2.6 fusion.4
  497.6 5.3 convolution_convert_fusion.2
  502.9 27.2 %fusion.72 = (bf16[1152,2048]{1,0:T(8,128)(2,1)S(1)}, f32[1152,2048]{1,0:T(8,128)}) fusion(bf16[4096,1152]{1,0:T(8,128)(2,1)} %bitcast.218, bf16[4096,2048]{1,0:T(8,128)(2,1)} %bitcast.217), kind=kOutput, calls=%fused_computation.135 | convolution fusion | flops 19329712128 | bytes 40370176 | tf_op jit(solution)/shard_map/dot_general | solution.py:62
  542.4 3.3 slice_bitcast_fusion
  545.7 9.4 %slice_bitcast_fusion.3 = (f32[1,352,2048]{2,1,0:T(8,128)}, f32[1,352,2048]{2,1,0:T(8,128)}, f32[1,352,2048]{2,1,0:T(8,128)}, f32[1,352,2048]{2,1,0:T(8,128)}) fusion(f32[896,2048]{1,0:T(8,128)} %convolution_bitcast_fusion, f32[768,2048]{1,0:T(8,128)} %fusion.73), kind=kLoop, calls=%fused_computation.35 | loop fusion | bytes 23068672 | tf_op jit(solution)/shard_map/stack | solution.py:1359
  556.2 6.1 pad_maximum_fusion
  562.3 3.1 maximum_bitcast_fusion.1
  565.5 3.1 maximum_bitcast_fusion
  568.6 3.7 convolution_convert_fusion
  573.3 5.8 reduce-scatter.2.cloned.1.call-done
  580.3 3.5 collective-permute-done.4
  588.5 4.5 fusion.66
  595.7 57.7 %scatter_grads.1 = (f32[256,896]{1,0:T(8,128)S(1)}, f32[512,256]{1,0:T(8,128)S(1)}, bf16[128,2048]{1,0:T(8,128)(2,1)S(1)}, bf16[8,96,256]{2,1,0:T(8,128)(2,1)S(1...) custom-call(bf16[2048,896]{1,0:T(8,128)(2,1)S(1)} %fusion.10.refs_0_, ...), custom_call_target="tpu_custom_call" | custom-call | tf_op jit(solution)/shard_map/scatter_grads/pallas_call | solution.py:1125
  (204 shorter events, 68.7 us)
Async XLA Ops:
  7.2 471.3 %all-gather.2.cloned.1.call-start = ((), (), s32[]{:S(2)}) async-start(), calls=%async_computation.1 | async-start | bytes 2621440 | tf_op jit(solution)/shard_map/all_gather | solution.py:1317
  95.8 7.4 %copy-start.40 = (f32[1,2048]{1,0:T(1,128)}, f32[1,2048]{1,0:T(1,128)S(1)}, u32[]{:S(2)}) copy-start(f32[1,2048]{1,0:T(1,128)S(1)} %get-tuple-element.196) | copy-start | bytes 24580
  117.1 304.5 %copy-start.37 = (f32[1,2048]{1,0:T(1,128)S(1)}, f32[1,2048]{1,0:T(1,128)}, u32[]{:S(2)}) copy-start(f32[1,2048]{1,0:T(1,128)} %get-tuple-element.195.refs_2_) | copy-start | bytes 24580
  117.1 306.9 %copy-start.19 = (bf16[128,2048]{1,0:T(8,128)(2,1)S(1)}, bf16[128,2048]{1,0:T(8,128)(2,1)}, u32[]{:S(2)}) copy-start(bf16[128,2048]{1,0:T(8,128)(2,1)} %refs_1_.2) | copy-start | bytes 1572868
  420.1 6.8 %copy-start.17 = (bf16[128,2048]{1,0:T(8,128)(2,1)S(1)}, bf16[128,2048]{1,0:T(8,128)(2,1)}, u32[]{:S(2)}) copy-start(bf16[128,2048]{1,0:T(8,128)(2,1)} %refs_1_.3) | copy-start | bytes 1572868
  420.1 29.6 %collective-permute-start = (bf16[4,512,2048]{2,1,0:T(8,128)(2,1)}, bf16[4,512,2048]{2,1,0:T(8,128)(2,1)}, u32[]{:S(2)}, u32[]{:S(2)}) collective-permute-start(bf16[4,512,2048]{2,1,0:T(8,128)(2,1)} %get-tuple-element.69), channel_id=1, source_target_pairs={{0,4},{4,0},{8,12},{12,8},{16,20},{20,16},{24,28},{28,24},{1,5},{5... | collective-permute-start | bytes 25165832 | tf_op jit(solution)/shard_map/ppermute | solution.py:72
  426.7 152.4 %reduce-scatter.2.cloned.1.call-start = ((), (), s32[]{:S(2)}) async-start(), calls=%async_computation.2 | async-start | bytes 2621440 | tf_op jit(solution)/shard_map/reduce_scatter | solution.py:1345
  427.5 22.1 %slice-start = ((s8[8388608]{0:T(1024)(128)(4,1)}), s8[4194304]{0:T(1024)(128)(4,1)S(1)}, s32[]{:S(2)}) async-start(s8[8388608]{0:T(1024)(128)(4,1)} %bitcast.193), calls=%async_computation.3 | async-start | bytes 8388608
  427.5 22.1 %slice-start.1 = ((s8[8388608]{0:T(1024)(128)(4,1)}), s8[4194304]{0:T(1024)(128)(4,1)S(1)}, s32[]{:S(2)}) async-start(s8[8388608]{0:T(1024)(128)(4,1)} %bitcast.193), calls=%async_computation.4 | async-start | bytes 8388608
  449.6 9.6 %slice-start.2 = ((s8[6291456]{0:T(1024)(128)(4,1)}), s8[4194304]{0:T(1024)(128)(4,1)S(1)}, s32[]{:S(2)}) async-start(s8[6291456]{0:T(1024)(128)(4,1)} %bitcast.219), calls=%async_computation.5 | async-start | bytes 8388608
  449.7 9.6 %slice-start.3 = ((s8[6291456]{0:T(1024)(128)(4,1)}), s8[2097152]{0:T(1024)(128)(4,1)S(1)}, s32[]{:S(2)}) async-start(s8[6291456]{0:T(1024)(128)(4,1)} %bitcast.219), calls=%async_computation.6 | async-start | bytes 4194304
  458.6 25.7 %collective-permute-start.1 = (bf16[256,2048]{1,0:T(8,128)(2,1)}, bf16[256,2048]{1,0:T(8,128)(2,1)S(1)}, u32[]{:S(2)}, u32[]{:S(2)}) collective-permute-start(bf16[256,2048]{1,0:T(8,128)(2,1)} %get-tuple-element.186), channel_id=1, source_target_pairs={{0,16},{4,20},{8,24},{12,28},{16,0},{20,4},{24,8},{28,12},{1,17},{... | collective-permute-start | bytes 3145736 | tf_op jit(solution)/shard_map/ppermute | solution.py:72
  459.2 25.5 %collective-permute-start.2 = (bf16[256,2048]{1,0:T(8,128)(2,1)}, bf16[256,2048]{1,0:T(8,128)(2,1)}, u32[]{:S(2)}, u32[]{:S(2)}) collective-permute-start(bf16[256,2048]{1,0:T(8,128)(2,1)} %get-tuple-element.185), channel_id=1, source_target_pairs={{0,8},{4,12},{8,0},{12,4},{16,24},{20,28},{24,16},{28,20},{1,9},{5... | collective-permute-start | bytes 3145736 | tf_op jit(solution)/shard_map/ppermute | solution.py:72
  478.4 9.9 %copy-start.22 = (pred[512,512]{0,1:T(8,128)(4,1)S(1)}, pred[512,512]{0,1:T(8,128)(4,1)}, u32[]{:S(2)}) copy-start(pred[512,512]{0,1:T(8,128)(4,1)} %copy-done.21) | copy-start | bytes 786436
  478.4 9.9 %copy-start.39 = (f32[4,512]{1,0:T(4,128)S(1)}, f32[4,512]{1,0:T(4,128)}, u32[]{:S(2)}) copy-start(f32[4,512]{1,0:T(4,128)} %copy-done.38) | copy-start | bytes 24580
  478.4 9.9 %copy-start.43 = (f32[4,512]{1,0:T(4,128)S(1)}, f32[4,512]{1,0:T(4,128)}, u32[]{:S(2)}) copy-start(f32[4,512]{1,0:T(4,128)} %copy-done.42) | copy-start | bytes 24580
  478.4 9.9 %copy-start.5 = (f32[512,512,4]{1,0,2:T(8,128)S(1)}, f32[512,512,4]{1,0,2:T(8,128)}, u32[]{:S(2)}) copy-start(f32[512,512,4]{1,0,2:T(8,128)} %copy-done.4) | copy-start | bytes 12582916
  484.3 6.6 copy-start.33
  502.9 29.3 %copy-start.16 = (bf16[512,2048]{1,0:T(8,128)(2,1)S(1)}, bf16[512,2048]{1,0:T(8,128)(2,1)}, u32[]{:S(2)}) copy-start(bf16[512,2048]{1,0:T(8,128)(2,1)} %get-tuple-element.83) | copy-start | bytes 6291460
  502.9 29.3 %copy-start.34 = (bf16[256,2048]{1,0:T(8,128)(2,1)S(1)}, bf16[256,2048]{1,0:T(8,128)(2,1)}, u32[]{:S(2)}) copy-start(bf16[256,2048]{1,0:T(8,128)(2,1)} %copy-done.33) | copy-start | bytes 3145732
  536.3 47.5 %collective-permute-start.4 = (bf16[512,2048]{1,0:T(8,128)(2,1)}, bf16[512,2048]{1,0:T(8,128)(2,1)}, u32[]{:S(2)}, u32[]{:S(2)}) collective-permute-start(bf16[512,2048]{1,0:T(8,128)(2,1)} %pad_maximum_fusion.2), channel_id=1, source_target_pairs={{0,16},{4,20},{8,24},{12,28},{16,0},{20,4},{24,8},{28,12},{1,17},{... | collective-permute-start | bytes 6291464 | tf_op jit(solution)/shard_map/ppermute | solution.py:72
  539.1 46.9 %collective-permute-start.3 = (bf16[512,2048]{1,0:T(8,128)(2,1)}, bf16[512,2048]{1,0:T(8,128)(2,1)}, u32[]{:S(2)}, u32[]{:S(2)}) collective-permute-start(bf16[512,2048]{1,0:T(8,128)(2,1)} %pad_maximum_fusion.1), channel_id=1, source_target_pairs={{0,8},{4,12},{8,0},{12,4},{16,24},{20,28},{24,16},{28,20},{1,9},{5... | collective-permute-start | bytes 6291464 | tf_op jit(solution)/shard_map/ppermute | solution.py:72
  545.7 10.5 %copy-start.29 = (bf16[96,2048]{1,0:T(8,128)(2,1)S(1)}, bf16[96,2048]{1,0:T(8,128)(2,1)}, u32[]{:S(2)}) copy-start(bf16[96,2048]{1,0:T(8,128)(2,1)} %get-tuple-element.178) | copy-start | bytes 1179652
  568.6 17.5 %copy-start.49 = (f32[128]{0:T(128)S(1)}, f32[128]{0:T(128)}, u32[]{:S(2)}) copy-start(f32[128]{0:T(128)} %add_rsqrt_fusion.1) | copy-start | bytes 1540
  (42 other events, 130.1 us)
Sparse Core Ops, SparseCore 0:
  426.9 43.8 all-gather.1
  537.8 41.2 reduce-scatter.1

commit v4 on v3

--- a/solution.py
+++ b/solution.py
@@ -88,7 +88,8 @@
         del refs[:count]
         return taken
 
-    attn_hbm, tokens_hbm, gain_ref, grads_ref, mask_hbm, gate_hbm, up_hbm, down_hbm = take(8)
+    attn_hbm, tokens_hbm, gain_ref, grads_ref, grads_x, grads_y = take(6)
+    mask_hbm, gate_hbm, up_hbm, down_hbm = take(4)
     shared_gate_hbm, shared_up_hbm, shared_down_hbm, router_hbm = take(4)
     all_rows, all_grads, act_hbm, gate_grad_hbm, up_grad_hbm = take(5)
     out_even, out_odd, d_act_hbm, back_ref, rows_ref, residual_ref = take(6)
@@ -148,16 +149,14 @@
             relay_v.at[side],
             chip(4 - 2 * side),
         )
-    copies["gc", 0, 0] = (grads_ref, all_grads.at[slot[1]], chip(1))
+    kept_grads = {0: grads_ref, 2: grads_x, 4: grads_y}
+    for r, ref in kept_grads.items():
+        copies["gc", r, 0] = (ref, all_grads.at[slot[r + 1]], chip(1))
     for h in range(2):
         part_h = pl.ds(h * half_rows, half_rows)
         via = 4 * h + 2 * (1 - h)
-        copies["gx", h] = (grads_ref.at[part_h], all_grads.at[slot[2], part_h], chip(2))
-        copies["gy", h] = (grads_ref.at[part_h], all_grads.at[slot[4], part_h], chip(4))
-        copies["gd", h] = (all_grads.at[slot[via], part_h], all_grads.at[slot[6], part_h], chip(6 - via))
-        for r in (2, 4, 6):
-            here = all_grads.at[slot[r], part_h]
-            copies["gc", r, h] = (here, all_grads.at[slot[r + 1], part_h], chip(1))
+        copies["gd", h] = (kept_grads[via].at[part_h], all_grads.at[slot[6], part_h], chip(6 - via))
+        copies["gc", 6, h] = (all_grads.at[slot[6], part_h], all_grads.at[slot[7], part_h], chip(1))
     number = {name: k for k, name in enumerate(copies)}
 
     def remote(*name):
@@ -202,11 +201,10 @@
         ]
     for load in loads:
         load.start()
-    remote("gx", 0).start()
-    remote("gy", 1).start()
-    remote("gc", 0, 0).start()
-    remote("gx", 1).start()
-    remote("gy", 0).start()
+    for h in range(2):
+        remote("gd", h).start()
+    for r in kept_grads:
+        remote("gc", r, 0).start()
 
     def spread(q):
         remote("x" if 2 * q < parts else "y", q).start()
@@ -236,12 +234,9 @@
         pltpu.make_async_copy(source, target, weight_sem.at[k])
         for k, (source, target) in enumerate(weights)
     ]
-    grads_copy = pltpu.make_async_copy(grads_ref, all_grads.at[slot[0]], local.at[3])
-
     def load_rows(u):
         return pltpu.make_async_copy(all_rows.at[u], rows_v, local.at[6])
 
-    grads_copy.start()
     for copy in weight_copies:
         copy.start()
     for ref, first, last in blanks:
@@ -297,25 +292,32 @@
                 remote("gd", h).wait_recv()
                 remote("gc", 6, h).start()
         elif r % 2:
-            for h in range(2 if r > 1 else 1):
+            for h in range(2 if r == 7 else 1):
                 remote("gc", r - 1, h).wait_recv()
-        source = grads_ref if r == 0 else all_grads.at[slot[r]]
+        source = kept_grads.get(r, all_grads.at[slot[r]])
         load = pltpu.make_async_copy(source, grads_v, local.at[5])
         load.start()
         if k >= 2:
             d_act_store(0, k % 2).wait()
         load.wait()
+        keep = pltpu.make_async_copy(grads_v, all_grads.at[slot[r]], local.at[3])
+        if r in kept_grads:
+            keep.start()
         for first in range(0, inner, 512):
             columns = pl.ds(first, min(512, inner - first))
             d_act_v[k % 2, :, columns] = dot(grads_v[...], down_v[columns, :], NT)
         d_act_store(slot[r], k % 2).start()
-
-    first_product(0, 0)
-    first_product(1, 1)
+        if r in kept_grads:
+            keep.wait()
+
+    for k in range(3):
+        first_product(k, k)
     for load in loads:
         load.wait()
     if summed:
         residual_ref[...] = jnp.zeros_like(residual_ref)
+        for k in range(3, 6):
+            first_product(k, k)
     else:
         @pl.when(middle)
         def _():
@@ -323,6 +325,8 @@
             sum_rows(quarter, (line_out.at[2], 0), [(attn_relay, 0)])
             remote("nm").start()
 
+        for k in range(3, 6):
+            first_product(k, k)
         remote("n", 1).wait_recv()
 
         def normed(arrived):
@@ -356,23 +360,14 @@
     own_copy = pltpu.make_async_copy(rows_ref, all_rows.at[slot[0], part(0)], local.at[0])
     own_copy.start()
     spread(0)
-    for h, r in ((0, 2), (1, 4), (1, 2), (0, 4)):
-        remote("gx" if r == 2 else "gy", h).wait_recv()
-        if r == 2 + 2 * h:
-            remote("gd", h).start()
-        remote("gc", r, h).start()
-    first_product(2, 2)
-    first_product(3, 3)
+    first_product(6, 6)
+    first_product(7, 7)
     remote("z", 1).wait_recv()
     spread(1)
-    first_product(4, 4)
-    first_product(5, 5)
     remote("z", 2).wait_recv()
     pl.when(middle)(remote("zr").start)
     spread(2)
     arrived_x(0)
-    first_product(6, 6)
-    first_product(7, 7)
     pl.when(middle)(remote("z", 3).wait_recv)
     pl.when(outside)(remote("zr").wait_recv)
     spread(3)
@@ -703,7 +698,6 @@
 
     lax.fori_loop(0, quarter // ROW_CHUNK, last_step, 0)
 
-    grads_copy.wait()
 
     @pl.when(middle)
     def _():
@@ -733,7 +727,7 @@
     wide = 2 * inner + LANES
     first_part = 2 * expert_tiles * LANES
     loads = 4 + 3 * local_experts
-    copies = 3 * (parts - 1) + 9 * parts + 6 + 13 + 3
+    copies = 3 * (parts - 1) + 9 * parts + 6 + 7 + 3
     hbm = pl.BlockSpec(memory_space=pl.ANY)
     every = jax.ShapeDtypeStruct((GROUP, seq_len, D), BF16)
     some = jax.ShapeDtypeStruct((GROUP // 2, seq_len, D), BF16)
@@ -753,7 +747,7 @@
             jax.ShapeDtypeStruct((quarter, D), BF16),
             jax.ShapeDtypeStruct((quarter, D), F32),
         ),
-        in_specs=[hbm] * 2 + [pl.BlockSpec(memory_space=pltpu.VMEM)] + [hbm] * (2 + len(weights)),
+        in_specs=[hbm] * 2 + [pl.BlockSpec(memory_space=pltpu.VMEM)] + [hbm] * (4 + len(weights)),
         out_specs=(hbm,) * 8 + (pl.BlockSpec(memory_space=pltpu.VMEM),) * 3,
         scratch_shapes=[
             pltpu.VMEM((wide, D), BF16),
@@ -779,7 +773,7 @@
             pltpu.VMEM((quarter, D), BF16),
             pltpu.SemaphoreType.DMA((copies,)),
             pltpu.SemaphoreType.DMA((copies,)),
-            pltpu.SemaphoreType.DMA((8,)),
+            pltpu.SemaphoreType.DMA((10,)),
             pltpu.SemaphoreType.DMA((loads,)),
             pltpu.SemaphoreType.DMA((parts,)),
             pltpu.SemaphoreType.DMA((2,)),
@@ -793,7 +787,7 @@
         ),
         cost_estimate=pl.CostEstimate(flops=flops, bytes_accessed=120_000_000, transcendentals=0),
         name="experts",
-    )(attn, tokens, gain, grads, mask, *weights)
+    )(attn, tokens, gain, *grads, mask, *weights)
 
 
 def line_rows(own_rows):
@@ -866,9 +860,10 @@
 
 def gather_kernel(parts, *refs):
     tokens_ref, grads_ref, proj_ref, narrow_ref, out_ref, mask_ref = refs[:6]
-    gate_ref, up_ref, down_ref, tokens_all, grads_all, proj_all = refs[6:12]
-    narrow_all, out_all, mask_all, gate_all, up_all, down_all = refs[12:18]
-    send, recv, local = refs[18:]
+    gate_ref, up_ref, down_ref, tokens_all, grads_all, grads_x, grads_y = refs[6:13]
+    proj_all, narrow_all, out_all, mask_all, gate_all, up_all, down_all = refs[13:20]
+    send, recv, local, local_out = refs[20:24]
+    staged = refs[24:]
     exp_index, tp_index = lax.axis_index("exp"), lax.axis_index("tp")
     line, near = neighbours(parts)
     quarter, depth, seq_len = tokens_ref.shape[0], proj_ref.shape[0], mask_ref.shape[0]
@@ -899,6 +894,11 @@
         grads_all.at[pl.ds(3 * quarter, quarter)],
         line[0],
     )
+    for q in range(parts):
+        rows = pl.ds(q * quarter, quarter)
+        held = grads_ref if q == 0 else grads_all.at[rows]
+        copies["x", q] = (held, grads_x.at[rows], near[1])
+        copies["y", q] = (held, grads_y.at[rows], near[3])
     for key, ref in own.items():
         mine = arrays(0)[key]
         copies["g", 2, key] = (ref, mine, near[1])
@@ -925,6 +925,8 @@
         for r in (2, 4):
             remote("g", r, key).start()
         remote("c", 0, key).start()
+    remote("x", 0).start()
+    remote("y", 0).start()
     kept = [
         (tokens_ref, tokens_all.at[my_rows]),
         (grads_ref, grads_all.at[pl.ds(0, quarter)]),
@@ -936,9 +938,15 @@
         (up_ref.at[exp_index], block(up_all, width, 0, 1)),
         (down_ref.at[exp_index], block(down_all, width, 0, 1)),
     ]
-    kept = [pltpu.make_async_copy(s, t, local.at[k]) for k, (s, t) in enumerate(kept)]
-    for copy in kept:
-        copy.start()
+    for k, (source, _) in enumerate(kept):
+        pltpu.make_async_copy(source, staged[k], local.at[k]).start()
+    for k, (source, target) in enumerate(kept):
+        pltpu.make_async_copy(source, staged[k], local.at[k]).wait()
+        pltpu.make_async_copy(staged[k], target, local_out.at[k]).start()
+    kept = [
+        pltpu.make_async_copy(staged[k], target, local_out.at[k])
+        for k, (_, target) in enumerate(kept)
+    ]
     for key in own:
         for r in (2, 4):
             remote("g", r, key).wait_recv()
@@ -951,6 +959,10 @@
     for kind in range(2):
         remote("z", kind, 2).wait_recv()
         pl.when(inside(tp_index))(remote("zr", kind).start)
+    remote("z", 1, 1).wait_recv()
+    for q in (2, 1):
+        remote("x", q).start()
+        remote("y", q).start()
     for key in own:
         remote("g", 6, key).wait_recv()
         remote("c", 6, key).start()
@@ -959,9 +971,8 @@
     for name in copies:
         if name[0] in "ca":
             remote(*name).wait_recv()
-    for kind in range(2):
-        remote("z", kind, 1).wait_recv()
-
+    remote("z", 0, 1).wait_recv()
+    for kind in (1, 0):
         @pl.when(inside(tp_index))
         def _(kind=kind):
             remote("z", kind, 3).wait_recv()
@@ -969,8 +980,14 @@
             remote("zr", kind).wait_send()
 
         pl.when(jnp.logical_not(inside(tp_index)))(remote("zr", kind).wait_recv)
+        if kind == 1:
+            remote("x", 3).start()
+            remote("y", 3).start()
         for k in (1, 2):
             remote("z", kind, k).wait_send()
+    for name in copies:
+        if name[0] in "xy":
+            remote(*name).wait_recv()
     for name in copies:
         if name[0] not in ("z", "zr"):
             remote(*name).wait_send()
@@ -981,26 +998,32 @@
     hbm = pl.BlockSpec(memory_space=pl.ANY)
     depth, seq_len = proj.shape[0], mask.shape[0]
     shapes = [
-        (parts * tokens.shape[0], D),
-        (parts * tokens.shape[0], D),
+        *((parts * tokens.shape[0], D) for _ in range(4)),
         (GROUP * depth, proj.shape[1]),
         (narrow.shape[0], GROUP * narrow.shape[1]),
         (out.shape[0], GROUP * out.shape[1]),
         (GROUP * seq_len, LANES),
         *((w.shape[1], GROUP * w.shape[2]) for w in (gate, up, down)),
     ]
-    copies = 2 * parts + 4 * 7 + 3 * (GROUP - 1)
+    copies = 4 * parts + 4 * 7 + 3 * (GROUP - 1)
     return pl.pallas_call(
         functools.partial(gather_kernel, parts),
         out_shape=tuple(jax.ShapeDtypeStruct(s, BF16) for s in shapes),
         in_specs=[hbm] * 9,
-        out_specs=(hbm,) * 9,
+        out_specs=(hbm,) * 11,
         scratch_shapes=[
             pltpu.SemaphoreType.DMA((copies,)),
             pltpu.SemaphoreType.DMA((copies,)),
             pltpu.SemaphoreType.DMA((9,)),
+            pltpu.SemaphoreType.DMA((9,)),
+            *(
+                pltpu.VMEM(x.shape[-2:], BF16)
+                for x in (tokens, grads, proj, narrow, out, mask, gate, up, down)
+            ),
         ],
-        compiler_params=pltpu.CompilerParams(collective_id=2, has_side_effects=True),
+        compiler_params=pltpu.CompilerParams(
+            collective_id=2, has_side_effects=True, vmem_limit_bytes=16 * 1024 * 1024
+        ),
         name="gather_inputs",
     )(tokens, grads, proj, narrow, out, mask, gate, up, down)
 
@@ -1155,6 +1178,46 @@
     )(proj, out, mine, line, gate, up, down)
 
 
+def cut_kernel(moves, *refs):
+    sources, targets, held, sem_in, sem_out = refs[:3], refs[3:6], *refs[6:]
+
+    def load(k):
+        s, first, t, _ = moves[k]
+        rows = pl.ds(first, targets[t].shape[1])
+        return pltpu.make_async_copy(sources[s].at[rows], held.at[k], sem_in.at[k])
+
+    def store(k):
+        _, _, t, e = moves[k]
+        return pltpu.make_async_copy(held.at[k], targets[t].at[e], sem_out.at[k])
+
+    for k in range(len(moves)):
+        load(k).start()
+    for k in range(len(moves)):
+        load(k).wait()
+        store(k).start()
+    for k in range(len(moves)):
+        store(k).wait()
+
+
+def cut_experts(moves, sums, count, hidden):
+    hbm = pl.BlockSpec(memory_space=pl.ANY)
+    shape = (count, hidden, D)
+    return pl.pallas_call(
+        functools.partial(cut_kernel, moves),
+        out_shape=(jax.ShapeDtypeStruct(shape, F32),) * 3,
+        in_specs=[hbm] * 3,
+        out_specs=(hbm,) * 3,
+        scratch_shapes=[
+            pltpu.VMEM((len(moves), hidden, D), F32),
+            pltpu.SemaphoreType.DMA((len(moves),)),
+            pltpu.SemaphoreType.DMA((len(moves),)),
+        ],
+        compiler_params=pltpu.CompilerParams(vmem_limit_bytes=24 * 1024 * 1024),
+        cost_estimate=pl.CostEstimate(flops=0, bytes_accessed=35_000_000, transcendentals=0),
+        name="cut_experts",
+    )(*sums)
+
+
 def pad_to(value, axis, multiple):
     widths = [(0, 0)] * value.ndim
     widths[axis] = (0, -value.shape[axis] % multiple)
@@ -1208,6 +1271,7 @@
         (
             whole,
             own_grads,
+            *near_grads,
             qkv_weight,
             narrow_weight,
             output_weight,
@@ -1221,6 +1285,7 @@
     else:
         whole = lax.all_gather(tokens, "tp", axis=0, tiled=True)
         own_grads = line_rows(cotangent)
+        near_grads = [swap(own_grads, "exp", 2), swap(own_grads, "exp", 4)]
         qkv_weight = lax.all_gather(proj, "exp", axis=0, tiled=True)
         narrow_weight = lax.all_gather(narrow_weight, "exp", axis=1, tiled=True)
         output_weight = lax.all_gather(attn_o, "exp", axis=1, tiled=True)
@@ -1278,14 +1343,15 @@
 
     d_normed_two, rest_sum, first_sum, down_sum = 0.0, 0.0, 0.0, 0.0
     for base in range(0, exp_count, GROUP):
-        rows_b, own_b = attn_part, own_grads
+        rows_b, grads_b = attn_part, (own_grads, *near_grads)
         if base:
-            rows_b, own_b = swap(normed_two, "exp", base), swap(own_grads, "exp", base)
+            rows_b = swap(normed_two, "exp", base)
+            grads_b = [swap(own_grads, "exp", base ^ r) for r in (0, 2, 4)]
         masks = lax.dynamic_index_in_dim(
             all_masks, (exp_index // GROUP) ^ (base // GROUP), keepdims=False
         )
         *results, back, rows_b, residual_b = expert_layer(
-            rows_b, tokens, gain_row, own_b, masks, weights, (*sizes, base > 0)
+            rows_b, tokens, gain_row, grads_b, masks, weights, (*sizes, base > 0)
         )
         all_rows, all_grads, act, first_grads, rest_grads, out_even, out_odd, _ = results
         if not base:
@@ -1351,14 +1417,14 @@
 
     padded = expert_tiles * LANES
 
-    spans = [first_sum] + [
-        rest_sum[2 * e * padded : 2 * (e + 1) * padded] for e in range(local_experts - 1)
-    ]
-    grad_egate = jnp.stack([s[:hidden] for s in spans]).transpose(0, 2, 1)
-    grad_eup = jnp.stack([s[padded : padded + hidden] for s in spans]).transpose(0, 2, 1)
-    grad_edown = jnp.stack(
-        [down_sum[e * padded : e * padded + hidden] for e in range(local_experts)]
+    moves = []
+    for e in range(local_experts):
+        held, first = (0, 0) if e == 0 else (1, 2 * (e - 1) * padded)
+        moves += [(held, first, 0, e), (held, first + padded, 1, e), (2, e * padded, 2, e)]
+    grad_egate, grad_eup, grad_edown = cut_experts(
+        moves, (first_sum, rest_sum, down_sum), local_experts, hidden
     )
+    grad_egate, grad_eup = grad_egate.transpose(0, 2, 1), grad_eup.transpose(0, 2, 1)
     shared_sum = rest_sum[2 * (local_experts - 1) * padded :]
     start = local_experts * padded
     shared_rows = my_gate.shape[0]

time: 674 us -> 667 us (0.990)
  Pallas kernels: 436 us -> 457 us
  other arithmetic: 60.1 us -> 46.2 us
  waiting for transfers between devices: 17.9 us -> 4.97 us
    pallas_call x1, Pallas kernels: 75.4 us -> 99.9 us  [gather_inputs(): pl.pallas_call(functools.partial(gather_kernel, parts), out_shape=tuple((...]
    unnamed x123 -> x133, local copies, waits for them, and re-layouts: 6.51 us -> 23.7 us
    another operation x2 -> x0, local copies, waits for them, and re-layouts: 12.7 us -> none  [the longest x1 9.37 us: shards(): jnp.stack([down_sum[e * padded:e * padded + hidden] for e in range(local_...]
    pallas_call x1, Pallas kernels: 303 us -> 292 us  [expert_layer(): pl.pallas_call(functools.partial(expert_kernel, sizes), out_shape=(every,...]
    pallas_call x0 -> x1, Pallas kernels: none -> 7.33 us  [cut_experts(): pl.pallas_call(functools.partial(cut_kernel, moves), out_shape=(jax.Shape...]
    ppermute x5, waiting for transfers between devices: 12.1 us -> 4.91 us  [swap(): return lax.ppermute(value, axis, [(i, i ^ bit) for i in range(size)])]
  transfers between devices with their start and end apart: 7 -> 7, of which waited for: 5 -> 2; matrix products, arithmetic and copies ran while one was open for 14% -> 14% of each run, Pallas kernels for 0% -> 1%
where the time goes in v4:
time: 667 us; the launch traced here: 661 us
  Pallas kernels  457 us (69%)
  matrix products  94.6 us (14%)
  other arithmetic  46.2 us (7%)
  local copies, waits for them, and re-layouts  39 us (6%)
  between operations  15.4 us (2%)
    pallas_call x1, Pallas kernels, expert_layer(): pl.pallas_call(functools.partial(expert_kernel, sizes), out_shape=(every,...  292 us
    pallas_call x1, Pallas kernels, gather_inputs(): pl.pallas_call(functools.partial(gather_kernel, parts), out_shape=tuple((...  99.9 us
    dot_general x9, matrix products, dot(): lax.dot_general(left, right, (dims, ((), ())), preferred_element_type=F32)  85.2 us
    pallas_call x1, Pallas kernels, scatter_grads(): pl.pallas_call(functools.partial(scatter_kernel, parts), out_shape=(jax.S...  58.1 us
    unnamed x133, local copies, waits for them, and re-layouts  23.7 us
  transfers between devices with their start and end apart: 7, of which 2 were waited for; matrix products, arithmetic and copies ran while one was open for 14% of the time, Pallas kernels for 1%

profile of v4, /device:TPU:0, one launch (start us, length us, event | category | flops | bytes accessed | tf_op | source)
XLA Modules:
  0.0 661.2 jit_solution(18122913138993312983)
XLA Ops:
  17.8 99.9 %gather_inputs.1 = (bf16[512,2048]{1,0:T(8,128)(2,1)S(1)}, bf16[512,2048]{1,0:T(8,128)(2,1)S(1)}, bf16[512,2048]{1,0:T(8,128)(2,1)S(1)}, bf16[512,2048]{1,0:T(8,...) custom-call(bf16[128,2048]{1,0:T(8,128)(2,1)S(1)} %copy-done, ...), custom_call_target="tpu_custom_call" | custom-call | tf_op jit(solution)/shard_map/gather_inputs/pallas_call | solution.py:1009
  122.4 1.9 fusion.46
  126.8 2.5 copy.141
  132.9 2.1 subtract_convert_fusion.1
  138.1 2.6 fusion.23
  140.8 2.6 convolution_convert_fusion.3.refs_0_
  144.4 291.6 %experts.1 = (bf16[8,512,2048]{2,1,0:T(8,128)(2,1)}, bf16[8,512,2048]{2,1,0:T(8,128)(2,1)}, bf16[8,512,896]{2,1,0:T(8,128)(2,1)}, bf16[8,512,768]{2,1,0:T(8,128)...) custom-call(bf16[512,2048]{1,0:T(8,128)(2,1)} %convolution_convert_f, ...), custom_call_target="tpu_custom_call" | custom-call | flops 94489280512 | bytes 120000000 | tf_op jit(solution)/shard_map/experts/pallas_call | solution.py:735
  439.4 2.7 fusion.65
  443.7 22.1 %convolution_bitcast_fusion.refs_2_ = f32[896,2048]{1,0:T(8,128)} fusion(bf16[8,512,896]{2,1,0:T(8,128)(2,1)} %get-tuple-element.77, bf16[8,512,2048]{2,1,0:T(8,128)(2,1)} %get-tuple-element.78), kind=kOutput, calls=%fused_computation.20 | convolution fusion | flops 15032385536 | bytes 31457280 | tf_op jit(solution)/shard_map/dot_general | solution.py:62
  465.9 7.1 %fusion.15 = (bf16[512,2048]{1,0:T(8,128)(2,1)S(1)}, bf16[512,2048]{1,0:T(8,128)(2,1)}, bf16[512,2048]{1,0:T(8,128)(2,1)}, bf16[512,2048]{1,0:T(8,128)(2,1)}) fusion(bf16[4,512,2048]{2,1,0:T(8,128)(2,1)} %collective-permute-done, bf16[4,512,2048]{2,1,0:T(8,128)(2,1)S(1)} %bitcast.180), kind=kLoop, calls=%fused_computation.32 | loop fusion | flops 16777216 | bytes 25165824 | tf_op jit(solution)/shard_map/convert_element_type | solution.py:799
  476.2 19.1 %fusion.73.refs_0_ = f32[768,2048]{1,0:T(8,128)} fusion(bf16[4096,768]{1,0:T(8,128)(2,1)S(1)} %bitcast.209, bf16[4096,2048]{1,0:T(8,128)(2,1)} %bitcast.204), kind=kOutput, calls=%fused_computation.127 | convolution fusion | flops 12884901888 | bytes 29360128 | tf_op jit(solution)/shard_map/dot_general | solution.py:62
  495.4 4.8 collective-permute-done.1
  500.3 2.9 convolution_convert_fusion.4
  503.2 2.6 fusion.4
  512.4 5.5 convolution_convert_fusion.2
  517.9 2.5 slice_add_fusion.2
  525.4 26.2 %fusion.72 = (bf16[1152,2048]{1,0:T(8,128)(2,1)S(1)}, f32[1152,2048]{1,0:T(8,128)S(1)}) fusion(bf16[4096,1152]{1,0:T(8,128)(2,1)} %bitcast.206, bf16[4096,2048]{1,0:T(8,128)(2,1)} %bitcast.205), kind=kOutput, calls=%fused_computation.126 | convolution fusion | flops 19329712128 | bytes 40370176 | tf_op jit(solution)/shard_map/dot_general | solution.py:62
  552.9 3.1 copy-done.2
  556.0 2.8 copy-done.3
  558.8 7.3 %cut_experts.1 = (f32[2,352,2048]{2,1,0:T(8,128)}, f32[2,352,2048]{2,1,0:T(8,128)}, f32[2,352,2048]{2,1,0:T(8,128)}) custom-call(f32[768,2048]{1,0:T(8,128)S(1)} %copy-done.3, f32[1152,2048]{1,0:T(8,128)S(1)} %get-tuple-element.209.refs_1_, f32[896,2048]{1,0:T(8,128)S(1)} %copy-done.2), custom_call_target="tpu_custom_call" | custom-call | bytes 35000000 | tf_op jit(solution)/shard_map/cut_experts/pallas_call | solution.py:1205
  568.9 3.7 convolution_convert_fusion
  578.3 1.9 copy.118
  580.3 4.5 fusion.66
  588.3 58.1 %scatter_grads.1 = (f32[256,896]{1,0:T(8,128)S(1)}, f32[512,256]{1,0:T(8,128)S(1)}, bf16[128,2048]{1,0:T(8,128)(2,1)S(1)}, bf16[8,96,256]{2,1,0:T(8,128)(2,1)S(1...) custom-call(bf16[2048,896]{1,0:T(8,128)(2,1)S(1)} %fusion.10.refs_0_, ...), custom_call_target="tpu_custom_call" | custom-call | tf_op jit(solution)/shard_map/scatter_grads/pallas_call | solution.py:1148
  (210 shorter events, 65.6 us)
Async XLA Ops:
  7.2 488.2 %all-gather.2.cloned.1.call-start = ((), (), s32[]{:S(2)}) async-start(), calls=%async_computation.1 | async-start | bytes 2621440 | tf_op jit(solution)/shard_map/all_gather | solution.py:1383
  124.7 8.0 %copy-start.48 = (s32[512]{0:T(512)S(1)}, s32[512]{0:T(512)}, u32[]{:S(2)}) copy-start(s32[512]{0:T(512)} %param.19) | copy-start | bytes 6148
  144.4 293.2 %copy-start.41 = (f32[1,2048]{1,0:T(1,128)S(1)}, f32[1,2048]{1,0:T(1,128)}, u32[]{:S(2)}) copy-start(f32[1,2048]{1,0:T(1,128)} %get-tuple-element.199.refs_2_) | copy-start | bytes 24580
  144.4 295.0 %copy-start.5 = (bf16[128,2048]{1,0:T(8,128)(2,1)S(1)}, bf16[128,2048]{1,0:T(8,128)(2,1)}, u32[]{:S(2)}) copy-start(bf16[128,2048]{1,0:T(8,128)(2,1)} %refs_1_.2) | copy-start | bytes 1572868
  436.0 7.0 %copy-start.1 = (bf16[128,2048]{1,0:T(8,128)(2,1)S(1)}, bf16[128,2048]{1,0:T(8,128)(2,1)}, u32[]{:S(2)}) copy-start(bf16[128,2048]{1,0:T(8,128)(2,1)} %refs_1_.3) | copy-start | bytes 1572868
  436.0 29.8 %collective-permute-start = (bf16[4,512,2048]{2,1,0:T(8,128)(2,1)}, bf16[4,512,2048]{2,1,0:T(8,128)(2,1)}, u32[]{:S(2)}, u32[]{:S(2)}) collective-permute-start(bf16[4,512,2048]{2,1,0:T(8,128)(2,1)} %get-tuple-element.76), channel_id=1, source_target_pairs={{0,4},{4,0},{8,12},{12,8},{16,20},{20,16},{24,28},{28,24},{1,5},{5... | collective-permute-start | bytes 25165832 | tf_op jit(solution)/shard_map/ppermute | solution.py:72
  437.5 28.3 %copy-start.49 = (f32[128]{0:T(128)}, f32[128]{0:T(128)S(1)}, u32[]{:S(2)}) copy-start(f32[128]{0:T(128)S(1)} %add_rsqrt_fusion.2) | copy-start | bytes 1540
  439.4 26.4 %copy-start.51 = (f32[128]{0:T(128)}, f32[128]{0:T(128)S(1)}, u32[]{:S(2)}) copy-start(f32[128]{0:T(128)S(1)} %broadcast_multiply_fusion.1) | copy-start | bytes 1540
  442.1 131.0 %reduce-scatter.2.cloned.1.call-start = ((), (), s32[]{:S(2)}) async-start(), calls=%async_computation.2 | async-start | bytes 2621440 | tf_op jit(solution)/shard_map/reduce_scatter | solution.py:1411
  443.7 22.1 %slice-start = ((s8[8388608]{0:T(1024)(128)(4,1)}), s8[4194304]{0:T(1024)(128)(4,1)S(1)}, s32[]{:S(2)}) async-start(s8[8388608]{0:T(1024)(128)(4,1)} %bitcast.179), calls=%async_computation.3 | async-start | bytes 8388608
  443.7 22.1 %slice-start.1 = ((s8[8388608]{0:T(1024)(128)(4,1)}), s8[4194304]{0:T(1024)(128)(4,1)S(1)}, s32[]{:S(2)}) async-start(s8[8388608]{0:T(1024)(128)(4,1)} %bitcast.179), calls=%async_computation.4 | async-start | bytes 8388608
  465.8 10.4 %slice-start.2 = ((s8[6291456]{0:T(1024)(128)(4,1)}), s8[4194304]{0:T(1024)(128)(4,1)S(1)}, s32[]{:S(2)}) async-start(s8[6291456]{0:T(1024)(128)(4,1)} %bitcast.207), calls=%async_computation.5 | async-start | bytes 8388608
  465.9 10.3 %slice-start.3 = ((s8[6291456]{0:T(1024)(128)(4,1)}), s8[2097152]{0:T(1024)(128)(4,1)S(1)}, s32[]{:S(2)}) async-start(s8[6291456]{0:T(1024)(128)(4,1)} %bitcast.207), calls=%async_computation.6 | async-start | bytes 4194304
  474.5 25.8 %collective-permute-start.1 = (bf16[256,2048]{1,0:T(8,128)(2,1)}, bf16[256,2048]{1,0:T(8,128)(2,1)}, u32[]{:S(2)}, u32[]{:S(2)}) collective-permute-start(bf16[256,2048]{1,0:T(8,128)(2,1)} %get-tuple-element.190), channel_id=1, source_target_pairs={{0,16},{4,20},{8,24},{12,28},{16,0},{20,4},{24,8},{28,12},{1,17},{... | collective-permute-start | bytes 3145736 | tf_op jit(solution)/shard_map/ppermute | solution.py:72
  474.7 25.6 %collective-permute-start.2 = (bf16[256,2048]{1,0:T(8,128)(2,1)}, bf16[256,2048]{1,0:T(8,128)(2,1)}, u32[]{:S(2)}, u32[]{:S(2)}) collective-permute-start(bf16[256,2048]{1,0:T(8,128)(2,1)} %get-tuple-element.189), channel_id=1, source_target_pairs={{0,8},{4,12},{8,0},{12,4},{16,24},{20,28},{24,16},{28,20},{1,9},{5... | collective-permute-start | bytes 3145736 | tf_op jit(solution)/shard_map/ppermute | solution.py:72
  495.3 7.9 %copy-start.31 = (pred[512,512]{0,1:T(8,128)(4,1)S(1)}, pred[512,512]{0,1:T(8,128)(4,1)}, u32[]{:S(2)}) copy-start(pred[512,512]{0,1:T(8,128)(4,1)} %copy-done.30) | copy-start | bytes 786436
  495.3 7.9 %copy-start.43 = (f32[4,512]{1,0:T(4,128)S(1)}, f32[4,512]{1,0:T(4,128)}, u32[]{:S(2)}) copy-start(f32[4,512]{1,0:T(4,128)} %copy-done.42) | copy-start | bytes 24580
  495.3 7.9 %copy-start.47 = (f32[4,512]{1,0:T(4,128)S(1)}, f32[4,512]{1,0:T(4,128)}, u32[]{:S(2)}) copy-start(f32[4,512]{1,0:T(4,128)} %copy-done.46) | copy-start | bytes 24580
  495.4 7.8 %copy-start.20 = (f32[512,512,4]{1,0,2:T(8,128)S(1)}, f32[512,512,4]{1,0,2:T(8,128)}, u32[]{:S(2)}) copy-start(f32[512,512,4]{1,0,2:T(8,128)} %copy-done.19) | copy-start | bytes 12582916
  512.4 5.5 copy-start.29
  521.9 52.4 %collective-permute-start.4 = (bf16[512,2048]{1,0:T(8,128)(2,1)}, bf16[512,2048]{1,0:T(8,128)(2,1)}, u32[]{:S(2)}, u32[]{:S(2)}) collective-permute-start(bf16[512,2048]{1,0:T(8,128)(2,1)} %pad_maximum_fusion.1), channel_id=1, source_target_pairs={{0,16},{4,20},{8,24},{12,28},{16,0},{20,4},{24,8},{28,12},{1,17},{... | collective-permute-start | bytes 6291464 | tf_op jit(solution)/shard_map/ppermute | solution.py:72
  525.0 49.3 %collective-permute-start.3 = (bf16[512,2048]{1,0:T(8,128)(2,1)}, bf16[512,2048]{1,0:T(8,128)(2,1)}, u32[]{:S(2)}, u32[]{:S(2)}) collective-permute-start(bf16[512,2048]{1,0:T(8,128)(2,1)} %pad_maximum_fusion), channel_id=1, source_target_pairs={{0,8},{4,12},{8,0},{12,4},{16,24},{20,28},{24,16},{28,20},{1,9},{5... | collective-permute-start | bytes 6291464 | tf_op jit(solution)/shard_map/ppermute | solution.py:72
  558.8 8.3 %copy-start.57 = (bf16[512,2048]{1,0:T(8,128)(2,1)S(1)}, bf16[512,2048]{1,0:T(8,128)(2,1)}, u32[]{:S(2)}) copy-start(bf16[512,2048]{1,0:T(8,128)(2,1)} %all-gather.2.cloned.1.call-done) | copy-start | bytes 6291460
  558.8 8.3 %copy-start.59 = (bf16[128,4,512]{2,0,1:T(8,128)(2,1)S(1)}, bf16[128,4,512]{2,0,1:T(8,128)(2,1)}, u32[]{:S(2)}) copy-start(bf16[128,4,512]{2,0,1:T(8,128)(2,1)} %copy-done.58) | copy-start | bytes 1572868
  (47 other events, 121.3 us)
Sparse Core Ops, SparseCore 0:
  442.3 43.5 all-gather.1
  525.5 41.4 reduce-scatter.1
